TPU v7x, 32 devices: a whole 2x2x4 slice. The times are simulated.
32 devices in a mesh: grp: 4 (over y, core), pair: 8 (over z, x).
Axes of the slice: x: 2, y: 2, z: 4, core: 2. Of those that a mesh axis runs over, the one named last changes fastest.
Arguments:
- amplitudes: bfloat16 [512, 10368], P('pair'), may hold values from -6 to 6
- integrals: bfloat16 [10368, 10368], P('pair', 'grp'), may hold values from -0.0625 to 0.0625
- hole_ints: bfloat16 [512, 512], replicated, may hold values from -0.25 to 0.25
- driver: bfloat16 [512, 10368], P('pair', 'grp'), may hold values from -6 to 6
- e_occ: float32 [128], replicated, may hold values from -1.2 to -0.2
- e_virt: float32 [288], replicated, may hold values from 0.3 to 1.5
- occ_pairs: int32 [2, 512], P(None, 'pair'), may hold values from 0 to 127
- virt_pairs: int32 [2, 10368], P(None, 'grp'), may hold values from 0 to 287
Outputs:
- amp_next: float32 [512, 10368], P('pair')
All inputs are finite; a program needn't handle non-finite values.
Results may differ from a plain program's by a relative error of at most 0.0003.
Values may be sent and summed in bfloat16 or wider, within the bound.
No kernel may reach another device: no remote copies, remote signals or barrier semaphores. Data moves between devices by JAX's collectives and lax.ppermute only.
A program may use at most 128 MiB of HBM per device.

v0:
```python
import jax
import jax.numpy as jnp
from jax import lax
from jax.sharding import PartitionSpec as P


def lookup(labels, energies):
    table = lax.broadcasted_iota(jnp.int32, labels.shape + energies.shape, labels.ndim)
    picked = jnp.where(labels[..., None] == table, energies, jnp.float32(0.0))
    return jnp.sum(picked, axis=-1)


def shards(amplitudes, integrals, hole_ints, driver, e_occ, e_virt, occ_pairs, virt_pairs):
    row_count = amplitudes.shape[0]
    col_count = integrals.shape[1]
    col_start = lax.axis_index("grp") * col_count
    own_cols = lax.dynamic_slice_in_dim(amplitudes, col_start, col_count, 1)
    row_start = lax.axis_index("pair") * row_count
    left = amplitudes
    ladder = jnp.dot(
        left,
        lax.all_gather(integrals, "pair", axis=0, tiled=True),
        preferred_element_type=jnp.float32,
    )
    my_holes = lax.dynamic_slice_in_dim(hole_ints, row_start, row_count, 0)
    left = my_holes
    ladder = ladder + jnp.dot(
        left,
        lax.all_gather(own_cols, "pair", axis=0, tiled=True),
        preferred_element_type=jnp.float32,
    )
    occ_energy = lookup(occ_pairs, e_occ)
    virt_energy = lookup(virt_pairs, e_virt)
    hole_energy = occ_energy[0] + occ_energy[1]
    pair_energy = virt_energy[0] + virt_energy[1]
    energy_gap = pair_energy[None, :] - hole_energy[:, None]
    update = (driver.astype(jnp.float32) + ladder) / energy_gap
    return lax.all_gather(update, "grp", axis=1, tiled=True)


def solution(mesh):
    placed = (
        P("pair", None),
        P("pair", "grp"),
        P(),
        P("pair", "grp"),
        P(),
        P(),
        P(None, "pair"),
        P(None, "grp"),
    )
    return jax.shard_map(
        shards, mesh=mesh, in_specs=placed, out_specs=P("pair", None), check_vma=False
    )
```

profile of v0, /device:TPU:1, one launch (start us, length us, event | category | flops | bytes accessed | tf_op | source)
XLA Modules:
  0.0 1167.3 jit_solution(8605180483468282615)
XLA Ops:
  6.5 0.0 copy-start
  6.5 0.0 all-gather.5.cloned.1.call-start
  6.6 0.7 all-gather.5.cloned.1.call-update
  7.3 0.0 all-gather.7.cloned.1.call-start
  7.3 0.5 copy-done
  7.9 0.9 constant_dynamic-slice_fusion
  8.8 0.0 all-gather.7.cloned.1.call-update
  8.8 0.0 all-gather.9.cloned.1.call-start
  8.8 0.0 copy-done.5
  8.8 0.0 copy-done.4
  8.8 0.2 select_reduce_fusion.1
  9.0 0.0 copy-done.3
  9.0 0.0 copy-done.2
  9.0 0.9 select_reduce_fusion
  10.0 0.0 copy-start.6
  10.0 1054.7 %all-gather.5.cloned.1.call-done = bf16[10368,2592]{1,0:T(8,128)(2,1)} async-done(((bf16[1296,2592]{1,0:T(8,128)(2,1)}), bf16[10368,2592]{1,0:T(8,128)(2,1)}) %all-gather.5.cloned.1.call-update) | async-done | bytes 53747728 | tf_op jit(solution)/shard_map/all_gather | solution.py:22
  1064.7 20.9 %fusion.6 = f32[64,2592]{1,0:T(8,128)S(1)} fusion(bf16[64,10368]{1,0:T(8,128)(2,1)S(1)} %copy-done, bf16[10368,2592]{1,0:T(8,128)(2,1)} %all-gather.5.cloned.1.call-done), kind=kOutput, calls=%fused_computation.14 | convolution fusion | flops 3439853568 | bytes 55738368 | tf_op jit(solution)/shard_map/dot_general | solution.py:20
  1085.6 36.1 %all-gather.7.cloned.1.call-done = bf16[512,2592]{1,0:T(8,128)(2,1)} async-done(((bf16[64,2592]{1,0:T(8,128)(2,1)}), bf16[512,2592]{1,0:T(8,128)(2,1)}) %all-gather.7.cloned.1.call-update) | async-done | bytes 2654224 | tf_op jit(solution)/shard_map/all_gather | solution.py:29
  1121.8 0.0 copy-done.6
  1121.8 3.3 fusion.2
  1125.1 0.0 all-gather.9.cloned.1.call-update
  1125.1 26.7 %all-gather.9.cloned.1.call-done = f32[4,2592,64]{1,2,0:T(8,128)} async-done(((f32[1,2592,64]{1,2,0:T(8,128)}), f32[4,2592,64]{1,2,0:T(8,128)}) %all-gather.9.cloned.1.call-update) | async-done | bytes 2654224 | tf_op jit(solution)/shard_map/all_gather | solution.py:38
  1151.7 5.2 copy.11
  1157.0 3.8 reshape.13
  (8 shorter events, 0.1 us)
Async XLA Ops:
  6.5 1.3 copy-start
  6.5 2.3 copy-start.5
  6.5 2.3 copy-start.4
  6.5 2.5 copy-start.3
  6.5 2.5 copy-start.2
  6.5 1058.2 %all-gather.5.cloned.1.call-start = ((), (), s32[]{:S(2)}) async-start(), calls=%async_computation | async-start | bytes 62705664 | tf_op jit(solution)/shard_map/all_gather | solution.py:22
  7.3 1114.5 %all-gather.7.cloned.1.call-start = ((), (), s32[]{:S(2)}) async-start(), calls=%async_computation.1 | async-start | bytes 3096576 | tf_op jit(solution)/shard_map/all_gather | solution.py:29
  8.8 1143.0 %all-gather.9.cloned.1.call-start = ((), (), s32[]{:S(2)}) async-start(), calls=%async_computation.2 | async-start | bytes 3440640 | tf_op jit(solution)/shard_map/all_gather | solution.py:38
  10.0 1111.7 %copy-start.6 = (bf16[64,2592]{1,0:T(8,128)(2,1)S(1)}, bf16[64,2592]{1,0:T(8,128)(2,1)}, u32[]{:S(2)}) copy-start(bf16[64,2592]{1,0:T(8,128)(2,1)} %param.11) | copy-start | bytes 995332
  1151.7 9.1 copy-start.1
Sparse Core Ops, SparseCore 0:
  8.9 1055.7 all-gather.4
  1066.9 54.8 all-gather.6
  1125.2 26.4 all-gather.8
where the time goes:
time: 1170 us
  waiting for transfers between devices  1120 us (96%)
  matrix products  24.2 us (2%)
  between operations  13.2 us (1%)
    all_gather x1, waiting for transfers between devices, shards(): lax.all_gather(integrals, 'pair', axis=0, tiled=True)  1050 us
    all_gather x1, waiting for transfers between devices, shards(): lax.all_gather(own_cols, 'pair', axis=0, tiled=True)  36.1 us
    all_gather x1, waiting for transfers between devices, shards(): return lax.all_gather(update, 'grp', axis=1, tiled=True)  26.7 us
  transfers between devices with their start and end apart: 3, of which 3 were waited for; matrix products, arithmetic and copies ran while one was open for 2% of the time, Pallas kernels for 0%

commit v1 on v0

v1 whole, which is shorter than its diff:
```python
import functools
import math

import jax
import jax.numpy as jnp
from jax import lax
from jax.experimental import pallas as pl
from jax.experimental.pallas import tpu as pltpu
from jax.sharding import PartitionSpec as P

TOP = 32752.0
STEP = 0.0625
LANES = 128
VMEM_LIMIT = 48 * 1024 * 1024
CUT_LIMIT = 8 * 1024 * 1024
SMALL = pl.CostEstimate(flops=1024, bytes_accessed=1024, transcendentals=0)


def lookup(labels, energies):
    table = lax.broadcasted_iota(jnp.int32, labels.shape + energies.shape, labels.ndim)
    picked = jnp.where(labels[..., None] == table, energies, jnp.float32(0.0))
    return jnp.sum(picked, axis=-1)


def layout(cols):
    width = cols // LANES * LANES + LANES
    tiles = width // LANES
    segments = next(n for n in (3, 2, 1) if tiles % n == 0)
    return width, segments


def columns(rows, size, start):
    return lax.broadcasted_iota(jnp.int32, (rows, size), 1) + start


def encode(x):
    most = jnp.max(jnp.abs(x), axis=1, keepdims=True)
    code = jnp.ceil(jnp.log2(jnp.maximum(most, 1e-30)) * (1.0 / STEP))
    whole = jnp.round(x * (jnp.exp2(code * -STEP) * TOP))
    return whole.astype(jnp.int32), code


def with_codes(whole, codes, cols, start):
    at = columns(whole.shape[0], whole.shape[1], start)
    for n, code in enumerate(codes):
        whole = jnp.where(at == cols + n, code.astype(jnp.int32), whole)
    return whole


def decode(coded, codes, n, cols, start):
    x = coded.astype(jnp.float32) * (jnp.exp2(codes[n] * STEP) * (1.0 / TOP))
    if start + x.shape[1] > cols:
        x = jnp.where(columns(x.shape[0], x.shape[1], start) < cols, x, 0.0)
    return x


def codes_of(coded_ref, at, cols, segments):
    tail = coded_ref[at, cols // LANES * LANES :].astype(jnp.float32)
    first = cols % LANES
    return [tail[:, first + n : first + n + 1] for n in range(segments)]


def in_hbm(x):
    return pltpu.with_memory_space_constraint(x, pltpu.HBM)


def params(*dims, limit=VMEM_LIMIT):
    return pltpu.CompilerParams(
        dimension_semantics=dims or None, vmem_limit_bytes=limit
    )


def turns(count):
    return [*range(count // 2, count), *range(count // 2 - 1, -1, -1)]


def cut_kernel(where, a_ref, *refs):
    outs, slots = refs[:-1], refs[-1]
    count, _, depth = slots.shape
    for n in range(2 * count):
        k = where[0] ^ n

        @pl.when(k % 2 == where[2])
        def _():
            slots[k // 2] = a_ref[:, n * depth : (n + 1) * depth]

    for j, turn in enumerate(turns(count)):
        outs[j][...] = slots[turn]


def cut(amplitudes, pair, part, core, pairs, depth):
    rows, total = amplitudes.shape
    high, count = rows // 2, pairs // 2
    return pl.pallas_call(
        cut_kernel,
        grid_spec=pltpu.PrefetchScalarGridSpec(
            num_scalar_prefetch=1,
            grid=(1,),
            in_specs=[pl.BlockSpec((high, total), lambda i, where: (where[1], 0))],
            out_specs=[pl.BlockSpec((high, depth), lambda i, where: (0, 0))] * count,
            scratch_shapes=[pltpu.VMEM((count, high, depth), jnp.bfloat16)],
        ),
        out_shape=[jax.ShapeDtypeStruct((high, depth), jnp.bfloat16)] * count,
        compiler_params=params("arbitrary", limit=CUT_LIMIT),
        cost_estimate=SMALL,
        name="cut_blocks",
    )(jnp.stack([pair, part, core]), in_hbm(amplitudes))


def pack_kernel(count, *refs):
    for n in range(count):
        refs[-1][n] = refs[n][...]


def pack(blocks, others):
    shape = (len(blocks),) + blocks[0].shape
    return pl.pallas_call(
        functools.partial(pack_kernel, len(blocks)),
        in_specs=[pl.BlockSpec(memory_space=pltpu.VMEM)] * len(blocks)
        + [pl.BlockSpec(memory_space=pl.ANY)] * len(others),
        out_shape=jax.ShapeDtypeStruct(shape, jnp.bfloat16),
        compiler_params=params(limit=CUT_LIMIT),
        cost_estimate=SMALL,
        name="pack_blocks",
    )(*blocks, *others)


def product_kernel(order, parts, cols, segments, where, *refs):
    a_refs, (h_ref, v_ref, o_ref), outs = refs[:parts], refs[parts : parts + 3], refs[parts + 3 : -4]
    left, left_rest, right_rest, codes = refs[-4:]
    part, depth = a_refs[0].shape[1] // parts, a_refs[0].shape[2]
    rows = o_ref.shape[0]
    main, second = split_depth(depth)
    step = pl.program_id(0)
    tile = v_ref.shape[1]
    high = outs[0].shape[0]

    @pl.when(step == 0)
    def _():
        left_rest[...] = jnp.zeros_like(left_rest)
        right_rest[...] = jnp.zeros_like(right_rest)
        count = a_refs[0].shape[0]
        spot = {entry: n for n, entry in enumerate(order)}
        for s, ref in enumerate(a_refs):
            swapped = where[1] ^ s
            for j, turn in enumerate(turns(count)):
                for q in range(parts):
                    even, odd = spot[q, 2 * turn], spot[q, 2 * turn + 1]
                    at = jnp.where(swapped == 0, even, odd) * part
                    at = pl.ds(pl.multiple_of(at, part), part)
                    block = ref.at[j, q * part : (q + 1) * part]
                    left[at, :] = block[:, :main]
                    left_rest[at, : depth - main] = block[:, main:]
                    source = where[0] ^ (2 * turn + swapped)
                    left_rest[at, second : second + rows] = h_ref[source, where[2 + q]]

    right_rest[: depth - main, :] = v_ref[main:, :]
    right_rest[second : second + rows, :] = o_ref[...]
    acc = jnp.dot(left[...], v_ref[:main, :], preferred_element_type=jnp.float32)
    acc = acc + jnp.dot(left_rest[...], right_rest[...], preferred_element_type=jnp.float32)
    acc = jnp.where(columns(acc.shape[0], tile, step * tile) < cols, acc, 0.0)
    given = parts * high
    for j in range(parts):
        outs[parts + j][...] = acc[given + j * high : given + (j + 1) * high]
    whole, code = encode(acc[:given])
    at = lax.broadcasted_iota(jnp.int32, codes.shape, 1)
    codes[...] = jnp.where(at == step, code, codes[...])

    @pl.when(step < segments - 1)
    def _():
        for j in range(parts):
            outs[j][...] = whole[j * high : (j + 1) * high].astype(jnp.int16)

    @pl.when(step == segments - 1)
    def _():
        kept = [codes[:, n : n + 1] for n in range(segments)]
        done = with_codes(whole, kept, cols, (segments - 1) * tile)
        for j in range(parts):
            outs[j][...] = done[j * high : (j + 1) * high].astype(jnp.int16)


def split_depth(depth):
    main = depth // LANES * LANES
    return main, -(-(depth - main) // 16) * 16


def product(order, where, sources, holes, integrals, own_cols):
    parts = len(sources)
    _, high_block, depth = sources[0].shape
    part = high_block // parts
    cols = integrals.shape[1]
    rows = own_cols.shape[0]
    width, segments = layout(cols)
    tile = width // segments
    total = len(order) * part
    high = total // (2 * parts)
    main, second = split_depth(depth)
    rest = -(-(second + rows) // LANES) * LANES
    whole = lambda x: pl.BlockSpec(x.shape, lambda i, where: (0,) * x.ndim)
    out = pl.BlockSpec((high, tile), lambda i, where: (0, i))
    return pl.pallas_call(
        functools.partial(product_kernel, order, parts, cols, segments),
        grid_spec=pltpu.PrefetchScalarGridSpec(
            num_scalar_prefetch=1,
            grid=(segments,),
            in_specs=[whole(x) for x in sources]
            + [
                whole(holes),
                pl.BlockSpec((depth, tile), lambda i, where: (0, i)),
                pl.BlockSpec((rows, tile), lambda i, where: (0, i)),
            ],
            out_specs=[out] * (2 * parts),
            scratch_shapes=[
                pltpu.VMEM((total, main), jnp.bfloat16),
                pltpu.VMEM((total, rest), jnp.bfloat16),
                pltpu.VMEM((rest, tile), jnp.bfloat16),
                pltpu.VMEM((total // 2, LANES), jnp.float32),
            ],
        ),
        out_shape=[jax.ShapeDtypeStruct((high, width), jnp.int16)] * parts
        + [jax.ShapeDtypeStruct((high, width), jnp.float32)] * parts,
        compiler_params=params("arbitrary"),
        cost_estimate=SMALL,
        name="partial_products",
    )(where, *sources, in_hbm(holes), integrals, in_hbm(own_cols))


def add_kernel(cols, segments, inputs, inner, *refs):
    keeps, coded, (give_ref, next_ref) = refs[:inputs], refs[inputs : 2 * inputs], refs[2 * inputs :]
    high, width = next_ref.shape
    half = high // (inputs * inner)
    tile = width // segments
    chunk = min(16, half)

    for index in range(inputs):
        keep_ref, coded_ref = keeps[index], coded[index]

        def total(at, n, codes):
            span = slice(n * tile, (n + 1) * tile)
            return keep_ref[at, span] + decode(coded_ref[at, span], codes, n, cols, n * tile)

        for group in range(inner):
            top, target = 2 * half * group, half * (inner * index + group)

            @pl.loop(0, half // chunk)
            def _(i):
                out = pl.ds(pl.multiple_of(target + i * chunk, chunk), chunk)
                at = pl.ds(pl.multiple_of(top + i * chunk, chunk), chunk)
                codes = codes_of(coded_ref, at, cols, segments)
                made = []
                for n in range(segments):
                    whole, code = encode(total(at, n, codes))
                    made.append(code)
                    if n == segments - 1:
                        whole = with_codes(whole, made, cols, n * tile)
                    give_ref[out, n * tile : (n + 1) * tile] = whole.astype(jnp.int16)

            @pl.loop(0, half // chunk)
            def _(i):
                out = pl.ds(pl.multiple_of(target + i * chunk, chunk), chunk)
                at = pl.ds(pl.multiple_of(top + half + i * chunk, chunk), chunk)
                codes = codes_of(coded_ref, at, cols, segments)
                for n in range(segments):
                    next_ref[out, n * tile : (n + 1) * tile] = total(at, n, codes)


def add(keeps, coded, inner, cols):
    high, width = keeps[0].shape
    out = (len(keeps) * high // 2, width)
    return pl.pallas_call(
        functools.partial(add_kernel, cols, layout(cols)[1], len(keeps), inner),
        out_shape=(
            jax.ShapeDtypeStruct(out, jnp.int16),
            jax.ShapeDtypeStruct(out, jnp.float32),
        ),
        compiler_params=params(),
        cost_estimate=SMALL,
        name="add_partial_sums",
    )(*keeps, *coded)


def update_kernel(cols, segments, inputs, where, *refs):
    keeps, coded, (d_ref, v_ref, o_ref, out_ref) = refs[:inputs], refs[inputs : 2 * inputs], refs[2 * inputs :]
    width = out_ref.shape[1]
    tile = width // segments
    part = out_ref.shape[0] // 2
    for j in range(2):
        keep_ref, coded_ref = keeps[j % inputs], coded[j % inputs]
        at = pl.ds((j // inputs) * part, part)
        here = pl.ds(pl.multiple_of(where[j] * part, part), part)
        mine = pl.ds(pl.multiple_of((where[j] % 2) * part, part), part)
        codes = codes_of(coded_ref, at, cols, segments)
        made = []
        for n in range(segments):
            start, stop = n * tile, (n + 1) * tile
            ladder = keep_ref[at, start:stop]
            ladder = ladder + decode(coded_ref[at, start:stop], codes, n, cols, start)
            driver = d_ref[mine, start : min(stop, cols)].astype(jnp.float32)
            if stop > cols:
                driver = jnp.concatenate(
                    [driver, jnp.zeros((part, stop - cols), jnp.float32)], axis=1
                )
            gap = v_ref[:, start:stop] - o_ref[here, 0:1]
            whole, code = encode((driver + ladder) / gap)
            made.append(code)
            if n == segments - 1:
                whole = with_codes(whole, made, cols, start)
            out_ref[j * part : (j + 1) * part, start:stop] = whole.astype(jnp.int16)


def updated(keeps, coded, driver, pair_energy, hole_energy, where, cols):
    high, width = keeps[0].shape
    high *= len(keeps)
    whole = lambda x: pl.BlockSpec(x.shape, lambda i, where: (0,) * x.ndim)
    return pl.pallas_call(
        functools.partial(update_kernel, cols, layout(cols)[1], len(keeps)),
        grid_spec=pltpu.PrefetchScalarGridSpec(
            num_scalar_prefetch=1,
            grid=(1,),
            in_specs=[whole(x) for x in (*keeps, *coded)]
            + [pl.BlockSpec((high, cols), lambda i, where: (where[0] // 2, 0))]
            + [whole(pair_energy), whole(hole_energy)],
            out_specs=pl.BlockSpec((high, width), lambda i, where: (0, 0)),
        ),
        out_shape=jax.ShapeDtypeStruct((high, width), jnp.int16),
        compiler_params=params("arbitrary"),
        cost_estimate=SMALL,
        name="update_amplitudes",
    )(where, *keeps, *coded, driver, pair_energy, hole_energy)


def place_kernel(cols, segments, groups, where, *refs):
    out_ref, slots = refs[-2:]
    rows = out_ref.shape[0]
    part = rows // 4
    width = refs[0].shape[1]
    tile = width // segments
    for index in range(2 * groups):
        rel, half = index // 2, index % 2
        ref = refs[index]
        group = where[0] ^ rel
        shift = (group * cols) % LANES
        for j in range(2):
            at = pl.ds(j * part, part)
            codes = codes_of(ref, at, cols, segments)
            pieces = [
                decode(ref[at, n * tile : (n + 1) * tile], codes, n, cols, n * tile)
                for n in range(segments)
            ]
            pieces += [jnp.zeros((part, slots.shape[2] - width), jnp.float32)] * (
                slots.shape[2] > width
            )
            x = pltpu.roll(jnp.concatenate(pieces, axis=1), shift, 1)
            quarter = 2 * ((group // 2) % 2 ^ half) + j
            slots[group, pl.ds(pl.multiple_of(quarter * part, part), part), :] = x
    lane = lax.broadcasted_iota(jnp.int32, (rows, LANES), 1)
    for group in range(groups):
        start = group * cols
        base, shift = start // LANES * LANES, start % LANES
        full = (shift + cols) // LANES * LANES
        if group == groups - 1:
            full = shift + cols
        first = 0
        if shift:
            before = (group - 1) * cols % LANES + cols
            before = before // LANES * LANES
            tail = slots[group - 1, :, before : before + LANES]
            out_ref[:, base : base + LANES] = jnp.where(
                lane < shift, tail, slots[group, :, 0:LANES]
            )
            first = LANES
        out_ref[:, base + first : base + full] = slots[group, :, first:full]


def place(blocks, grp, rows, cols, groups):
    width, segments = layout(cols)
    unit = math.gcd(cols, LANES)
    room = width + LANES * (cols % LANES > unit)
    whole = lambda shape: pl.BlockSpec(shape, lambda i, where: (0,) * len(shape))
    out = (rows, groups * cols)
    return pl.pallas_call(
        functools.partial(place_kernel, cols, segments, groups),
        grid_spec=pltpu.PrefetchScalarGridSpec(
            num_scalar_prefetch=1,
            grid=(1,),
            in_specs=[whole(x.shape) for x in blocks],
            out_specs=whole(out),
            scratch_shapes=[pltpu.VMEM((groups, rows, room), jnp.float32)],
        ),
        out_shape=jax.ShapeDtypeStruct(out, jnp.float32),
        compiler_params=params("arbitrary"),
        name="place_columns",
    )(grp, *blocks)


def spans_of(cols, chip):
    first = chip * 2 * cols % LANES
    second = first + cols
    return first, second // LANES, second % LANES, -(-(second + cols) // LANES)


def half_kernel(cols, segments, late, where, *refs):
    coded, refs = refs[:4], refs[4:]
    if late:
        seam_in, _, out_ref, slots, strips, sems = refs
    else:
        out_ref, seam_ref, slots, strips, sems = refs
    high = coded[0].shape[0]
    part = high // 2
    width = coded[0].shape[1]
    tile = width // segments
    for rel, ref in enumerate(coded):
        group = where[0] ^ rel
        for j in range(2):
            at = pl.ds(j * part, part)
            codes = codes_of(ref, at, cols, segments)
            pieces = [
                decode(ref[at, n * tile : (n + 1) * tile], codes, n, cols, n * tile)
                for n in range(segments)
            ]
            x = pltpu.roll(jnp.concatenate(pieces, axis=1), (group * cols) % LANES, 1)
            slots[group, j * part : (j + 1) * part, :] = x
    lane = lax.broadcasted_iota(jnp.int32, (high, LANES), 1)
    stores = []
    for chip in range(2):
        _, turn, shift, tiles = spans_of(cols, chip)
        one, two = slots.at[2 * chip], slots.at[2 * chip + 1]
        strip = strips.at[chip]
        strip[:, : turn * LANES] = one[:, : turn * LANES]
        seam = turn * LANES
        strip[:, seam : seam + LANES] = jnp.where(
            lane < shift, one[:, seam : seam + LANES], two[:, :LANES]
        )
        strip[:, seam + LANES : tiles * LANES] = two[:, LANES : tiles * LANES - seam]
        top = (chip ^ late) * high
        shared = slice(0, LANES) if chip else slice((tiles - 1) * LANES, tiles * LANES)
        if late:
            strip[:, shared] = strip[:, shared] + seam_in[top : top + high, :]
            start, stop = 0, tiles * LANES
        else:
            seam_ref[top : top + high, :] = strip[:, shared]
            start, stop = (LANES, tiles * LANES) if chip else (0, (tiles - 1) * LANES)
        base = chip * 2 * cols // LANES * LANES
        store = pltpu.make_async_copy(
            strip.at[:, start:stop],
            out_ref.at[top : top + high, base + start : base + stop],
            sems.at[chip],
        )
        store.start()
        stores.append(store)
    for store in stores:
        store.wait()


def place_half(blocks, grp, rows, cols, so_far=None):
    width, segments = layout(cols)
    high = rows // 2
    tiles = max(spans_of(cols, chip)[3] for chip in range(2))
    whole = lambda x: pl.BlockSpec(x.shape, lambda i, where: (0,) * x.ndim)
    anywhere = pl.BlockSpec(memory_space=pl.ANY)
    out = jax.ShapeDtypeStruct((rows, 4 * cols), jnp.float32)
    seam = jax.ShapeDtypeStruct((rows, LANES), jnp.float32)
    late = so_far is not None
    return pl.pallas_call(
        functools.partial(half_kernel, cols, segments, late),
        grid_spec=pltpu.PrefetchScalarGridSpec(
            num_scalar_prefetch=1,
            grid=(1,),
            in_specs=[whole(x) for x in blocks] + [whole(seam), anywhere] * late,
            out_specs=anywhere if late else (anywhere, whole(seam)),
            scratch_shapes=[
                pltpu.VMEM((4, high, width), jnp.float32),
                pltpu.VMEM((2, high, tiles * LANES), jnp.float32),
                pltpu.SemaphoreType.DMA((2,)),
            ],
        ),
        out_shape=out if late else (out, seam),
        input_output_aliases={6: 0} if late else {},
        compiler_params=params("arbitrary"),
        name="place_late_half" if late else "place_early_half",
    )(grp, *blocks, *(so_far[::-1] if late else ()))


def shards(amplitudes, integrals, hole_ints, driver, e_occ, e_virt, occ_pairs, virt_pairs):
    groups, pairs = lax.axis_size("grp"), lax.axis_size("pair")
    grp, pair = lax.axis_index("grp"), lax.axis_index("pair")
    rows = amplitudes.shape[0]
    part = rows // 4
    depth, cols = integrals.shape
    width, _ = layout(cols)

    def swap(x, axis, flip):
        size = lax.axis_size(axis)
        return lax.ppermute(x, axis, [(i, i ^ flip) for i in range(size)])

    own_cols = lax.dynamic_slice_in_dim(amplitudes, grp * cols, cols, 1)
    holes = lax.dynamic_slice_in_dim(hole_ints, pair * rows, rows, 1)
    holes = holes.reshape(pairs, 4, part, rows)
    chip_half, core_at, count = (grp // 2) % 2, grp % 2, pairs // 2
    blocks = list(cut(amplitudes, pair, chip_half, core_at, pairs, depth))
    for j, turn in enumerate(turns(count)):
        moves = [
            (g * pairs + p, g * pairs + (p ^ (2 * turn + g % 2)))
            for g in range(groups)
            for p in range(pairs)
        ]
        blocks[j] = lax.ppermute(blocks[j], ("grp", "pair"), moves)
    own = pack(blocks, (own_cols, holes))
    core = swap(own, "grp", 1)
    chip = swap(own, "grp", 2)

    bits = [1 << n for n in range(pairs.bit_length() - 1)]
    x_first, z_first = bits, bits[1::-1] + bits[2:]
    x_then_far = bits[:1] + bits[2:] + bits[1:2]
    routes = ((z_first, x_then_far), (x_then_far, z_first))

    def listed(value, left):
        if not left:
            return [value]
        return listed(value | left[0], left[1:]) + listed(value, left[1:])

    def place_of(half):
        first = 2 * (chip_half ^ half)
        return jnp.stack([first, first + 1])

    def products(half, *sources):
        given = [(q, k) for q, r in enumerate(routes[half]) for k in listed(r[0], r[1:])]
        order = given + [(q, k ^ routes[half][q][0]) for q, k in given]
        where = jnp.concatenate([jnp.stack([pair, core_at]), place_of(half)])
        made = product(order, where, sources, holes, integrals, own_cols)
        return list(zip(made[:2], made[2:]))

    first = products(0, own, core)
    chip, _ = lax.optimization_barrier((chip, first[0][1]))
    both = swap(chip, "grp", 1)
    second = products(1, chip, both)

    state = [first, second]
    for n in range(len(bits)):
        for half in range(2):
            one, two = routes[half]
            steps = [one[n]] if len(state[half]) == 1 else [one[n], two[n]]
            got = [swap(give, "pair", bit) for (give, _), bit in zip(state[half], steps)]
            keeps = [keep for _, keep in state[half]]
            inner = 3 - len(keeps)
            if n == 0 and half == 0:
                after_first = got[0]
            if n == len(bits) - 1:
                state[half] = (keeps, got)
            elif inner == 2 or one[n + 1 :] == two[n + 1 :]:
                state[half] = [add(keeps, got, inner, cols)]
            else:
                state[half] = [add([k], [g], 1, cols) for k, g in zip(keeps, got)]
    (occ_pairs, virt_pairs), _ = lax.optimization_barrier(
        ((occ_pairs, virt_pairs), after_first)
    )
    occ_energy = lookup(occ_pairs, e_occ)
    virt_energy = lookup(virt_pairs, e_virt)
    hole_energy = jnp.broadcast_to((occ_energy[0] + occ_energy[1])[:, None], (rows, LANES))
    pair_energy = jnp.pad(
        (virt_energy[0] + virt_energy[1])[None, :],
        ((0, 0), (0, width - cols)),
        constant_values=8.0,
    )

    sent = []
    in_halves = groups == 4 and 2 * cols % LANES != 0
    for half in range(2):
        keeps, got = state[half]
        coded = updated(keeps, got, driver, pair_energy, hole_energy, place_of(half), cols)
        here = [coded] + [swap(coded, "grp", 2 * k) for k in range(1, groups // 2)]
        if half and in_halves:
            early = place_half(sent[0], grp[None], rows, cols)
        sent.append([x for own_x in here for x in (own_x, swap(own_x, "grp", 1))])

    if in_halves:
        return place_half(sent[1], grp[None], rows, cols, early)
    ordered = [sent[half][rel] for rel in range(groups) for half in range(2)]
    return place(ordered, grp[None], rows, cols, groups)


def solution(mesh):
    placed = (
        P("pair", None),
        P("pair", "grp"),
        P(),
        P("pair", "grp"),
        P(),
        P(),
        P(None, "pair"),
        P(None, "grp"),
    )
    return jax.shard_map(
        shards, mesh=mesh, in_specs=placed, out_specs=P("pair", None), check_vma=False
    )
```

time: 1170 us -> 80.9 us (0.07)
  waiting for transfers between devices: 1120 us -> 9.04 us
  starting transfers between devices: 0.12 us -> 41.7 us
  Pallas kernels: 0 us -> 26.6 us
  matrix products: 24.2 us -> 0 us
  between operations: 13.2 us -> 0.27 us
    all_gather x3 -> x0, waiting for transfers between devices: 1120 us -> none  [the longest x1 1050 us: shards(): lax.all_gather(integrals, 'pair', axis=0, tiled=True)]
    ppermute x0 -> x25, starting transfers between devices: none -> 41.7 us  [the longest x21 33.3 us: swap(): return lax.ppermute(x, axis, [(i, i ^ flip) for i in range(size)])]
    pallas_call x0 -> x16, Pallas kernels: none -> 26.6 us  [the longest x2 13.5 us: product(): pl.pallas_call(functools.partial(product_kernel, order, parts, cols, segm...]
    dot_general x2 -> x0, matrix products: 24.2 us -> none  [the longest x1 20.9 us: shards(): jnp.dot(left, lax.all_gather(integrals, 'pair', axis=0, tiled=True), pref...]
  transfers between devices with their start and end apart: 3 -> 25, of which waited for: 3 -> 8; matrix products, arithmetic and copies ran while one was open for 2% -> 3% of each run, Pallas kernels for 0% -> 28%
where the time goes in v1:
time: 80.9 us; the launch traced here: 80.6 us
  starting transfers between devices  41.7 us (52%)
  Pallas kernels  26.6 us (33%)
  waiting for transfers between devices  9.04 us (11%)
  other arithmetic  1.5 us (2%)
  local copies, waits for them, and re-layouts  1.37 us (2%)
    ppermute x21, starting transfers between devices, swap(): return lax.ppermute(x, axis, [(i, i ^ flip) for i in range(size)])  33.3 us
    pallas_call x2, Pallas kernels, product(): pl.pallas_call(functools.partial(product_kernel, order, parts, cols, segm...  13.5 us
    ppermute x4, starting transfers between devices, shards(): blocks[j] = lax.ppermute(blocks[j], ('grp', 'pair'), moves)  8.44 us
    ppermute x21, waiting for transfers between devices, swap(): return lax.ppermute(x, axis, [(i, i ^ flip) for i in range(size)])  6.29 us
    pallas_call x8, Pallas kernels, add(): pl.pallas_call(functools.partial(add_kernel, cols, layout(cols)[1], len(k...  5.13 us
    pallas_call x2, Pallas kernels, place_half(): pl.pallas_call(functools.partial(half_kernel, cols, segments, late), grid...  4.21 us
    ppermute x4, waiting for transfers between devices, shards(): blocks[j] = lax.ppermute(blocks[j], ('grp', 'pair'), moves)  2.75 us
    pallas_call x1, Pallas kernels, cut(): pl.pallas_call(cut_kernel, grid_spec=pltpu.PrefetchScalarGridSpec(num_sca...  2.08 us
  transfers between devices with their start and end apart: 25, of which 8 were waited for; matrix products, arithmetic and copies ran while one was open for 3% of the time, Pallas kernels for 28%

profile of v1, /device:TPU:1, one launch (start us, length us, event | category | flops | bytes accessed | tf_op | source)
XLA Modules:
  0.0 80.6 jit_solution(17357433013099187982)
XLA Ops:
  0.1 2.1 %cut_blocks.1 = (bf16[32,1296]{1,0:T(8,128)(2,1)S(1)}, bf16[32,1296]{1,0:T(8,128)(2,1)S(1)}, bf16[32,1296]{1,0:T(8,128)(2,1)S(1)}, bf16[32,1296]{1,0:T(8,128)(2,1)S(1)}) custom-call(s32[3]{0:T(128)S(1)} %pad_add_fusion.3.where, bf16[64,10368]{1,0:T(8,128)(2,1)} %a_ref.1), custom_call_target="tpu_custom_call" | custom-call | flops 1024 | bytes 1024 | tf_op jit(solution)/shard_map/cut_blocks/pallas_call | solution.py:94
  2.2 4.1 %collective-permute-start = (bf16[32,1296]{1,0:T(8,128)(2,1)S(1)}, bf16[32,1296]{1,0:T(8,128)(2,1)S(1)}, u32[]{:S(2)}, u32[]{:S(2)}) collective-permute-start(bf16[32,1296]{1,0:T(8,128)(2,1)S(1)} %get-tuple-element.38), channel_id=1, source_target_pairs={{0,4},{1,5},{2,6},{3,7},{4,0},{5,1},{6,2},{7,3},{8,13},{9,12},{10,... | collective-permute-start | bytes 248840 | tf_op jit(solution)/shard_map/ppermute | solution.py:507
  7.6 3.0 %collective-permute-start.3 = (bf16[32,1296]{1,0:T(8,128)(2,1)S(1)}, bf16[32,1296]{1,0:T(8,128)(2,1)S(1)}, u32[]{:S(2)}, u32[]{:S(2)}) collective-permute-start(bf16[32,1296]{1,0:T(8,128)(2,1)S(1)} %get-tuple-element.41), channel_id=1, source_target_pairs={{0,0},{1,1},{2,2},{3,3},{4,4},{5,5},{6,6},{7,7},{8,9},{9,8},{10,11... | collective-permute-start | bytes 248840 | tf_op jit(solution)/shard_map/ppermute | solution.py:507
  10.6 1.1 %constant_dynamic-slice_fusion.1.refs_4_ = bf16[64,2592]{1,0:T(8,128)(2,1)S(1)} fusion(bf16[64,10368]{1,0:T(8,128)(2,1)} %a_ref.1, s32[]{:T(128)S(6)} %select_n.32), kind=kLoop, calls=%fused_computation.13 | loop fusion | bytes 663556 | tf_op jit(solution)/shard_map/dynamic_slice | solution.py:496
  12.9 1.8 %collective-permute-done.2.refs_2_ = bf16[32,1296]{1,0:T(8,128)(2,1)S(1)} collective-permute-done((bf16[32,1296]{1,0:T(8,128)(2,1)S(1)}, bf16[32,1296]{1,0:T(8,128)(2,1)S(1)}, u32[]{:S(2)}, u32[]{:S(2)}) %collective-permute-start.2) | collective-permute-done | bytes 82976 | tf_op jit(solution)/shard_map/ppermute | solution.py:507
  15.6 1.4 %collective-permute-start.4 = (bf16[4,32,1296]{2,1,0:T(8,128)(2,1)S(1)}, bf16[4,32,1296]{2,1,0:T(8,128)(2,1)S(1)}, u32[]{:S(2)}, u32[]{:S(2)}) collective-permute-start(bf16[4,32,1296]{2,1,0:T(8,128)(2,1)S(1)} %pack_blocks.1.refs_0_), channel_id=1, source_target_pairs={{0,16},{8,24},{16,0},{24,8},{1,17},{9,25},{17,1},{25,9},{2,18},{10... | collective-permute-start | bytes 995336 | tf_op jit(solution)/shard_map/ppermute | solution.py:494
  17.1 7.1 %partial_products.2 = (s16[64,2688]{1,0:T(8,128)(2,1)}, s16[64,2688]{1,0:T(8,128)(2,1)}, f32[64,2688]{1,0:T(8,128)S(1)}, f32[64,2688]{1,0:T(8,128)S(1)}) custom-call(s32[4]{0:T(128)S(1)} %pad_add_fusion.4.where, bf16[4,32,1296]{2,1,0:T(8,128)(2,1)S(1)} %pack_blocks.1.refs_0_, bf16[4,32,1296]{2,1,0:T(8,128)(2,1)S(1)} %collective-permute-done.5.refs_1_, ...), custom_call_target="tpu_custom_call" | custom-call | flops 1024 | bytes 1024 | tf_op jit(solution)/shard_map/partial_products/pallas_call | solution.py:201
  24.1 1.5 %collective-permute-done.4.refs_0_ = bf16[4,32,1296]{2,1,0:T(8,128)(2,1)S(1)} collective-permute-done((bf16[4,32,1296]{2,1,0:T(8,128)(2,1)S(1)}, bf16[4,32,1296]{2,1,0:T(8,128)(2,1)S(1)}, u32[]{:S(2)}, u32[]{:S(2)}) %collective-permute-start.4) | collective-permute-done | bytes 331808 | tf_op jit(solution)/shard_map/ppermute | solution.py:494
  28.0 6.4 %partial_products.3 = (s16[64,2688]{1,0:T(8,128)(2,1)S(1)}, s16[64,2688]{1,0:T(8,128)(2,1)S(1)}, f32[64,2688]{1,0:T(8,128)S(1)}, f32[64,2688]{1,0:T(8,128)S(1)}) custom-call(s32[4]{0:T(128)S(1)} %pad_add_fusion.1.where, bf16[4,32,1296]{2,1,0:T(8,128)(2,1)S(1)} %collective-permute-done.4.refs_0_, bf16[4,32,1296]{2,1,0:T(8,128)(2,1)S(1)} %collective-permute-done.6.refs_1_, ...), custom_call_target="tpu_custom_call" | custom-call | flops 1024 | bytes 1024 | tf_op jit(solution)/shard_map/partial_products/pallas_call | solution.py:201
  36.5 1.6 %add_partial_sums.12 = (s16[32,2688]{1,0:T(8,128)(2,1)S(1)}, f32[32,2688]{1,0:T(8,128)S(1)}) custom-call(f32[64,2688]{1,0:T(8,128)S(1)} %get-tuple-element.42.refs_0_, s16[64,2688]{1,0:T(8,128)(2,1)} %collective-permute-done.13.refs_1_), custom_call_target="tpu_custom_call" | custom-call | flops 1024 | bytes 1024 | tf_op jit(solution)/shard_map/add_partial_sums/pallas_call | solution.py:270
  38.7 1.6 %add_partial_sums.14 = (s16[32,2688]{1,0:T(8,128)(2,1)S(1)}, f32[32,2688]{1,0:T(8,128)S(1)}) custom-call(f32[64,2688]{1,0:T(8,128)S(1)} %get-tuple-element.62.refs_0_, s16[64,2688]{1,0:T(8,128)(2,1)} %collective-permute-done.18.refs_1_), custom_call_target="tpu_custom_call" | custom-call | flops 1024 | bytes 1024 | tf_op jit(solution)/shard_map/add_partial_sums/pallas_call | solution.py:270
  40.2 2.5 %collective-permute-start.19 = (s16[32,2688]{1,0:T(8,128)(2,1)S(1)}, s16[32,2688]{1,0:T(8,128)(2,1)S(1)}, u32[]{:S(2)}, u32[]{:S(2)}) collective-permute-start(s16[32,2688]{1,0:T(8,128)(2,1)S(1)} %get-tuple-element.65), channel_id=1, source_target_pairs={{0,4},{1,5},{2,6},{3,7},{4,0},{5,1},{6,2},{7,3},{8,12},{9,13},{10,... | collective-permute-start | bytes 516104 | tf_op jit(solution)/shard_map/ppermute | solution.py:494
  44.4 3.3 %collective-permute-start.8 = (s16[32,2688]{1,0:T(8,128)(2,1)S(1)}, s16[32,2688]{1,0:T(8,128)(2,1)S(1)}, u32[]{:S(2)}, u32[]{:S(2)}) collective-permute-start(s16[32,2688]{1,0:T(8,128)(2,1)S(1)} %get-tuple-element.47), channel_id=1, source_target_pairs={{0,4},{1,5},{2,6},{3,7},{4,0},{5,1},{6,2},{7,3},{8,12},{9,13},{10,... | collective-permute-start | bytes 516104 | tf_op jit(solution)/shard_map/ppermute | solution.py:494
  49.0 2.0 %collective-permute-start.20 = (s16[16,2688]{1,0:T(8,128)(2,1)S(1)}, s16[16,2688]{1,0:T(8,128)(2,1)S(1)}, u32[]{:S(2)}, u32[]{:S(2)}) collective-permute-start(s16[16,2688]{1,0:T(8,128)(2,1)S(1)} %get-tuple-element.67), channel_id=1, source_target_pairs={{0,4},{1,5},{2,6},{3,7},{4,0},{5,1},{6,2},{7,3},{8,12},{9,13},{10,... | collective-permute-start | bytes 258056 | tf_op jit(solution)/shard_map/ppermute | solution.py:494
  51.2 5.5 %collective-permute-start.21 = (s16[16,2688]{1,0:T(8,128)(2,1)S(1)}, s16[16,2688]{1,0:T(8,128)(2,1)S(1)}, u32[]{:S(2)}, u32[]{:S(2)}) collective-permute-start(s16[16,2688]{1,0:T(8,128)(2,1)S(1)} %get-tuple-element.68), channel_id=1, source_target_pairs={{0,2},{1,3},{2,0},{3,1},{4,6},{5,7},{6,4},{7,5},{8,10},{9,11},{10,... | collective-permute-start | bytes 258056 | tf_op jit(solution)/shard_map/ppermute | solution.py:494
  56.7 3.7 %collective-permute-done.8.refs_1_ = s16[32,2688]{1,0:T(8,128)(2,1)S(1)} collective-permute-done((s16[32,2688]{1,0:T(8,128)(2,1)S(1)}, s16[32,2688]{1,0:T(8,128)(2,1)S(1)}, u32[]{:S(2)}, u32[]{:S(2)}) %collective-permute-start.8) | collective-permute-done | bytes 172064 | tf_op jit(solution)/shard_map/ppermute | solution.py:494
  61.0 2.8 %collective-permute-start.12 = (s16[16,2688]{1,0:T(8,128)(2,1)S(1)}, s16[16,2688]{1,0:T(8,128)(2,1)S(1)}, u32[]{:S(2)}, u32[]{:S(2)}) collective-permute-start(s16[16,2688]{1,0:T(8,128)(2,1)S(1)} %get-tuple-element.55), channel_id=1, source_target_pairs={{0,4},{1,5},{2,6},{3,7},{4,0},{5,1},{6,2},{7,3},{8,12},{9,13},{10,... | collective-permute-start | bytes 258056 | tf_op jit(solution)/shard_map/ppermute | solution.py:494
  65.3 1.3 %collective-permute-start.23 = (s16[32,2688]{1,0:T(8,128)(2,1)S(1)}, s16[32,2688]{1,0:T(8,128)(2,1)S(1)}, u32[]{:S(2)}, u32[]{:S(2)}) collective-permute-start(s16[32,2688]{1,0:T(8,128)(2,1)S(1)} %update_amplitudes.3.refs_0_), channel_id=1, source_target_pairs={{0,16},{8,24},{16,0},{24,8},{1,17},{9,25},{17,1},{25,9},{2,18},{10... | collective-permute-start | bytes 516104 | tf_op jit(solution)/shard_map/ppermute | solution.py:494
  67.6 1.3 %collective-permute-start.15 = (s16[32,2688]{1,0:T(8,128)(2,1)S(1)}, s16[32,2688]{1,0:T(8,128)(2,1)S(1)}, u32[]{:S(2)}, u32[]{:S(2)}) collective-permute-start(s16[32,2688]{1,0:T(8,128)(2,1)S(1)} %update_amplitudes.2.refs_0_), channel_id=1, source_target_pairs={{0,16},{8,24},{16,0},{24,8},{1,17},{9,25},{17,1},{25,9},{2,18},{10... | collective-permute-start | bytes 516104 | tf_op jit(solution)/shard_map/ppermute | solution.py:494
  68.9 3.6 %collective-permute-start.22 = (s16[32,2688]{1,0:T(8,128)(2,1)S(1)}, s16[32,2688]{1,0:T(8,128)(2,1)S(1)}, u32[]{:S(2)}, u32[]{:S(2)}) collective-permute-start(s16[32,2688]{1,0:T(8,128)(2,1)S(1)} %update_amplitudes.3.refs_0_), channel_id=1, source_target_pairs={{0,8},{8,0},{16,24},{24,16},{1,9},{9,1},{17,25},{25,17},{2,10},{10... | collective-permute-start | bytes 516104 | tf_op jit(solution)/shard_map/ppermute | solution.py:494
  72.4 2.0 %collective-permute-start.24 = (s16[32,2688]{1,0:T(8,128)(2,1)S(1)}, s16[32,2688]{1,0:T(8,128)(2,1)S(1)}, u32[]{:S(2)}, u32[]{:S(2)}) collective-permute-start(s16[32,2688]{1,0:T(8,128)(2,1)S(1)} %collective-permute-done.23.refs_2_), channel_id=1, source_target_pairs={{0,8},{8,0},{16,24},{24,16},{1,9},{9,1},{17,25},{25,17},{2,10},{10... | collective-permute-start | bytes 516104 | tf_op jit(solution)/shard_map/ppermute | solution.py:494
  74.4 1.9 %collective-permute-start.16 = (s16[32,2688]{1,0:T(8,128)(2,1)S(1)}, s16[32,2688]{1,0:T(8,128)(2,1)S(1)}, u32[]{:S(2)}, u32[]{:S(2)}) collective-permute-start(s16[32,2688]{1,0:T(8,128)(2,1)S(1)} %collective-permute-done.15.refs_2_), channel_id=1, source_target_pairs={{0,8},{8,0},{16,24},{24,16},{1,9},{9,1},{17,25},{25,17},{2,10},{10... | collective-permute-start | bytes 516104 | tf_op jit(solution)/shard_map/ppermute | solution.py:494
  76.3 2.1 %place_early_half.1 = (f32[64,10368]{1,0:T(8,128)}, f32[64,128]{1,0:T(8,128)S(1)}) custom-call(s32[1]{0:T(128)} %bitcast.where, s16[32,2688]{1,0:T(8,128)(2,1)S(1)} %update_amplitudes.3.refs_0_, s16[32,2688]{1,0:T(8,128)(2,1)S(1)} %collective-permute-done.22.refs_1_, s16[32,2688]{1,0:T(8,128)(2,1)S(1)} %collective-permute-done.23.refs_2_, ...), custom_call_target="tpu_custom_call" | custom-call | tf_op jit(solution)/shard_map/place_early_half/pallas_call | solution.py:464
  78.4 2.1 %place_late_half.1 = f32[64,10368]{1,0:T(8,128)} custom-call(s32[1]{0:T(128)} %bitcast.where, s16[32,2688]{1,0:T(8,128)(2,1)S(1)} %update_amplitudes.2.refs_0_, s16[32,2688]{1,0:T(8,128)(2,1)S(1)} %collective-permute-done.14.refs_1_, s16[32,2688]{1,0:T(8,128)(2,1)S(1)} %collective-permute-done.15.refs_2_, ...), custom_call_target="tpu_custom_call", output_to_operand_aliasing={{}: (6, {})} | custom-call | tf_op jit(solution)/shard_map/place_late_half/pallas_call | solution.py:464
  (71 shorter events, 14.6 us)
Async XLA Ops:
  2.2 9.8 %collective-permute-start = (bf16[32,1296]{1,0:T(8,128)(2,1)S(1)}, bf16[32,1296]{1,0:T(8,128)(2,1)S(1)}, u32[]{:S(2)}, u32[]{:S(2)}) collective-permute-start(bf16[32,1296]{1,0:T(8,128)(2,1)S(1)} %get-tuple-element.38), channel_id=1, source_target_pairs={{0,4},{1,5},{2,6},{3,7},{4,0},{5,1},{6,2},{7,3},{8,13},{9,12},{10,... | collective-permute-start | bytes 248840 | tf_op jit(solution)/shard_map/ppermute | solution.py:507
  6.2 6.7 %collective-permute-start.1 = (bf16[32,1296]{1,0:T(8,128)(2,1)S(1)}, bf16[32,1296]{1,0:T(8,128)(2,1)S(1)}, u32[]{:S(2)}, u32[]{:S(2)}) collective-permute-start(bf16[32,1296]{1,0:T(8,128)(2,1)S(1)} %get-tuple-element.39), channel_id=1, source_target_pairs={{0,6},{1,7},{2,4},{3,5},{4,2},{5,3},{6,0},{7,1},{8,15},{9,14},{10,... | collective-permute-start | bytes 248840 | tf_op jit(solution)/shard_map/ppermute | solution.py:507
  7.3 7.3 %collective-permute-start.2 = (bf16[32,1296]{1,0:T(8,128)(2,1)S(1)}, bf16[32,1296]{1,0:T(8,128)(2,1)S(1)}, u32[]{:S(2)}, u32[]{:S(2)}) collective-permute-start(bf16[32,1296]{1,0:T(8,128)(2,1)S(1)} %get-tuple-element.40), channel_id=1, source_target_pairs={{0,2},{1,3},{2,0},{3,1},{4,6},{5,7},{6,4},{7,5},{8,11},{9,10},{10,... | collective-permute-start | bytes 248840 | tf_op jit(solution)/shard_map/ppermute | solution.py:507
  7.6 7.1 %collective-permute-start.3 = (bf16[32,1296]{1,0:T(8,128)(2,1)S(1)}, bf16[32,1296]{1,0:T(8,128)(2,1)S(1)}, u32[]{:S(2)}, u32[]{:S(2)}) collective-permute-start(bf16[32,1296]{1,0:T(8,128)(2,1)S(1)} %get-tuple-element.41), channel_id=1, source_target_pairs={{0,0},{1,1},{2,2},{3,3},{4,4},{5,5},{6,6},{7,7},{8,9},{9,8},{10,11... | collective-permute-start | bytes 248840 | tf_op jit(solution)/shard_map/ppermute | solution.py:507
  15.6 10.0 %collective-permute-start.4 = (bf16[4,32,1296]{2,1,0:T(8,128)(2,1)S(1)}, bf16[4,32,1296]{2,1,0:T(8,128)(2,1)S(1)}, u32[]{:S(2)}, u32[]{:S(2)}) collective-permute-start(bf16[4,32,1296]{2,1,0:T(8,128)(2,1)S(1)} %pack_blocks.1.refs_0_), channel_id=1, source_target_pairs={{0,16},{8,24},{16,0},{24,8},{1,17},{9,25},{17,1},{25,9},{2,18},{10... | collective-permute-start | bytes 995336 | tf_op jit(solution)/shard_map/ppermute | solution.py:494
  25.6 2.4 %collective-permute-start.6 = (bf16[4,32,1296]{2,1,0:T(8,128)(2,1)S(1)}, bf16[4,32,1296]{2,1,0:T(8,128)(2,1)S(1)}, u32[]{:S(2)}, u32[]{:S(2)}) collective-permute-start(bf16[4,32,1296]{2,1,0:T(8,128)(2,1)S(1)} %collective-permute-done.4.refs_0_), channel_id=1, source_target_pairs={{0,8},{8,0},{16,24},{24,16},{1,9},{9,1},{17,25},{25,17},{2,10},{10... | collective-permute-start | bytes 995336 | tf_op jit(solution)/shard_map/ppermute | solution.py:494
  26.5 10.0 %collective-permute-start.13 = (s16[64,2688]{1,0:T(8,128)(2,1)}, s16[64,2688]{1,0:T(8,128)(2,1)}, u32[]{:S(2)}, u32[]{:S(2)}) collective-permute-start(s16[64,2688]{1,0:T(8,128)(2,1)} %get-tuple-element.56), channel_id=1, source_target_pairs={{0,2},{1,3},{2,0},{3,1},{4,6},{5,7},{6,4},{7,5},{8,10},{9,11},{10,... | collective-permute-start | bytes 1032200 | tf_op jit(solution)/shard_map/ppermute | solution.py:494
  27.0 11.6 %collective-permute-start.18 = (s16[64,2688]{1,0:T(8,128)(2,1)}, s16[64,2688]{1,0:T(8,128)(2,1)}, u32[]{:S(2)}, u32[]{:S(2)}) collective-permute-start(s16[64,2688]{1,0:T(8,128)(2,1)} %get-tuple-element.63), channel_id=1, source_target_pairs={{0,1},{1,0},{2,3},{3,2},{4,5},{5,4},{6,7},{7,6},{8,9},{9,8},{10,11... | collective-permute-start | bytes 1032200 | tf_op jit(solution)/shard_map/ppermute | solution.py:494
  34.4 9.4 %collective-permute-start.7 = (s16[64,2688]{1,0:T(8,128)(2,1)S(1)}, s16[64,2688]{1,0:T(8,128)(2,1)S(1)}, u32[]{:S(2)}, u32[]{:S(2)}) collective-permute-start(s16[64,2688]{1,0:T(8,128)(2,1)S(1)} %get-tuple-element.45), channel_id=1, source_target_pairs={{0,1},{1,0},{2,3},{3,2},{4,5},{5,4},{6,7},{7,6},{8,9},{9,8},{10,11... | collective-permute-start | bytes 1032200 | tf_op jit(solution)/shard_map/ppermute | solution.py:494
  35.2 12.5 %collective-permute-start.9 = (s16[64,2688]{1,0:T(8,128)(2,1)S(1)}, s16[64,2688]{1,0:T(8,128)(2,1)S(1)}, u32[]{:S(2)}, u32[]{:S(2)}) collective-permute-start(s16[64,2688]{1,0:T(8,128)(2,1)S(1)} %get-tuple-element.50), channel_id=1, source_target_pairs={{0,2},{1,3},{2,0},{3,1},{4,6},{5,7},{6,4},{7,5},{8,10},{9,11},{10,... | collective-permute-start | bytes 1032200 | tf_op jit(solution)/shard_map/ppermute | solution.py:494
  38.0 10.8 %collective-permute-start.17 = (s16[32,2688]{1,0:T(8,128)(2,1)S(1)}, s16[32,2688]{1,0:T(8,128)(2,1)S(1)}, u32[]{:S(2)}, u32[]{:S(2)}) collective-permute-start(s16[32,2688]{1,0:T(8,128)(2,1)S(1)} %get-tuple-element.60), channel_id=1, source_target_pairs={{0,1},{1,0},{2,3},{3,2},{4,5},{5,4},{6,7},{7,6},{8,9},{9,8},{10,11... | collective-permute-start | bytes 516104 | tf_op jit(solution)/shard_map/ppermute | solution.py:494
  40.2 10.8 %collective-permute-start.19 = (s16[32,2688]{1,0:T(8,128)(2,1)S(1)}, s16[32,2688]{1,0:T(8,128)(2,1)S(1)}, u32[]{:S(2)}, u32[]{:S(2)}) collective-permute-start(s16[32,2688]{1,0:T(8,128)(2,1)S(1)} %get-tuple-element.65), channel_id=1, source_target_pairs={{0,4},{1,5},{2,6},{3,7},{4,0},{5,1},{6,2},{7,3},{8,12},{9,13},{10,... | collective-permute-start | bytes 516104 | tf_op jit(solution)/shard_map/ppermute | solution.py:494
  44.4 16.1 %collective-permute-start.8 = (s16[32,2688]{1,0:T(8,128)(2,1)S(1)}, s16[32,2688]{1,0:T(8,128)(2,1)S(1)}, u32[]{:S(2)}, u32[]{:S(2)}) collective-permute-start(s16[32,2688]{1,0:T(8,128)(2,1)S(1)} %get-tuple-element.47), channel_id=1, source_target_pairs={{0,4},{1,5},{2,6},{3,7},{4,0},{5,1},{6,2},{7,3},{8,12},{9,13},{10,... | collective-permute-start | bytes 516104 | tf_op jit(solution)/shard_map/ppermute | solution.py:494
  48.3 12.5 %collective-permute-start.10 = (s16[32,2688]{1,0:T(8,128)(2,1)S(1)}, s16[32,2688]{1,0:T(8,128)(2,1)S(1)}, u32[]{:S(2)}, u32[]{:S(2)}) collective-permute-start(s16[32,2688]{1,0:T(8,128)(2,1)S(1)} %get-tuple-element.52), channel_id=1, source_target_pairs={{0,1},{1,0},{2,3},{3,2},{4,5},{5,4},{6,7},{7,6},{8,9},{9,8},{10,11... | collective-permute-start | bytes 516104 | tf_op jit(solution)/shard_map/ppermute | solution.py:494
  49.0 14.8 %collective-permute-start.20 = (s16[16,2688]{1,0:T(8,128)(2,1)S(1)}, s16[16,2688]{1,0:T(8,128)(2,1)S(1)}, u32[]{:S(2)}, u32[]{:S(2)}) collective-permute-start(s16[16,2688]{1,0:T(8,128)(2,1)S(1)} %get-tuple-element.67), channel_id=1, source_target_pairs={{0,4},{1,5},{2,6},{3,7},{4,0},{5,1},{6,2},{7,3},{8,12},{9,13},{10,... | collective-permute-start | bytes 258056 | tf_op jit(solution)/shard_map/ppermute | solution.py:494
  51.2 13.1 %collective-permute-start.21 = (s16[16,2688]{1,0:T(8,128)(2,1)S(1)}, s16[16,2688]{1,0:T(8,128)(2,1)S(1)}, u32[]{:S(2)}, u32[]{:S(2)}) collective-permute-start(s16[16,2688]{1,0:T(8,128)(2,1)S(1)} %get-tuple-element.68), channel_id=1, source_target_pairs={{0,2},{1,3},{2,0},{3,1},{4,6},{5,7},{6,4},{7,5},{8,10},{9,11},{10,... | collective-permute-start | bytes 258056 | tf_op jit(solution)/shard_map/ppermute | solution.py:494
  60.7 5.9 %collective-permute-start.11 = (s16[16,2688]{1,0:T(8,128)(2,1)S(1)}, s16[16,2688]{1,0:T(8,128)(2,1)S(1)}, u32[]{:S(2)}, u32[]{:S(2)}) collective-permute-start(s16[16,2688]{1,0:T(8,128)(2,1)S(1)} %get-tuple-element.54), channel_id=1, source_target_pairs={{0,2},{1,3},{2,0},{3,1},{4,6},{5,7},{6,4},{7,5},{8,10},{9,11},{10,... | collective-permute-start | bytes 258056 | tf_op jit(solution)/shard_map/ppermute | solution.py:494
  61.0 5.7 %collective-permute-start.12 = (s16[16,2688]{1,0:T(8,128)(2,1)S(1)}, s16[16,2688]{1,0:T(8,128)(2,1)S(1)}, u32[]{:S(2)}, u32[]{:S(2)}) collective-permute-start(s16[16,2688]{1,0:T(8,128)(2,1)S(1)} %get-tuple-element.55), channel_id=1, source_target_pairs={{0,4},{1,5},{2,6},{3,7},{4,0},{5,1},{6,2},{7,3},{8,12},{9,13},{10,... | collective-permute-start | bytes 258056 | tf_op jit(solution)/shard_map/ppermute | solution.py:494
  65.3 7.2 %collective-permute-start.23 = (s16[32,2688]{1,0:T(8,128)(2,1)S(1)}, s16[32,2688]{1,0:T(8,128)(2,1)S(1)}, u32[]{:S(2)}, u32[]{:S(2)}) collective-permute-start(s16[32,2688]{1,0:T(8,128)(2,1)S(1)} %update_amplitudes.3.refs_0_), channel_id=1, source_target_pairs={{0,16},{8,24},{16,0},{24,8},{1,17},{9,25},{17,1},{25,9},{2,18},{10... | collective-permute-start | bytes 516104 | tf_op jit(solution)/shard_map/ppermute | solution.py:494
  67.6 6.9 %collective-permute-start.15 = (s16[32,2688]{1,0:T(8,128)(2,1)S(1)}, s16[32,2688]{1,0:T(8,128)(2,1)S(1)}, u32[]{:S(2)}, u32[]{:S(2)}) collective-permute-start(s16[32,2688]{1,0:T(8,128)(2,1)S(1)} %update_amplitudes.2.refs_0_), channel_id=1, source_target_pairs={{0,16},{8,24},{16,0},{24,8},{1,17},{9,25},{17,1},{25,9},{2,18},{10... | collective-permute-start | bytes 516104 | tf_op jit(solution)/shard_map/ppermute | solution.py:494
  68.9 7.5 %collective-permute-start.22 = (s16[32,2688]{1,0:T(8,128)(2,1)S(1)}, s16[32,2688]{1,0:T(8,128)(2,1)S(1)}, u32[]{:S(2)}, u32[]{:S(2)}) collective-permute-start(s16[32,2688]{1,0:T(8,128)(2,1)S(1)} %update_amplitudes.3.refs_0_), channel_id=1, source_target_pairs={{0,8},{8,0},{16,24},{24,16},{1,9},{9,1},{17,25},{25,17},{2,10},{10... | collective-permute-start | bytes 516104 | tf_op jit(solution)/shard_map/ppermute | solution.py:494
  72.4 3.9 %collective-permute-start.24 = (s16[32,2688]{1,0:T(8,128)(2,1)S(1)}, s16[32,2688]{1,0:T(8,128)(2,1)S(1)}, u32[]{:S(2)}, u32[]{:S(2)}) collective-permute-start(s16[32,2688]{1,0:T(8,128)(2,1)S(1)} %collective-permute-done.23.refs_2_), channel_id=1, source_target_pairs={{0,8},{8,0},{16,24},{24,16},{1,9},{9,1},{17,25},{25,17},{2,10},{10... | collective-permute-start | bytes 516104 | tf_op jit(solution)/shard_map/ppermute | solution.py:494
  74.4 4.0 %collective-permute-start.14 = (s16[32,2688]{1,0:T(8,128)(2,1)S(1)}, s16[32,2688]{1,0:T(8,128)(2,1)S(1)}, u32[]{:S(2)}, u32[]{:S(2)}) collective-permute-start(s16[32,2688]{1,0:T(8,128)(2,1)S(1)} %update_amplitudes.2.refs_0_), channel_id=1, source_target_pairs={{0,8},{8,0},{16,24},{24,16},{1,9},{9,1},{17,25},{25,17},{2,10},{10... | collective-permute-start | bytes 516104 | tf_op jit(solution)/shard_map/ppermute | solution.py:494
  74.4 4.0 %collective-permute-start.16 = (s16[32,2688]{1,0:T(8,128)(2,1)S(1)}, s16[32,2688]{1,0:T(8,128)(2,1)S(1)}, u32[]{:S(2)}, u32[]{:S(2)}) collective-permute-start(s16[32,2688]{1,0:T(8,128)(2,1)S(1)} %collective-permute-done.15.refs_2_), channel_id=1, source_target_pairs={{0,8},{8,0},{16,24},{24,16},{1,9},{9,1},{17,25},{25,17},{2,10},{10... | collective-permute-start | bytes 516104 | tf_op jit(solution)/shard_map/ppermute | solution.py:494
  (9 other events, 139.7 us)

commit v2 on v1

--- a/solution.py
+++ b/solution.py
@@ -70,22 +70,18 @@
     )
 
 
-def turns(count):
-    return [*range(count // 2, count), *range(count // 2 - 1, -1, -1)]
-
-
 def cut_kernel(where, a_ref, *refs):
     outs, slots = refs[:-1], refs[-1]
     count, _, depth = slots.shape
     for n in range(2 * count):
         k = where[0] ^ n
 
-        @pl.when(k % 2 == where[2])
+        @pl.when(k // count == where[2])
         def _():
-            slots[k // 2] = a_ref[:, n * depth : (n + 1) * depth]
-
-    for j, turn in enumerate(turns(count)):
-        outs[j][...] = slots[turn]
+            slots[k % count] = a_ref[:, n * depth : (n + 1) * depth]
+
+    for j in range(count):
+        outs[j][...] = slots[(j + 1) % count]
 
 
 def cut(amplitudes, pair, part, core, pairs, depth):
@@ -143,15 +139,16 @@
         spot = {entry: n for n, entry in enumerate(order)}
         for s, ref in enumerate(a_refs):
             swapped = where[1] ^ s
-            for j, turn in enumerate(turns(count)):
+            for j in range(count):
+                low = (j + 1) % count
                 for q in range(parts):
-                    even, odd = spot[q, 2 * turn], spot[q, 2 * turn + 1]
-                    at = jnp.where(swapped == 0, even, odd) * part
+                    near, far = spot[q, low], spot[q, low + count]
+                    at = jnp.where(swapped == 0, near, far) * part
                     at = pl.ds(pl.multiple_of(at, part), part)
                     block = ref.at[j, q * part : (q + 1) * part]
                     left[at, :] = block[:, :main]
                     left_rest[at, : depth - main] = block[:, main:]
-                    source = where[0] ^ (2 * turn + swapped)
+                    source = where[0] ^ (low + count * swapped)
                     left_rest[at, second : second + rows] = h_ref[source, where[2 + q]]
 
     right_rest[: depth - main, :] = v_ref[main:, :]
@@ -184,7 +181,7 @@
     return main, -(-(depth - main) // 16) * 16
 
 
-def product(order, where, sources, holes, integrals, own_cols):
+def product(order, where, sources, holes, integrals, own_cols, give_space):
     parts = len(sources)
     _, high_block, depth = sources[0].shape
     part = high_block // parts
@@ -217,7 +214,7 @@
                 pltpu.VMEM((total // 2, LANES), jnp.float32),
             ],
         ),
-        out_shape=[jax.ShapeDtypeStruct((high, width), jnp.int16)] * parts
+        out_shape=[give_space((high, width), jnp.int16)] * parts
         + [jax.ShapeDtypeStruct((high, width), jnp.float32)] * parts,
         compiler_params=params("arbitrary"),
         cost_estimate=SMALL,
@@ -496,17 +493,26 @@
     own_cols = lax.dynamic_slice_in_dim(amplitudes, grp * cols, cols, 1)
     holes = lax.dynamic_slice_in_dim(hole_ints, pair * rows, rows, 1)
     holes = holes.reshape(pairs, 4, part, rows)
+    occ_energy = lookup(occ_pairs, e_occ)
+    virt_energy = lookup(virt_pairs, e_virt)
+    hole_energy = jnp.broadcast_to((occ_energy[0] + occ_energy[1])[:, None], (rows, LANES))
+    pair_energy = jnp.pad(
+        (virt_energy[0] + virt_energy[1])[None, :],
+        ((0, 0), (0, width - cols)),
+        constant_values=8.0,
+    )
+
     chip_half, core_at, count = (grp // 2) % 2, grp % 2, pairs // 2
     blocks = list(cut(amplitudes, pair, chip_half, core_at, pairs, depth))
-    for j, turn in enumerate(turns(count)):
+    for j in range(count):
         moves = [
-            (g * pairs + p, g * pairs + (p ^ (2 * turn + g % 2)))
+            (g * pairs + p, g * pairs + (p ^ (g % 2 * count + (j + 1) % count)))
             for g in range(groups)
             for p in range(pairs)
         ]
         blocks[j] = lax.ppermute(blocks[j], ("grp", "pair"), moves)
-    own = pack(blocks, (own_cols, holes))
-    core = swap(own, "grp", 1)
+    own = pack(blocks, (own_cols, holes, pair_energy, hole_energy))
+    core = pack([swap(x, "grp", 1) for x in blocks], ())
     chip = swap(own, "grp", 2)
 
     bits = [1 << n for n in range(pairs.bit_length() - 1)]
@@ -527,7 +533,8 @@
         given = [(q, k) for q, r in enumerate(routes[half]) for k in listed(r[0], r[1:])]
         order = given + [(q, k ^ routes[half][q][0]) for q, k in given]
         where = jnp.concatenate([jnp.stack([pair, core_at]), place_of(half)])
-        made = product(order, where, sources, holes, integrals, own_cols)
+        space = jax.ShapeDtypeStruct if half else pltpu.HBM
+        made = product(order, where, sources, holes, integrals, own_cols, space)
         return list(zip(made[:2], made[2:]))
 
     first = products(0, own, core)
@@ -543,26 +550,12 @@
             got = [swap(give, "pair", bit) for (give, _), bit in zip(state[half], steps)]
             keeps = [keep for _, keep in state[half]]
             inner = 3 - len(keeps)
-            if n == 0 and half == 0:
-                after_first = got[0]
             if n == len(bits) - 1:
                 state[half] = (keeps, got)
             elif inner == 2 or one[n + 1 :] == two[n + 1 :]:
                 state[half] = [add(keeps, got, inner, cols)]
             else:
                 state[half] = [add([k], [g], 1, cols) for k, g in zip(keeps, got)]
-    (occ_pairs, virt_pairs), _ = lax.optimization_barrier(
-        ((occ_pairs, virt_pairs), after_first)
-    )
-    occ_energy = lookup(occ_pairs, e_occ)
-    virt_energy = lookup(virt_pairs, e_virt)
-    hole_energy = jnp.broadcast_to((occ_energy[0] + occ_energy[1])[:, None], (rows, LANES))
-    pair_energy = jnp.pad(
-        (virt_energy[0] + virt_energy[1])[None, :],
-        ((0, 0), (0, width - cols)),
-        constant_values=8.0,
-    )
-
     sent = []
     in_halves = groups == 4 and 2 * cols % LANES != 0
     for half in range(2):

time: 80.9 us -> 79.5 us (0.983)
  starting transfers between devices: 41.7 us -> 34.9 us
  waiting for transfers between devices: 9.04 us -> 15 us
  Pallas kernels: 26.6 us -> 24.6 us
  other arithmetic: 1.5 us -> 2.94 us
    ppermute x21 -> x24, waiting for transfers between devices: 6.29 us -> 14.4 us  [swap(): return lax.ppermute(x, axis, [(i, i ^ flip) for i in range(size)])]
    ppermute x21 -> x24, starting transfers between devices: 33.3 us -> 25.7 us  [swap(): return lax.ppermute(x, axis, [(i, i ^ flip) for i in range(size)])]
    ppermute x4, waiting for transfers between devices: 2.75 us -> 0.56 us  [shards(): blocks[j] = lax.ppermute(blocks[j], ('grp', 'pair'), moves)]
    pallas_call x8, Pallas kernels: 5.13 us -> 3.17 us  [add(): pl.pallas_call(functools.partial(add_kernel, cols, layout(cols)[1], len(k...]
    reduce_sum x2, other arithmetic: 1.1 us -> 2.54 us  [lookup(): return jnp.sum(picked, axis=-1)]
    ppermute x4, starting transfers between devices: 8.44 us -> 9.25 us  [shards(): blocks[j] = lax.ppermute(blocks[j], ('grp', 'pair'), moves)]
  transfers between devices with their start and end apart: 25 -> 28, of which waited for: 8 -> 11; matrix products, arithmetic and copies ran while one was open for 3% -> 5% of each run, Pallas kernels for 28% -> 26%
where the time goes in v2:
time: 79.5 us; the launch traced here: 79.1 us
  starting transfers between devices  34.9 us (44%)
  Pallas kernels  24.6 us (31%)
  waiting for transfers between devices  15 us (19%)
  other arithmetic  2.94 us (4%)
  local copies, waits for them, and re-layouts  1.36 us (2%)
    ppermute x24, starting transfers between devices, swap(): return lax.ppermute(x, axis, [(i, i ^ flip) for i in range(size)])  25.7 us
    ppermute x24, waiting for transfers between devices, swap(): return lax.ppermute(x, axis, [(i, i ^ flip) for i in range(size)])  14.4 us
    pallas_call x2, Pallas kernels, product(): pl.pallas_call(functools.partial(product_kernel, order, parts, cols, segm...  13.5 us
    ppermute x4, starting transfers between devices, shards(): blocks[j] = lax.ppermute(blocks[j], ('grp', 'pair'), moves)  9.25 us
    pallas_call x2, Pallas kernels, place_half(): pl.pallas_call(functools.partial(half_kernel, cols, segments, late), grid...  4.21 us
    pallas_call x8, Pallas kernels, add(): pl.pallas_call(functools.partial(add_kernel, cols, layout(cols)[1], len(k...  3.17 us
    reduce_sum x2, other arithmetic, lookup(): return jnp.sum(picked, axis=-1)  2.54 us
    pallas_call x1, Pallas kernels, cut(): pl.pallas_call(cut_kernel, grid_spec=pltpu.PrefetchScalarGridSpec(num_sca...  2.04 us
  transfers between devices with their start and end apart: 28, of which 11 were waited for; matrix products, arithmetic and copies ran while one was open for 5% of the time, Pallas kernels for 26%

profile of v2, /device:TPU:1, one launch (start us, length us, event | category | flops | bytes accessed | tf_op | source)
XLA Modules:
  0.0 79.1 jit_solution(14859036285702321658)
XLA Ops:
  0.1 2.0 %cut_blocks.1 = (bf16[32,1296]{1,0:T(8,128)(2,1)S(1)}, bf16[32,1296]{1,0:T(8,128)(2,1)S(1)}, bf16[32,1296]{1,0:T(8,128)(2,1)S(1)}, bf16[32,1296]{1,0:T(8,128)(2,1)S(1)}) custom-call(s32[3]{0:T(128)S(1)} %pad_add_fusion.3.where, bf16[64,10368]{1,0:T(8,128)(2,1)} %a_ref.1), custom_call_target="tpu_custom_call" | custom-call | flops 1024 | bytes 1024 | tf_op jit(solution)/shard_map/cut_blocks/pallas_call | solution.py:90
  2.1 4.1 %collective-permute-start = (bf16[32,1296]{1,0:T(8,128)(2,1)S(1)}, bf16[32,1296]{1,0:T(8,128)(2,1)S(1)}, u32[]{:S(2)}, u32[]{:S(2)}) collective-permute-start(bf16[32,1296]{1,0:T(8,128)(2,1)S(1)} %get-tuple-element.36), channel_id=1, source_target_pairs={{0,1},{1,0},{2,3},{3,2},{4,5},{5,4},{6,7},{7,6},{8,13},{9,12},{10,... | collective-permute-start | bytes 248840 | tf_op jit(solution)/shard_map/ppermute | solution.py:513
  6.2 1.1 %collective-permute-start.1 = (bf16[32,1296]{1,0:T(8,128)(2,1)S(1)}, bf16[32,1296]{1,0:T(8,128)(2,1)S(1)}, u32[]{:S(2)}, u32[]{:S(2)}) collective-permute-start(bf16[32,1296]{1,0:T(8,128)(2,1)S(1)} %get-tuple-element.37), channel_id=1, source_target_pairs={{0,2},{1,3},{2,0},{3,1},{4,6},{5,7},{6,4},{7,5},{8,14},{9,15},{10,... | collective-permute-start | bytes 248840 | tf_op jit(solution)/shard_map/ppermute | solution.py:513
  7.3 2.1 %collective-permute-start.2 = (bf16[32,1296]{1,0:T(8,128)(2,1)S(1)}, bf16[32,1296]{1,0:T(8,128)(2,1)S(1)}, u32[]{:S(2)}, u32[]{:S(2)}) collective-permute-start(bf16[32,1296]{1,0:T(8,128)(2,1)S(1)} %get-tuple-element.38), channel_id=1, source_target_pairs={{0,3},{1,2},{2,1},{3,0},{4,7},{5,6},{6,5},{7,4},{8,15},{9,14},{10,... | collective-permute-start | bytes 248840 | tf_op jit(solution)/shard_map/ppermute | solution.py:513
  9.5 1.9 %collective-permute-start.3 = (bf16[32,1296]{1,0:T(8,128)(2,1)S(1)}, bf16[32,1296]{1,0:T(8,128)(2,1)S(1)}, u32[]{:S(2)}, u32[]{:S(2)}) collective-permute-start(bf16[32,1296]{1,0:T(8,128)(2,1)S(1)} %get-tuple-element.39), channel_id=1, source_target_pairs={{0,0},{1,1},{2,2},{3,3},{4,4},{5,5},{6,6},{7,7},{8,12},{9,13},{10,... | collective-permute-start | bytes 248840 | tf_op jit(solution)/shard_map/ppermute | solution.py:513
  12.3 1.7 %select_reduce_fusion = f32[2,2592]{1,0:T(2,128)S(1)} fusion(f32[288]{0:T(512)} %param.13, s32[2,2592]{1,0:T(2,128)} %param.15), kind=kLoop, calls=%fused_computation | loop fusion | flops 4473792 | bytes 42624 | tf_op jit(solution)/shard_map/reduce_sum | solution.py:22
  14.0 1.2 %constant_dynamic-slice_fusion.1.refs_4_ = bf16[64,2592]{1,0:T(8,128)(2,1)S(1)} fusion(bf16[64,10368]{1,0:T(8,128)(2,1)} %a_ref.1, s32[]{:T(128)S(6)} %select_n.32), kind=kLoop, calls=%fused_computation.13 | loop fusion | bytes 663556 | tf_op jit(solution)/shard_map/dynamic_slice | solution.py:493
  16.0 1.3 %collective-permute-start.4 = (bf16[4,32,1296]{2,1,0:T(8,128)(2,1)S(1)}, bf16[4,32,1296]{2,1,0:T(8,128)(2,1)S(1)}, u32[]{:S(2)}, u32[]{:S(2)}) collective-permute-start(bf16[4,32,1296]{2,1,0:T(8,128)(2,1)S(1)} %pack_blocks.2.refs_0_), channel_id=1, source_target_pairs={{0,16},{8,24},{16,0},{24,8},{1,17},{9,25},{17,1},{25,9},{2,18},{10... | collective-permute-start | bytes 995336 | tf_op jit(solution)/shard_map/ppermute | solution.py:491
  19.3 7.0 %partial_products.2 = (s16[64,2688]{1,0:T(8,128)(2,1)}, s16[64,2688]{1,0:T(8,128)(2,1)}, f32[64,2688]{1,0:T(8,128)S(1)}, f32[64,2688]{1,0:T(8,128)S(1)}) custom-call(s32[4]{0:T(128)S(1)} %pad_add_fusion.4.where, bf16[4,32,1296]{2,1,0:T(8,128)(2,1)S(1)} %pack_blocks.2.refs_0_, bf16[4,32,1296]{2,1,0:T(8,128)(2,1)S(1)} %pack_blocks.3.refs_1_, ...), custom_call_target="tpu_custom_call" | custom-call | flops 1024 | bytes 1024 | tf_op jit(solution)/shard_map/partial_products/pallas_call | solution.py:198
  27.6 1.2 %collective-permute-start.21 = (s16[64,2688]{1,0:T(8,128)(2,1)}, s16[64,2688]{1,0:T(8,128)(2,1)S(1)}, u32[]{:S(2)}, u32[]{:S(2)}) collective-permute-start(s16[64,2688]{1,0:T(8,128)(2,1)} %get-tuple-element.59), channel_id=1, source_target_pairs={{0,1},{1,0},{2,3},{3,2},{4,5},{5,4},{6,7},{7,6},{8,9},{9,8},{10,11... | collective-permute-start | bytes 1032200 | tf_op jit(solution)/shard_map/ppermute | solution.py:491
  28.9 6.4 %partial_products.3 = (s16[64,2688]{1,0:T(8,128)(2,1)S(1)}, s16[64,2688]{1,0:T(8,128)(2,1)S(1)}, f32[64,2688]{1,0:T(8,128)S(1)}, f32[64,2688]{1,0:T(8,128)S(1)}) custom-call(s32[4]{0:T(128)S(1)} %pad_add_fusion.1.where, bf16[4,32,1296]{2,1,0:T(8,128)(2,1)S(1)} %collective-permute-done.4.refs_0_, bf16[4,32,1296]{2,1,0:T(8,128)(2,1)S(1)} %collective-permute-done.9.refs_1_, ...), custom_call_target="tpu_custom_call" | custom-call | flops 1024 | bytes 1024 | tf_op jit(solution)/shard_map/partial_products/pallas_call | solution.py:198
  38.9 1.9 %collective-permute-start.22 = (s16[32,2688]{1,0:T(8,128)(2,1)S(1)}, s16[32,2688]{1,0:T(8,128)(2,1)S(1)}, u32[]{:S(2)}, u32[]{:S(2)}) collective-permute-start(s16[32,2688]{1,0:T(8,128)(2,1)S(1)} %get-tuple-element.61), channel_id=1, source_target_pairs={{0,4},{1,5},{2,6},{3,7},{4,0},{5,1},{6,2},{7,3},{8,12},{9,13},{10,... | collective-permute-start | bytes 516104 | tf_op jit(solution)/shard_map/ppermute | solution.py:491
  40.8 3.4 %collective-permute-done.10.refs_1_ = s16[64,2688]{1,0:T(8,128)(2,1)S(1)} collective-permute-done((s16[64,2688]{1,0:T(8,128)(2,1)S(1)}, s16[64,2688]{1,0:T(8,128)(2,1)S(1)}, u32[]{:S(2)}, u32[]{:S(2)}) %collective-permute-start.10) | collective-permute-done | bytes 344096 | tf_op jit(solution)/shard_map/ppermute | solution.py:491
  44.8 2.1 %collective-permute-start.11 = (s16[32,2688]{1,0:T(8,128)(2,1)S(1)}, s16[32,2688]{1,0:T(8,128)(2,1)S(1)}, u32[]{:S(2)}, u32[]{:S(2)}) collective-permute-start(s16[32,2688]{1,0:T(8,128)(2,1)S(1)} %get-tuple-element.45), channel_id=1, source_target_pairs={{0,4},{1,5},{2,6},{3,7},{4,0},{5,1},{6,2},{7,3},{8,12},{9,13},{10,... | collective-permute-start | bytes 516104 | tf_op jit(solution)/shard_map/ppermute | solution.py:491
  47.0 1.1 %collective-permute-done.12.refs_1_ = s16[64,2688]{1,0:T(8,128)(2,1)S(1)} collective-permute-done((s16[64,2688]{1,0:T(8,128)(2,1)S(1)}, s16[64,2688]{1,0:T(8,128)(2,1)S(1)}, u32[]{:S(2)}, u32[]{:S(2)}) %collective-permute-start.12) | collective-permute-done | bytes 344096 | tf_op jit(solution)/shard_map/ppermute | solution.py:491
  48.6 1.1 %collective-permute-start.13 = (s16[32,2688]{1,0:T(8,128)(2,1)S(1)}, s16[32,2688]{1,0:T(8,128)(2,1)S(1)}, u32[]{:S(2)}, u32[]{:S(2)}) collective-permute-start(s16[32,2688]{1,0:T(8,128)(2,1)S(1)} %get-tuple-element.50), channel_id=1, source_target_pairs={{0,1},{1,0},{2,3},{3,2},{4,5},{5,4},{6,7},{7,6},{8,9},{9,8},{10,11... | collective-permute-start | bytes 516104 | tf_op jit(solution)/shard_map/ppermute | solution.py:491
  50.5 2.3 %collective-permute-start.24 = (s16[16,2688]{1,0:T(8,128)(2,1)S(1)}, s16[16,2688]{1,0:T(8,128)(2,1)S(1)}, u32[]{:S(2)}, u32[]{:S(2)}) collective-permute-start(s16[16,2688]{1,0:T(8,128)(2,1)S(1)} %get-tuple-element.64), channel_id=1, source_target_pairs={{0,2},{1,3},{2,0},{3,1},{4,6},{5,7},{6,4},{7,5},{8,10},{9,11},{10,... | collective-permute-start | bytes 258056 | tf_op jit(solution)/shard_map/ppermute | solution.py:491
  52.8 7.2 %collective-permute-done.11.refs_1_ = s16[32,2688]{1,0:T(8,128)(2,1)S(1)} collective-permute-done((s16[32,2688]{1,0:T(8,128)(2,1)S(1)}, s16[32,2688]{1,0:T(8,128)(2,1)S(1)}, u32[]{:S(2)}, u32[]{:S(2)}) %collective-permute-start.11) | collective-permute-done | bytes 172064 | tf_op jit(solution)/shard_map/ppermute | solution.py:491
  60.6 1.6 %collective-permute-start.15 = (s16[16,2688]{1,0:T(8,128)(2,1)S(1)}, s16[16,2688]{1,0:T(8,128)(2,1)S(1)}, u32[]{:S(2)}, u32[]{:S(2)}) collective-permute-start(s16[16,2688]{1,0:T(8,128)(2,1)S(1)} %get-tuple-element.53), channel_id=1, source_target_pairs={{0,4},{1,5},{2,6},{3,7},{4,0},{5,1},{6,2},{7,3},{8,12},{9,13},{10,... | collective-permute-start | bytes 258056 | tf_op jit(solution)/shard_map/ppermute | solution.py:491
  63.7 1.3 %collective-permute-done.15.refs_3_ = s16[16,2688]{1,0:T(8,128)(2,1)S(1)} collective-permute-done((s16[16,2688]{1,0:T(8,128)(2,1)S(1)}, s16[16,2688]{1,0:T(8,128)(2,1)S(1)}, u32[]{:S(2)}, u32[]{:S(2)}) %collective-permute-start.15) | collective-permute-done | bytes 86048 | tf_op jit(solution)/shard_map/ppermute | solution.py:491
  66.1 3.9 %collective-permute-start.25 = (s16[32,2688]{1,0:T(8,128)(2,1)S(1)}, s16[32,2688]{1,0:T(8,128)(2,1)S(1)}, u32[]{:S(2)}, u32[]{:S(2)}) collective-permute-start(s16[32,2688]{1,0:T(8,128)(2,1)S(1)} %update_amplitudes.3.refs_0_), channel_id=1, source_target_pairs={{0,8},{8,0},{16,24},{24,16},{1,9},{9,1},{17,25},{25,17},{2,10},{10... | collective-permute-start | bytes 516104 | tf_op jit(solution)/shard_map/ppermute | solution.py:491
  71.1 3.8 %collective-permute-start.18 = (s16[32,2688]{1,0:T(8,128)(2,1)S(1)}, s16[32,2688]{1,0:T(8,128)(2,1)S(1)}, u32[]{:S(2)}, u32[]{:S(2)}) collective-permute-start(s16[32,2688]{1,0:T(8,128)(2,1)S(1)} %collective-permute-done.17.refs_2_), channel_id=1, source_target_pairs={{0,8},{8,0},{16,24},{24,16},{1,9},{9,1},{17,25},{25,17},{2,10},{10... | collective-permute-start | bytes 516104 | tf_op jit(solution)/shard_map/ppermute | solution.py:491
  74.9 2.1 %place_early_half.1 = (f32[64,10368]{1,0:T(8,128)}, f32[64,128]{1,0:T(8,128)S(1)}) custom-call(s32[1]{0:T(128)} %bitcast.where, s16[32,2688]{1,0:T(8,128)(2,1)S(1)} %update_amplitudes.3.refs_0_, s16[32,2688]{1,0:T(8,128)(2,1)S(1)} %collective-permute-done.25.refs_1_, s16[32,2688]{1,0:T(8,128)(2,1)S(1)} %collective-permute-done.26.refs_2_, ...), custom_call_target="tpu_custom_call" | custom-call | tf_op jit(solution)/shard_map/place_early_half/pallas_call | solution.py:461
  77.0 2.1 %place_late_half.1 = f32[64,10368]{1,0:T(8,128)} custom-call(s32[1]{0:T(128)} %bitcast.where, s16[32,2688]{1,0:T(8,128)(2,1)S(1)} %update_amplitudes.2.refs_0_, s16[32,2688]{1,0:T(8,128)(2,1)S(1)} %collective-permute-done.16.refs_1_, s16[32,2688]{1,0:T(8,128)(2,1)S(1)} %collective-permute-done.17.refs_2_, ...), custom_call_target="tpu_custom_call", output_to_operand_aliasing={{}: (6, {})} | custom-call | tf_op jit(solution)/shard_map/place_late_half/pallas_call | solution.py:461
  (70 shorter events, 14.8 us)
Async XLA Ops:
  2.1 13.2 %collective-permute-start = (bf16[32,1296]{1,0:T(8,128)(2,1)S(1)}, bf16[32,1296]{1,0:T(8,128)(2,1)S(1)}, u32[]{:S(2)}, u32[]{:S(2)}) collective-permute-start(bf16[32,1296]{1,0:T(8,128)(2,1)S(1)} %get-tuple-element.36), channel_id=1, source_target_pairs={{0,1},{1,0},{2,3},{3,2},{4,5},{5,4},{6,7},{7,6},{8,13},{9,12},{10,... | collective-permute-start | bytes 248840 | tf_op jit(solution)/shard_map/ppermute | solution.py:513
  6.2 9.1 %collective-permute-start.1 = (bf16[32,1296]{1,0:T(8,128)(2,1)S(1)}, bf16[32,1296]{1,0:T(8,128)(2,1)S(1)}, u32[]{:S(2)}, u32[]{:S(2)}) collective-permute-start(bf16[32,1296]{1,0:T(8,128)(2,1)S(1)} %get-tuple-element.37), channel_id=1, source_target_pairs={{0,2},{1,3},{2,0},{3,1},{4,6},{5,7},{6,4},{7,5},{8,14},{9,15},{10,... | collective-permute-start | bytes 248840 | tf_op jit(solution)/shard_map/ppermute | solution.py:513
  7.3 8.0 %collective-permute-start.2 = (bf16[32,1296]{1,0:T(8,128)(2,1)S(1)}, bf16[32,1296]{1,0:T(8,128)(2,1)S(1)}, u32[]{:S(2)}, u32[]{:S(2)}) collective-permute-start(bf16[32,1296]{1,0:T(8,128)(2,1)S(1)} %get-tuple-element.38), channel_id=1, source_target_pairs={{0,3},{1,2},{2,1},{3,0},{4,7},{5,6},{6,5},{7,4},{8,15},{9,14},{10,... | collective-permute-start | bytes 248840 | tf_op jit(solution)/shard_map/ppermute | solution.py:513
  9.5 6.4 %collective-permute-start.3 = (bf16[32,1296]{1,0:T(8,128)(2,1)S(1)}, bf16[32,1296]{1,0:T(8,128)(2,1)S(1)}, u32[]{:S(2)}, u32[]{:S(2)}) collective-permute-start(bf16[32,1296]{1,0:T(8,128)(2,1)S(1)} %get-tuple-element.39), channel_id=1, source_target_pairs={{0,0},{1,1},{2,2},{3,3},{4,4},{5,5},{6,6},{7,7},{8,12},{9,13},{10,... | collective-permute-start | bytes 248840 | tf_op jit(solution)/shard_map/ppermute | solution.py:513
  16.0 10.4 %collective-permute-start.4 = (bf16[4,32,1296]{2,1,0:T(8,128)(2,1)S(1)}, bf16[4,32,1296]{2,1,0:T(8,128)(2,1)S(1)}, u32[]{:S(2)}, u32[]{:S(2)}) collective-permute-start(bf16[4,32,1296]{2,1,0:T(8,128)(2,1)S(1)} %pack_blocks.2.refs_0_), channel_id=1, source_target_pairs={{0,16},{8,24},{16,0},{24,8},{1,17},{9,25},{17,1},{25,9},{2,18},{10... | collective-permute-start | bytes 995336 | tf_op jit(solution)/shard_map/ppermute | solution.py:491
  26.4 2.5 %collective-permute-start.9 = (bf16[4,32,1296]{2,1,0:T(8,128)(2,1)S(1)}, bf16[4,32,1296]{2,1,0:T(8,128)(2,1)S(1)}, u32[]{:S(2)}, u32[]{:S(2)}) collective-permute-start(bf16[4,32,1296]{2,1,0:T(8,128)(2,1)S(1)} %collective-permute-done.4.refs_0_), channel_id=1, source_target_pairs={{0,8},{8,0},{16,24},{24,16},{1,9},{9,1},{17,25},{25,17},{2,10},{10... | collective-permute-start | bytes 995336 | tf_op jit(solution)/shard_map/ppermute | solution.py:491
  26.8 9.9 %collective-permute-start.19 = (s16[64,2688]{1,0:T(8,128)(2,1)}, s16[64,2688]{1,0:T(8,128)(2,1)S(1)}, u32[]{:S(2)}, u32[]{:S(2)}) collective-permute-start(s16[64,2688]{1,0:T(8,128)(2,1)} %get-tuple-element.54), channel_id=1, source_target_pairs={{0,2},{1,3},{2,0},{3,1},{4,6},{5,7},{6,4},{7,5},{8,10},{9,11},{10,... | collective-permute-start | bytes 1032200 | tf_op jit(solution)/shard_map/ppermute | solution.py:491
  27.6 10.7 %collective-permute-start.21 = (s16[64,2688]{1,0:T(8,128)(2,1)}, s16[64,2688]{1,0:T(8,128)(2,1)S(1)}, u32[]{:S(2)}, u32[]{:S(2)}) collective-permute-start(s16[64,2688]{1,0:T(8,128)(2,1)} %get-tuple-element.59), channel_id=1, source_target_pairs={{0,1},{1,0},{2,3},{3,2},{4,5},{5,4},{6,7},{7,6},{8,9},{9,8},{10,11... | collective-permute-start | bytes 1032200 | tf_op jit(solution)/shard_map/ppermute | solution.py:491
  35.3 8.9 %collective-permute-start.10 = (s16[64,2688]{1,0:T(8,128)(2,1)S(1)}, s16[64,2688]{1,0:T(8,128)(2,1)S(1)}, u32[]{:S(2)}, u32[]{:S(2)}) collective-permute-start(s16[64,2688]{1,0:T(8,128)(2,1)S(1)} %get-tuple-element.43), channel_id=1, source_target_pairs={{0,1},{1,0},{2,3},{3,2},{4,5},{5,4},{6,7},{7,6},{8,9},{9,8},{10,11... | collective-permute-start | bytes 1032200 | tf_op jit(solution)/shard_map/ppermute | solution.py:491
  35.7 12.3 %collective-permute-start.12 = (s16[64,2688]{1,0:T(8,128)(2,1)S(1)}, s16[64,2688]{1,0:T(8,128)(2,1)S(1)}, u32[]{:S(2)}, u32[]{:S(2)}) collective-permute-start(s16[64,2688]{1,0:T(8,128)(2,1)S(1)} %get-tuple-element.48), channel_id=1, source_target_pairs={{0,2},{1,3},{2,0},{3,1},{4,6},{5,7},{6,4},{7,5},{8,10},{9,11},{10,... | collective-permute-start | bytes 1032200 | tf_op jit(solution)/shard_map/ppermute | solution.py:491
  37.2 12.6 %collective-permute-start.20 = (s16[32,2688]{1,0:T(8,128)(2,1)S(1)}, s16[32,2688]{1,0:T(8,128)(2,1)S(1)}, u32[]{:S(2)}, u32[]{:S(2)}) collective-permute-start(s16[32,2688]{1,0:T(8,128)(2,1)S(1)} %get-tuple-element.56), channel_id=1, source_target_pairs={{0,1},{1,0},{2,3},{3,2},{4,5},{5,4},{6,7},{7,6},{8,9},{9,8},{10,11... | collective-permute-start | bytes 516104 | tf_op jit(solution)/shard_map/ppermute | solution.py:491
  38.9 11.5 %collective-permute-start.22 = (s16[32,2688]{1,0:T(8,128)(2,1)S(1)}, s16[32,2688]{1,0:T(8,128)(2,1)S(1)}, u32[]{:S(2)}, u32[]{:S(2)}) collective-permute-start(s16[32,2688]{1,0:T(8,128)(2,1)S(1)} %get-tuple-element.61), channel_id=1, source_target_pairs={{0,4},{1,5},{2,6},{3,7},{4,0},{5,1},{6,2},{7,3},{8,12},{9,13},{10,... | collective-permute-start | bytes 516104 | tf_op jit(solution)/shard_map/ppermute | solution.py:491
  44.8 15.2 %collective-permute-start.11 = (s16[32,2688]{1,0:T(8,128)(2,1)S(1)}, s16[32,2688]{1,0:T(8,128)(2,1)S(1)}, u32[]{:S(2)}, u32[]{:S(2)}) collective-permute-start(s16[32,2688]{1,0:T(8,128)(2,1)S(1)} %get-tuple-element.45), channel_id=1, source_target_pairs={{0,4},{1,5},{2,6},{3,7},{4,0},{5,1},{6,2},{7,3},{8,12},{9,13},{10,... | collective-permute-start | bytes 516104 | tf_op jit(solution)/shard_map/ppermute | solution.py:491
  48.6 11.7 %collective-permute-start.13 = (s16[32,2688]{1,0:T(8,128)(2,1)S(1)}, s16[32,2688]{1,0:T(8,128)(2,1)S(1)}, u32[]{:S(2)}, u32[]{:S(2)}) collective-permute-start(s16[32,2688]{1,0:T(8,128)(2,1)S(1)} %get-tuple-element.50), channel_id=1, source_target_pairs={{0,1},{1,0},{2,3},{3,2},{4,5},{5,4},{6,7},{7,6},{8,9},{9,8},{10,11... | collective-permute-start | bytes 516104 | tf_op jit(solution)/shard_map/ppermute | solution.py:491
  50.0 12.2 %collective-permute-start.23 = (s16[16,2688]{1,0:T(8,128)(2,1)S(1)}, s16[16,2688]{1,0:T(8,128)(2,1)S(1)}, u32[]{:S(2)}, u32[]{:S(2)}) collective-permute-start(s16[16,2688]{1,0:T(8,128)(2,1)S(1)} %get-tuple-element.63), channel_id=1, source_target_pairs={{0,4},{1,5},{2,6},{3,7},{4,0},{5,1},{6,2},{7,3},{8,12},{9,13},{10,... | collective-permute-start | bytes 258056 | tf_op jit(solution)/shard_map/ppermute | solution.py:491
  50.5 11.7 %collective-permute-start.24 = (s16[16,2688]{1,0:T(8,128)(2,1)S(1)}, s16[16,2688]{1,0:T(8,128)(2,1)S(1)}, u32[]{:S(2)}, u32[]{:S(2)}) collective-permute-start(s16[16,2688]{1,0:T(8,128)(2,1)S(1)} %get-tuple-element.64), channel_id=1, source_target_pairs={{0,2},{1,3},{2,0},{3,1},{4,6},{5,7},{6,4},{7,5},{8,10},{9,11},{10,... | collective-permute-start | bytes 258056 | tf_op jit(solution)/shard_map/ppermute | solution.py:491
  60.3 3.4 %collective-permute-start.14 = (s16[16,2688]{1,0:T(8,128)(2,1)S(1)}, s16[16,2688]{1,0:T(8,128)(2,1)S(1)}, u32[]{:S(2)}, u32[]{:S(2)}) collective-permute-start(s16[16,2688]{1,0:T(8,128)(2,1)S(1)} %get-tuple-element.52), channel_id=1, source_target_pairs={{0,2},{1,3},{2,0},{3,1},{4,6},{5,7},{6,4},{7,5},{8,10},{9,11},{10,... | collective-permute-start | bytes 258056 | tf_op jit(solution)/shard_map/ppermute | solution.py:491
  60.6 4.4 %collective-permute-start.15 = (s16[16,2688]{1,0:T(8,128)(2,1)S(1)}, s16[16,2688]{1,0:T(8,128)(2,1)S(1)}, u32[]{:S(2)}, u32[]{:S(2)}) collective-permute-start(s16[16,2688]{1,0:T(8,128)(2,1)S(1)} %get-tuple-element.53), channel_id=1, source_target_pairs={{0,4},{1,5},{2,6},{3,7},{4,0},{5,1},{6,2},{7,3},{8,12},{9,13},{10,... | collective-permute-start | bytes 258056 | tf_op jit(solution)/shard_map/ppermute | solution.py:491
  63.1 6.9 %collective-permute-start.26 = (s16[32,2688]{1,0:T(8,128)(2,1)S(1)}, s16[32,2688]{1,0:T(8,128)(2,1)S(1)}, u32[]{:S(2)}, u32[]{:S(2)}) collective-permute-start(s16[32,2688]{1,0:T(8,128)(2,1)S(1)} %update_amplitudes.3.refs_0_), channel_id=1, source_target_pairs={{0,16},{8,24},{16,0},{24,8},{1,17},{9,25},{17,1},{25,9},{2,18},{10... | collective-permute-start | bytes 516104 | tf_op jit(solution)/shard_map/ppermute | solution.py:491
  65.8 5.3 %collective-permute-start.17 = (s16[32,2688]{1,0:T(8,128)(2,1)S(1)}, s16[32,2688]{1,0:T(8,128)(2,1)S(1)}, u32[]{:S(2)}, u32[]{:S(2)}) collective-permute-start(s16[32,2688]{1,0:T(8,128)(2,1)S(1)} %update_amplitudes.2.refs_0_), channel_id=1, source_target_pairs={{0,16},{8,24},{16,0},{24,8},{1,17},{9,25},{17,1},{25,9},{2,18},{10... | collective-permute-start | bytes 516104 | tf_op jit(solution)/shard_map/ppermute | solution.py:491
  66.1 8.8 %collective-permute-start.25 = (s16[32,2688]{1,0:T(8,128)(2,1)S(1)}, s16[32,2688]{1,0:T(8,128)(2,1)S(1)}, u32[]{:S(2)}, u32[]{:S(2)}) collective-permute-start(s16[32,2688]{1,0:T(8,128)(2,1)S(1)} %update_amplitudes.3.refs_0_), channel_id=1, source_target_pairs={{0,8},{8,0},{16,24},{24,16},{1,9},{9,1},{17,25},{25,17},{2,10},{10... | collective-permute-start | bytes 516104 | tf_op jit(solution)/shard_map/ppermute | solution.py:491
  70.0 4.9 %collective-permute-start.27 = (s16[32,2688]{1,0:T(8,128)(2,1)S(1)}, s16[32,2688]{1,0:T(8,128)(2,1)S(1)}, u32[]{:S(2)}, u32[]{:S(2)}) collective-permute-start(s16[32,2688]{1,0:T(8,128)(2,1)S(1)} %collective-permute-done.26.refs_2_), channel_id=1, source_target_pairs={{0,8},{8,0},{16,24},{24,16},{1,9},{9,1},{17,25},{25,17},{2,10},{10... | collective-permute-start | bytes 516104 | tf_op jit(solution)/shard_map/ppermute | solution.py:491
  70.9 6.1 %collective-permute-start.16 = (s16[32,2688]{1,0:T(8,128)(2,1)S(1)}, s16[32,2688]{1,0:T(8,128)(2,1)S(1)}, u32[]{:S(2)}, u32[]{:S(2)}) collective-permute-start(s16[32,2688]{1,0:T(8,128)(2,1)S(1)} %update_amplitudes.2.refs_0_), channel_id=1, source_target_pairs={{0,8},{8,0},{16,24},{24,16},{1,9},{9,1},{17,25},{25,17},{2,10},{10... | collective-permute-start | bytes 516104 | tf_op jit(solution)/shard_map/ppermute | solution.py:491
  71.1 5.9 %collective-permute-start.18 = (s16[32,2688]{1,0:T(8,128)(2,1)S(1)}, s16[32,2688]{1,0:T(8,128)(2,1)S(1)}, u32[]{:S(2)}, u32[]{:S(2)}) collective-permute-start(s16[32,2688]{1,0:T(8,128)(2,1)S(1)} %collective-permute-done.17.refs_2_), channel_id=1, source_target_pairs={{0,8},{8,0},{16,24},{24,16},{1,9},{9,1},{17,25},{25,17},{2,10},{10... | collective-permute-start | bytes 516104 | tf_op jit(solution)/shard_map/ppermute | solution.py:491
  (8 other events, 62.2 us)

commit v3 on v2

--- a/solution.py
+++ b/solution.py
@@ -407,16 +407,20 @@
     width = coded[0].shape[1]
     tile = width // segments
     for rel, ref in enumerate(coded):
-        group = where[0] ^ rel
-        for j in range(2):
-            at = pl.ds(j * part, part)
-            codes = codes_of(ref, at, cols, segments)
-            pieces = [
-                decode(ref[at, n * tile : (n + 1) * tile], codes, n, cols, n * tile)
-                for n in range(segments)
-            ]
-            x = pltpu.roll(jnp.concatenate(pieces, axis=1), (group * cols) % LANES, 1)
-            slots[group, j * part : (j + 1) * part, :] = x
+        for group in range(4):
+
+            @pl.when(where[0] ^ rel == group)
+            def _():
+                shift = group * cols % LANES
+                for j in range(2):
+                    at = slice(j * part, (j + 1) * part)
+                    codes = codes_of(ref, at, cols, segments)
+                    pieces = [
+                        decode(ref[at, n * tile : (n + 1) * tile], codes, n, cols, n * tile)
+                        for n in range(segments)
+                    ]
+                    x = jnp.concatenate(pieces, axis=1)
+                    slots[group, at, :] = pltpu.roll(x, shift, 1) if shift else x
     lane = lax.broadcasted_iota(jnp.int32, (high, LANES), 1)
     stores = []
     for chip in range(2):
@@ -518,7 +522,7 @@
     bits = [1 << n for n in range(pairs.bit_length() - 1)]
     x_first, z_first = bits, bits[1::-1] + bits[2:]
     x_then_far = bits[:1] + bits[2:] + bits[1:2]
-    routes = ((z_first, x_then_far), (x_then_far, z_first))
+    routes = ((z_first, x_then_far), (z_first, x_first))
 
     def listed(value, left):
         if not left:
@@ -552,7 +556,7 @@
             inner = 3 - len(keeps)
             if n == len(bits) - 1:
                 state[half] = (keeps, got)
-            elif inner == 2 or one[n + 1 :] == two[n + 1 :]:
+            elif inner == 2:
                 state[half] = [add(keeps, got, inner, cols)]
             else:
                 state[half] = [add([k], [g], 1, cols) for k, g in zip(keeps, got)]

time: 79.5 us -> 76.9 us (0.967)
  starting transfers between devices: 34.9 us -> 27.7 us
  waiting for transfers between devices: 15 us -> 19.7 us
    ppermute x24, starting transfers between devices: 25.7 us -> 18.5 us  [swap(): return lax.ppermute(x, axis, [(i, i ^ flip) for i in range(size)])]
    ppermute x24, waiting for transfers between devices: 14.4 us -> 19.1 us  [swap(): return lax.ppermute(x, axis, [(i, i ^ flip) for i in range(size)])]
  transfers between devices with their start and end apart: 28 -> 28, of which waited for: 11 -> 11; matrix products, arithmetic and copies ran while one was open for 5% -> 5% of each run, Pallas kernels for 26% -> 27%
where the time goes in v3:
time: 76.9 us; the launch traced here: 76.5 us
  starting transfers between devices  27.7 us (36%)
  Pallas kernels  24.5 us (32%)
  waiting for transfers between devices  19.7 us (26%)
  other arithmetic  2.95 us (4%)
  local copies, waits for them, and re-layouts  1.36 us (2%)
    ppermute x24, waiting for transfers between devices, swap(): return lax.ppermute(x, axis, [(i, i ^ flip) for i in range(size)])  19.1 us
    ppermute x24, starting transfers between devices, swap(): return lax.ppermute(x, axis, [(i, i ^ flip) for i in range(size)])  18.5 us
    pallas_call x2, Pallas kernels, product(): pl.pallas_call(functools.partial(product_kernel, order, parts, cols, segm...  13.5 us
    ppermute x4, starting transfers between devices, shards(): blocks[j] = lax.ppermute(blocks[j], ('grp', 'pair'), moves)  9.25 us
    pallas_call x2, Pallas kernels, place_half(): pl.pallas_call(functools.partial(half_kernel, cols, segments, late), grid...  4.03 us
    pallas_call x8, Pallas kernels, add(): pl.pallas_call(functools.partial(add_kernel, cols, layout(cols)[1], len(k...  3.17 us
    reduce_sum x2, other arithmetic, lookup(): return jnp.sum(picked, axis=-1)  2.54 us
    pallas_call x1, Pallas kernels, cut(): pl.pallas_call(cut_kernel, grid_spec=pltpu.PrefetchScalarGridSpec(num_sca...  2.04 us
  transfers between devices with their start and end apart: 28, of which 11 were waited for; matrix products, arithmetic and copies ran while one was open for 5% of the time, Pallas kernels for 27%

profile of v3, /device:TPU:1, one launch (start us, length us, event | category | flops | bytes accessed | tf_op | source)
XLA Modules:
  0.0 76.5 jit_solution(5981065525478110520)
XLA Ops:
  0.1 2.0 %cut_blocks.1 = (bf16[32,1296]{1,0:T(8,128)(2,1)S(1)}, bf16[32,1296]{1,0:T(8,128)(2,1)S(1)}, bf16[32,1296]{1,0:T(8,128)(2,1)S(1)}, bf16[32,1296]{1,0:T(8,128)(2,1)S(1)}) custom-call(s32[3]{0:T(128)S(1)} %pad_add_fusion.3.where, bf16[64,10368]{1,0:T(8,128)(2,1)} %a_ref.1), custom_call_target="tpu_custom_call" | custom-call | flops 1024 | bytes 1024 | tf_op jit(solution)/shard_map/cut_blocks/pallas_call | solution.py:90
  2.1 4.1 %collective-permute-start = (bf16[32,1296]{1,0:T(8,128)(2,1)S(1)}, bf16[32,1296]{1,0:T(8,128)(2,1)S(1)}, u32[]{:S(2)}, u32[]{:S(2)}) collective-permute-start(bf16[32,1296]{1,0:T(8,128)(2,1)S(1)} %get-tuple-element.36), channel_id=1, source_target_pairs={{0,1},{1,0},{2,3},{3,2},{4,5},{5,4},{6,7},{7,6},{8,13},{9,12},{10,... | collective-permute-start | bytes 248840 | tf_op jit(solution)/shard_map/ppermute | solution.py:517
  6.2 1.1 %collective-permute-start.1 = (bf16[32,1296]{1,0:T(8,128)(2,1)S(1)}, bf16[32,1296]{1,0:T(8,128)(2,1)S(1)}, u32[]{:S(2)}, u32[]{:S(2)}) collective-permute-start(bf16[32,1296]{1,0:T(8,128)(2,1)S(1)} %get-tuple-element.37), channel_id=1, source_target_pairs={{0,2},{1,3},{2,0},{3,1},{4,6},{5,7},{6,4},{7,5},{8,14},{9,15},{10,... | collective-permute-start | bytes 248840 | tf_op jit(solution)/shard_map/ppermute | solution.py:517
  7.3 2.1 %collective-permute-start.2 = (bf16[32,1296]{1,0:T(8,128)(2,1)S(1)}, bf16[32,1296]{1,0:T(8,128)(2,1)S(1)}, u32[]{:S(2)}, u32[]{:S(2)}) collective-permute-start(bf16[32,1296]{1,0:T(8,128)(2,1)S(1)} %get-tuple-element.38), channel_id=1, source_target_pairs={{0,3},{1,2},{2,1},{3,0},{4,7},{5,6},{6,5},{7,4},{8,15},{9,14},{10,... | collective-permute-start | bytes 248840 | tf_op jit(solution)/shard_map/ppermute | solution.py:517
  9.5 1.9 %collective-permute-start.3 = (bf16[32,1296]{1,0:T(8,128)(2,1)S(1)}, bf16[32,1296]{1,0:T(8,128)(2,1)S(1)}, u32[]{:S(2)}, u32[]{:S(2)}) collective-permute-start(bf16[32,1296]{1,0:T(8,128)(2,1)S(1)} %get-tuple-element.39), channel_id=1, source_target_pairs={{0,0},{1,1},{2,2},{3,3},{4,4},{5,5},{6,6},{7,7},{8,12},{9,13},{10,... | collective-permute-start | bytes 248840 | tf_op jit(solution)/shard_map/ppermute | solution.py:517
  12.3 1.7 %select_reduce_fusion = f32[2,2592]{1,0:T(2,128)S(1)} fusion(f32[288]{0:T(512)} %param.13, s32[2,2592]{1,0:T(2,128)} %param.15), kind=kLoop, calls=%fused_computation | loop fusion | flops 4473792 | bytes 42624 | tf_op jit(solution)/shard_map/reduce_sum | solution.py:22
  14.0 1.2 %constant_dynamic-slice_fusion.1.refs_4_ = bf16[64,2592]{1,0:T(8,128)(2,1)S(1)} fusion(bf16[64,10368]{1,0:T(8,128)(2,1)} %a_ref.1, s32[]{:T(128)S(6)} %select_n.32), kind=kLoop, calls=%fused_computation.13 | loop fusion | bytes 663556 | tf_op jit(solution)/shard_map/dynamic_slice | solution.py:497
  16.0 1.3 %collective-permute-start.4 = (bf16[4,32,1296]{2,1,0:T(8,128)(2,1)S(1)}, bf16[4,32,1296]{2,1,0:T(8,128)(2,1)S(1)}, u32[]{:S(2)}, u32[]{:S(2)}) collective-permute-start(bf16[4,32,1296]{2,1,0:T(8,128)(2,1)S(1)} %pack_blocks.2.refs_0_), channel_id=1, source_target_pairs={{0,16},{8,24},{16,0},{24,8},{1,17},{9,25},{17,1},{25,9},{2,18},{10... | collective-permute-start | bytes 995336 | tf_op jit(solution)/shard_map/ppermute | solution.py:495
  19.3 7.0 %partial_products.2 = (s16[64,2688]{1,0:T(8,128)(2,1)}, s16[64,2688]{1,0:T(8,128)(2,1)}, f32[64,2688]{1,0:T(8,128)S(1)}, f32[64,2688]{1,0:T(8,128)S(1)}) custom-call(s32[4]{0:T(128)S(1)} %pad_add_fusion.4.where, bf16[4,32,1296]{2,1,0:T(8,128)(2,1)S(1)} %pack_blocks.2.refs_0_, bf16[4,32,1296]{2,1,0:T(8,128)(2,1)S(1)} %pack_blocks.3.refs_1_, ...), custom_call_target="tpu_custom_call" | custom-call | flops 1024 | bytes 1024 | tf_op jit(solution)/shard_map/partial_products/pallas_call | solution.py:198
  27.6 1.2 %collective-permute-start.21 = (s16[64,2688]{1,0:T(8,128)(2,1)}, s16[64,2688]{1,0:T(8,128)(2,1)S(1)}, u32[]{:S(2)}, u32[]{:S(2)}) collective-permute-start(s16[64,2688]{1,0:T(8,128)(2,1)} %get-tuple-element.59), channel_id=1, source_target_pairs={{0,1},{1,0},{2,3},{3,2},{4,5},{5,4},{6,7},{7,6},{8,9},{9,8},{10,11... | collective-permute-start | bytes 1032200 | tf_op jit(solution)/shard_map/ppermute | solution.py:495
  28.9 6.4 %partial_products.3 = (s16[64,2688]{1,0:T(8,128)(2,1)S(1)}, s16[64,2688]{1,0:T(8,128)(2,1)S(1)}, f32[64,2688]{1,0:T(8,128)S(1)}, f32[64,2688]{1,0:T(8,128)S(1)}) custom-call(s32[4]{0:T(128)S(1)} %pad_add_fusion.1.where, bf16[4,32,1296]{2,1,0:T(8,128)(2,1)S(1)} %collective-permute-done.4.refs_0_, bf16[4,32,1296]{2,1,0:T(8,128)(2,1)S(1)} %collective-permute-done.9.refs_1_, ...), custom_call_target="tpu_custom_call" | custom-call | flops 1024 | bytes 1024 | tf_op jit(solution)/shard_map/partial_products/pallas_call | solution.py:198
  37.2 1.1 %collective-permute-start.20 = (s16[32,2688]{1,0:T(8,128)(2,1)S(1)}, s16[32,2688]{1,0:T(8,128)(2,1)S(1)}, u32[]{:S(2)}, u32[]{:S(2)}) collective-permute-start(s16[32,2688]{1,0:T(8,128)(2,1)S(1)} %get-tuple-element.56), channel_id=1, source_target_pairs={{0,1},{1,0},{2,3},{3,2},{4,5},{5,4},{6,7},{7,6},{8,9},{9,8},{10,11... | collective-permute-start | bytes 516104 | tf_op jit(solution)/shard_map/ppermute | solution.py:495
  38.9 1.9 %collective-permute-start.22 = (s16[32,2688]{1,0:T(8,128)(2,1)S(1)}, s16[32,2688]{1,0:T(8,128)(2,1)S(1)}, u32[]{:S(2)}, u32[]{:S(2)}) collective-permute-start(s16[32,2688]{1,0:T(8,128)(2,1)S(1)} %get-tuple-element.61), channel_id=1, source_target_pairs={{0,4},{1,5},{2,6},{3,7},{4,0},{5,1},{6,2},{7,3},{8,12},{9,13},{10,... | collective-permute-start | bytes 516104 | tf_op jit(solution)/shard_map/ppermute | solution.py:495
  40.8 7.1 %collective-permute-done.10.refs_1_ = s16[64,2688]{1,0:T(8,128)(2,1)S(1)} collective-permute-done((s16[64,2688]{1,0:T(8,128)(2,1)S(1)}, s16[64,2688]{1,0:T(8,128)(2,1)S(1)}, u32[]{:S(2)}, u32[]{:S(2)}) %collective-permute-start.10) | collective-permute-done | bytes 344096 | tf_op jit(solution)/shard_map/ppermute | solution.py:495
  50.0 2.0 %collective-permute-start.23 = (s16[16,2688]{1,0:T(8,128)(2,1)S(1)}, s16[16,2688]{1,0:T(8,128)(2,1)S(1)}, u32[]{:S(2)}, u32[]{:S(2)}) collective-permute-start(s16[16,2688]{1,0:T(8,128)(2,1)S(1)} %get-tuple-element.63), channel_id=1, source_target_pairs={{0,4},{1,5},{2,6},{3,7},{4,0},{5,1},{6,2},{7,3},{8,12},{9,13},{10,... | collective-permute-start | bytes 258056 | tf_op jit(solution)/shard_map/ppermute | solution.py:495
  53.1 1.4 %collective-permute-start.14 = (s16[16,2688]{1,0:T(8,128)(2,1)S(1)}, s16[16,2688]{1,0:T(8,128)(2,1)S(1)}, u32[]{:S(2)}, u32[]{:S(2)}) collective-permute-start(s16[16,2688]{1,0:T(8,128)(2,1)S(1)} %get-tuple-element.52), channel_id=1, source_target_pairs={{0,4},{1,5},{2,6},{3,7},{4,0},{5,1},{6,2},{7,3},{8,12},{9,13},{10,... | collective-permute-start | bytes 258056 | tf_op jit(solution)/shard_map/ppermute | solution.py:495
  54.4 1.1 %collective-permute-done.13.refs_1_ = s16[32,2688]{1,0:T(8,128)(2,1)S(1)} collective-permute-done((s16[32,2688]{1,0:T(8,128)(2,1)S(1)}, s16[32,2688]{1,0:T(8,128)(2,1)S(1)}, u32[]{:S(2)}, u32[]{:S(2)}) %collective-permute-start.13) | collective-permute-done | bytes 172064 | tf_op jit(solution)/shard_map/ppermute | solution.py:495
  55.9 3.3 %collective-permute-done.24.refs_3_ = s16[16,2688]{1,0:T(8,128)(2,1)S(1)} collective-permute-done((s16[16,2688]{1,0:T(8,128)(2,1)S(1)}, s16[16,2688]{1,0:T(8,128)(2,1)S(1)}, u32[]{:S(2)}, u32[]{:S(2)}) %collective-permute-start.24) | collective-permute-done | bytes 86048 | tf_op jit(solution)/shard_map/ppermute | solution.py:495
  60.4 4.4 %collective-permute-done.15.refs_3_ = s16[16,2688]{1,0:T(8,128)(2,1)S(1)} collective-permute-done((s16[16,2688]{1,0:T(8,128)(2,1)S(1)}, s16[16,2688]{1,0:T(8,128)(2,1)S(1)}, u32[]{:S(2)}, u32[]{:S(2)}) %collective-permute-start.15) | collective-permute-done | bytes 86048 | tf_op jit(solution)/shard_map/ppermute | solution.py:495
  65.7 2.0 %collective-permute-start.25 = (s16[32,2688]{1,0:T(8,128)(2,1)S(1)}, s16[32,2688]{1,0:T(8,128)(2,1)S(1)}, u32[]{:S(2)}, u32[]{:S(2)}) collective-permute-start(s16[32,2688]{1,0:T(8,128)(2,1)S(1)} %update_amplitudes.3.refs_0_), channel_id=1, source_target_pairs={{0,8},{8,0},{16,24},{24,16},{1,9},{9,1},{17,25},{25,17},{2,10},{10... | collective-permute-start | bytes 516104 | tf_op jit(solution)/shard_map/ppermute | solution.py:495
  68.2 1.8 %collective-permute-done.17.refs_2_ = s16[32,2688]{1,0:T(8,128)(2,1)S(1)} collective-permute-done((s16[32,2688]{1,0:T(8,128)(2,1)S(1)}, s16[32,2688]{1,0:T(8,128)(2,1)S(1)}, u32[]{:S(2)}, u32[]{:S(2)}) %collective-permute-start.17) | collective-permute-done | bytes 172064 | tf_op jit(solution)/shard_map/ppermute | solution.py:495
  69.9 2.5 %collective-permute-start.18 = (s16[32,2688]{1,0:T(8,128)(2,1)S(1)}, s16[32,2688]{1,0:T(8,128)(2,1)S(1)}, u32[]{:S(2)}, u32[]{:S(2)}) collective-permute-start(s16[32,2688]{1,0:T(8,128)(2,1)S(1)} %collective-permute-done.17.refs_2_), channel_id=1, source_target_pairs={{0,8},{8,0},{16,24},{24,16},{1,9},{9,1},{17,25},{25,17},{2,10},{10... | collective-permute-start | bytes 516104 | tf_op jit(solution)/shard_map/ppermute | solution.py:495
  72.5 2.0 %place_early_half.1 = (f32[64,10368]{1,0:T(8,128)}, f32[64,128]{1,0:T(8,128)S(1)}) custom-call(s32[1]{0:T(128)} %bitcast.where, s16[32,2688]{1,0:T(8,128)(2,1)S(1)} %update_amplitudes.3.refs_0_, s16[32,2688]{1,0:T(8,128)(2,1)S(1)} %collective-permute-done.25.refs_1_, s16[32,2688]{1,0:T(8,128)(2,1)S(1)} %collective-permute-done.26.refs_2_, ...), custom_call_target="tpu_custom_call" | custom-call | tf_op jit(solution)/shard_map/place_early_half/pallas_call | solution.py:465
  74.5 2.0 %place_late_half.1 = f32[64,10368]{1,0:T(8,128)} custom-call(s32[1]{0:T(128)} %bitcast.where, s16[32,2688]{1,0:T(8,128)(2,1)S(1)} %update_amplitudes.2.refs_0_, s16[32,2688]{1,0:T(8,128)(2,1)S(1)} %collective-permute-done.16.refs_1_, s16[32,2688]{1,0:T(8,128)(2,1)S(1)} %collective-permute-done.17.refs_2_, ...), custom_call_target="tpu_custom_call", output_to_operand_aliasing={{}: (6, {})} | custom-call | tf_op jit(solution)/shard_map/place_late_half/pallas_call | solution.py:465
  (70 shorter events, 13.5 us)
Async XLA Ops:
  2.1 13.2 %collective-permute-start = (bf16[32,1296]{1,0:T(8,128)(2,1)S(1)}, bf16[32,1296]{1,0:T(8,128)(2,1)S(1)}, u32[]{:S(2)}, u32[]{:S(2)}) collective-permute-start(bf16[32,1296]{1,0:T(8,128)(2,1)S(1)} %get-tuple-element.36), channel_id=1, source_target_pairs={{0,1},{1,0},{2,3},{3,2},{4,5},{5,4},{6,7},{7,6},{8,13},{9,12},{10,... | collective-permute-start | bytes 248840 | tf_op jit(solution)/shard_map/ppermute | solution.py:517
  6.2 9.1 %collective-permute-start.1 = (bf16[32,1296]{1,0:T(8,128)(2,1)S(1)}, bf16[32,1296]{1,0:T(8,128)(2,1)S(1)}, u32[]{:S(2)}, u32[]{:S(2)}) collective-permute-start(bf16[32,1296]{1,0:T(8,128)(2,1)S(1)} %get-tuple-element.37), channel_id=1, source_target_pairs={{0,2},{1,3},{2,0},{3,1},{4,6},{5,7},{6,4},{7,5},{8,14},{9,15},{10,... | collective-permute-start | bytes 248840 | tf_op jit(solution)/shard_map/ppermute | solution.py:517
  7.3 8.0 %collective-permute-start.2 = (bf16[32,1296]{1,0:T(8,128)(2,1)S(1)}, bf16[32,1296]{1,0:T(8,128)(2,1)S(1)}, u32[]{:S(2)}, u32[]{:S(2)}) collective-permute-start(bf16[32,1296]{1,0:T(8,128)(2,1)S(1)} %get-tuple-element.38), channel_id=1, source_target_pairs={{0,3},{1,2},{2,1},{3,0},{4,7},{5,6},{6,5},{7,4},{8,15},{9,14},{10,... | collective-permute-start | bytes 248840 | tf_op jit(solution)/shard_map/ppermute | solution.py:517
  9.5 6.4 %collective-permute-start.3 = (bf16[32,1296]{1,0:T(8,128)(2,1)S(1)}, bf16[32,1296]{1,0:T(8,128)(2,1)S(1)}, u32[]{:S(2)}, u32[]{:S(2)}) collective-permute-start(bf16[32,1296]{1,0:T(8,128)(2,1)S(1)} %get-tuple-element.39), channel_id=1, source_target_pairs={{0,0},{1,1},{2,2},{3,3},{4,4},{5,5},{6,6},{7,7},{8,12},{9,13},{10,... | collective-permute-start | bytes 248840 | tf_op jit(solution)/shard_map/ppermute | solution.py:517
  16.0 10.4 %collective-permute-start.4 = (bf16[4,32,1296]{2,1,0:T(8,128)(2,1)S(1)}, bf16[4,32,1296]{2,1,0:T(8,128)(2,1)S(1)}, u32[]{:S(2)}, u32[]{:S(2)}) collective-permute-start(bf16[4,32,1296]{2,1,0:T(8,128)(2,1)S(1)} %pack_blocks.2.refs_0_), channel_id=1, source_target_pairs={{0,16},{8,24},{16,0},{24,8},{1,17},{9,25},{17,1},{25,9},{2,18},{10... | collective-permute-start | bytes 995336 | tf_op jit(solution)/shard_map/ppermute | solution.py:495
  26.4 2.5 %collective-permute-start.9 = (bf16[4,32,1296]{2,1,0:T(8,128)(2,1)S(1)}, bf16[4,32,1296]{2,1,0:T(8,128)(2,1)S(1)}, u32[]{:S(2)}, u32[]{:S(2)}) collective-permute-start(bf16[4,32,1296]{2,1,0:T(8,128)(2,1)S(1)} %collective-permute-done.4.refs_0_), channel_id=1, source_target_pairs={{0,8},{8,0},{16,24},{24,16},{1,9},{9,1},{17,25},{25,17},{2,10},{10... | collective-permute-start | bytes 995336 | tf_op jit(solution)/shard_map/ppermute | solution.py:495
  26.8 9.9 %collective-permute-start.19 = (s16[64,2688]{1,0:T(8,128)(2,1)}, s16[64,2688]{1,0:T(8,128)(2,1)S(1)}, u32[]{:S(2)}, u32[]{:S(2)}) collective-permute-start(s16[64,2688]{1,0:T(8,128)(2,1)} %get-tuple-element.54), channel_id=1, source_target_pairs={{0,2},{1,3},{2,0},{3,1},{4,6},{5,7},{6,4},{7,5},{8,10},{9,11},{10,... | collective-permute-start | bytes 1032200 | tf_op jit(solution)/shard_map/ppermute | solution.py:495
  27.6 10.7 %collective-permute-start.21 = (s16[64,2688]{1,0:T(8,128)(2,1)}, s16[64,2688]{1,0:T(8,128)(2,1)S(1)}, u32[]{:S(2)}, u32[]{:S(2)}) collective-permute-start(s16[64,2688]{1,0:T(8,128)(2,1)} %get-tuple-element.59), channel_id=1, source_target_pairs={{0,1},{1,0},{2,3},{3,2},{4,5},{5,4},{6,7},{7,6},{8,9},{9,8},{10,11... | collective-permute-start | bytes 1032200 | tf_op jit(solution)/shard_map/ppermute | solution.py:495
  35.3 12.6 %collective-permute-start.10 = (s16[64,2688]{1,0:T(8,128)(2,1)S(1)}, s16[64,2688]{1,0:T(8,128)(2,1)S(1)}, u32[]{:S(2)}, u32[]{:S(2)}) collective-permute-start(s16[64,2688]{1,0:T(8,128)(2,1)S(1)} %get-tuple-element.43), channel_id=1, source_target_pairs={{0,2},{1,3},{2,0},{3,1},{4,6},{5,7},{6,4},{7,5},{8,10},{9,11},{10,... | collective-permute-start | bytes 1032200 | tf_op jit(solution)/shard_map/ppermute | solution.py:495
  35.9 13.1 %collective-permute-start.12 = (s16[64,2688]{1,0:T(8,128)(2,1)S(1)}, s16[64,2688]{1,0:T(8,128)(2,1)S(1)}, u32[]{:S(2)}, u32[]{:S(2)}) collective-permute-start(s16[64,2688]{1,0:T(8,128)(2,1)S(1)} %get-tuple-element.48), channel_id=1, source_target_pairs={{0,1},{1,0},{2,3},{3,2},{4,5},{5,4},{6,7},{7,6},{8,9},{9,8},{10,11... | collective-permute-start | bytes 1032200 | tf_op jit(solution)/shard_map/ppermute | solution.py:495
  37.2 12.6 %collective-permute-start.20 = (s16[32,2688]{1,0:T(8,128)(2,1)S(1)}, s16[32,2688]{1,0:T(8,128)(2,1)S(1)}, u32[]{:S(2)}, u32[]{:S(2)}) collective-permute-start(s16[32,2688]{1,0:T(8,128)(2,1)S(1)} %get-tuple-element.56), channel_id=1, source_target_pairs={{0,1},{1,0},{2,3},{3,2},{4,5},{5,4},{6,7},{7,6},{8,9},{9,8},{10,11... | collective-permute-start | bytes 516104 | tf_op jit(solution)/shard_map/ppermute | solution.py:495
  38.9 13.1 %collective-permute-start.22 = (s16[32,2688]{1,0:T(8,128)(2,1)S(1)}, s16[32,2688]{1,0:T(8,128)(2,1)S(1)}, u32[]{:S(2)}, u32[]{:S(2)}) collective-permute-start(s16[32,2688]{1,0:T(8,128)(2,1)S(1)} %get-tuple-element.61), channel_id=1, source_target_pairs={{0,4},{1,5},{2,6},{3,7},{4,0},{5,1},{6,2},{7,3},{8,12},{9,13},{10,... | collective-permute-start | bytes 516104 | tf_op jit(solution)/shard_map/ppermute | solution.py:495
  48.5 4.3 %collective-permute-start.11 = (s16[32,2688]{1,0:T(8,128)(2,1)S(1)}, s16[32,2688]{1,0:T(8,128)(2,1)S(1)}, u32[]{:S(2)}, u32[]{:S(2)}) collective-permute-start(s16[32,2688]{1,0:T(8,128)(2,1)S(1)} %get-tuple-element.45), channel_id=1, source_target_pairs={{0,1},{1,0},{2,3},{3,2},{4,5},{5,4},{6,7},{7,6},{8,9},{9,8},{10,11... | collective-permute-start | bytes 516104 | tf_op jit(solution)/shard_map/ppermute | solution.py:495
  49.6 5.9 %collective-permute-start.13 = (s16[32,2688]{1,0:T(8,128)(2,1)S(1)}, s16[32,2688]{1,0:T(8,128)(2,1)S(1)}, u32[]{:S(2)}, u32[]{:S(2)}) collective-permute-start(s16[32,2688]{1,0:T(8,128)(2,1)S(1)} %get-tuple-element.50), channel_id=1, source_target_pairs={{0,2},{1,3},{2,0},{3,1},{4,6},{5,7},{6,4},{7,5},{8,10},{9,11},{10,... | collective-permute-start | bytes 516104 | tf_op jit(solution)/shard_map/ppermute | solution.py:495
  50.0 5.9 %collective-permute-start.23 = (s16[16,2688]{1,0:T(8,128)(2,1)S(1)}, s16[16,2688]{1,0:T(8,128)(2,1)S(1)}, u32[]{:S(2)}, u32[]{:S(2)}) collective-permute-start(s16[16,2688]{1,0:T(8,128)(2,1)S(1)} %get-tuple-element.63), channel_id=1, source_target_pairs={{0,4},{1,5},{2,6},{3,7},{4,0},{5,1},{6,2},{7,3},{8,12},{9,13},{10,... | collective-permute-start | bytes 258056 | tf_op jit(solution)/shard_map/ppermute | solution.py:495
  52.2 7.0 %collective-permute-start.24 = (s16[16,2688]{1,0:T(8,128)(2,1)S(1)}, s16[16,2688]{1,0:T(8,128)(2,1)S(1)}, u32[]{:S(2)}, u32[]{:S(2)}) collective-permute-start(s16[16,2688]{1,0:T(8,128)(2,1)S(1)} %get-tuple-element.64), channel_id=1, source_target_pairs={{0,2},{1,3},{2,0},{3,1},{4,6},{5,7},{6,4},{7,5},{8,10},{9,11},{10,... | collective-permute-start | bytes 258056 | tf_op jit(solution)/shard_map/ppermute | solution.py:495
  53.1 7.3 %collective-permute-start.14 = (s16[16,2688]{1,0:T(8,128)(2,1)S(1)}, s16[16,2688]{1,0:T(8,128)(2,1)S(1)}, u32[]{:S(2)}, u32[]{:S(2)}) collective-permute-start(s16[16,2688]{1,0:T(8,128)(2,1)S(1)} %get-tuple-element.52), channel_id=1, source_target_pairs={{0,4},{1,5},{2,6},{3,7},{4,0},{5,1},{6,2},{7,3},{8,12},{9,13},{10,... | collective-permute-start | bytes 258056 | tf_op jit(solution)/shard_map/ppermute | solution.py:495
  55.8 9.0 %collective-permute-start.15 = (s16[16,2688]{1,0:T(8,128)(2,1)S(1)}, s16[16,2688]{1,0:T(8,128)(2,1)S(1)}, u32[]{:S(2)}, u32[]{:S(2)}) collective-permute-start(s16[16,2688]{1,0:T(8,128)(2,1)S(1)} %get-tuple-element.53), channel_id=1, source_target_pairs={{0,4},{1,5},{2,6},{3,7},{4,0},{5,1},{6,2},{7,3},{8,12},{9,13},{10,... | collective-permute-start | bytes 258056 | tf_op jit(solution)/shard_map/ppermute | solution.py:495
  60.1 7.5 %collective-permute-start.26 = (s16[32,2688]{1,0:T(8,128)(2,1)S(1)}, s16[32,2688]{1,0:T(8,128)(2,1)S(1)}, u32[]{:S(2)}, u32[]{:S(2)}) collective-permute-start(s16[32,2688]{1,0:T(8,128)(2,1)S(1)} %update_amplitudes.3.refs_0_), channel_id=1, source_target_pairs={{0,16},{8,24},{16,0},{24,8},{1,17},{9,25},{17,1},{25,9},{2,18},{10... | collective-permute-start | bytes 516104 | tf_op jit(solution)/shard_map/ppermute | solution.py:495
  65.6 4.3 %collective-permute-start.17 = (s16[32,2688]{1,0:T(8,128)(2,1)S(1)}, s16[32,2688]{1,0:T(8,128)(2,1)S(1)}, u32[]{:S(2)}, u32[]{:S(2)}) collective-permute-start(s16[32,2688]{1,0:T(8,128)(2,1)S(1)} %update_amplitudes.2.refs_0_), channel_id=1, source_target_pairs={{0,16},{8,24},{16,0},{24,8},{1,17},{9,25},{17,1},{25,9},{2,18},{10... | collective-permute-start | bytes 516104 | tf_op jit(solution)/shard_map/ppermute | solution.py:495
  65.7 6.8 %collective-permute-start.25 = (s16[32,2688]{1,0:T(8,128)(2,1)S(1)}, s16[32,2688]{1,0:T(8,128)(2,1)S(1)}, u32[]{:S(2)}, u32[]{:S(2)}) collective-permute-start(s16[32,2688]{1,0:T(8,128)(2,1)S(1)} %update_amplitudes.3.refs_0_), channel_id=1, source_target_pairs={{0,8},{8,0},{16,24},{24,16},{1,9},{9,1},{17,25},{25,17},{2,10},{10... | collective-permute-start | bytes 516104 | tf_op jit(solution)/shard_map/ppermute | solution.py:495
  67.6 4.8 %collective-permute-start.27 = (s16[32,2688]{1,0:T(8,128)(2,1)S(1)}, s16[32,2688]{1,0:T(8,128)(2,1)S(1)}, u32[]{:S(2)}, u32[]{:S(2)}) collective-permute-start(s16[32,2688]{1,0:T(8,128)(2,1)S(1)} %collective-permute-done.26.refs_2_), channel_id=1, source_target_pairs={{0,8},{8,0},{16,24},{24,16},{1,9},{9,1},{17,25},{25,17},{2,10},{10... | collective-permute-start | bytes 516104 | tf_op jit(solution)/shard_map/ppermute | solution.py:495
  68.1 6.3 %collective-permute-start.16 = (s16[32,2688]{1,0:T(8,128)(2,1)S(1)}, s16[32,2688]{1,0:T(8,128)(2,1)S(1)}, u32[]{:S(2)}, u32[]{:S(2)}) collective-permute-start(s16[32,2688]{1,0:T(8,128)(2,1)S(1)} %update_amplitudes.2.refs_0_), channel_id=1, source_target_pairs={{0,8},{8,0},{16,24},{24,16},{1,9},{9,1},{17,25},{25,17},{2,10},{10... | collective-permute-start | bytes 516104 | tf_op jit(solution)/shard_map/ppermute | solution.py:495
  69.9 4.6 %collective-permute-start.18 = (s16[32,2688]{1,0:T(8,128)(2,1)S(1)}, s16[32,2688]{1,0:T(8,128)(2,1)S(1)}, u32[]{:S(2)}, u32[]{:S(2)}) collective-permute-start(s16[32,2688]{1,0:T(8,128)(2,1)S(1)} %collective-permute-done.17.refs_2_), channel_id=1, source_target_pairs={{0,8},{8,0},{16,24},{24,16},{1,9},{9,1},{17,25},{25,17},{2,10},{10... | collective-permute-start | bytes 516104 | tf_op jit(solution)/shard_map/ppermute | solution.py:495
  (8 other events, 59.2 us)

commit v4 on v3

--- a/solution.py
+++ b/solution.py
@@ -497,15 +497,6 @@
     own_cols = lax.dynamic_slice_in_dim(amplitudes, grp * cols, cols, 1)
     holes = lax.dynamic_slice_in_dim(hole_ints, pair * rows, rows, 1)
     holes = holes.reshape(pairs, 4, part, rows)
-    occ_energy = lookup(occ_pairs, e_occ)
-    virt_energy = lookup(virt_pairs, e_virt)
-    hole_energy = jnp.broadcast_to((occ_energy[0] + occ_energy[1])[:, None], (rows, LANES))
-    pair_energy = jnp.pad(
-        (virt_energy[0] + virt_energy[1])[None, :],
-        ((0, 0), (0, width - cols)),
-        constant_values=8.0,
-    )
-
     chip_half, core_at, count = (grp // 2) % 2, grp % 2, pairs // 2
     blocks = list(cut(amplitudes, pair, chip_half, core_at, pairs, depth))
     for j in range(count):
@@ -515,7 +506,7 @@
             for p in range(pairs)
         ]
         blocks[j] = lax.ppermute(blocks[j], ("grp", "pair"), moves)
-    own = pack(blocks, (own_cols, holes, pair_energy, hole_energy))
+    own = pack(blocks, (own_cols, holes))
     core = pack([swap(x, "grp", 1) for x in blocks], ())
     chip = swap(own, "grp", 2)
 
@@ -554,12 +545,26 @@
             got = [swap(give, "pair", bit) for (give, _), bit in zip(state[half], steps)]
             keeps = [keep for _, keep in state[half]]
             inner = 3 - len(keeps)
+            if n == 0 and half == 0:
+                after_first = got[0]
             if n == len(bits) - 1:
                 state[half] = (keeps, got)
             elif inner == 2:
                 state[half] = [add(keeps, got, inner, cols)]
             else:
                 state[half] = [add([k], [g], 1, cols) for k, g in zip(keeps, got)]
+    (occ_pairs, virt_pairs), _ = lax.optimization_barrier(
+        ((occ_pairs, virt_pairs), after_first)
+    )
+    occ_energy = lookup(occ_pairs, e_occ)
+    virt_energy = lookup(virt_pairs, e_virt)
+    hole_energy = jnp.broadcast_to((occ_energy[0] + occ_energy[1])[:, None], (rows, LANES))
+    pair_energy = jnp.pad(
+        (virt_energy[0] + virt_energy[1])[None, :],
+        ((0, 0), (0, width - cols)),
+        constant_values=8.0,
+    )
+
     sent = []
     in_halves = groups == 4 and 2 * cols % LANES != 0
     for half in range(2):

time: 76.9 us -> 77.3 us (level)
  waiting for transfers between devices: 19.7 us -> 16.8 us
  starting transfers between devices: 27.7 us -> 30.5 us
  Pallas kernels: 24.5 us -> 26.4 us
  other arithmetic: 2.95 us -> 1.5 us
    ppermute x24, waiting for transfers between devices: 19.1 us -> 13.7 us  [swap(): return lax.ppermute(x, axis, [(i, i ^ flip) for i in range(size)])]
    ppermute x24, starting transfers between devices: 18.5 us -> 21.2 us  [swap(): return lax.ppermute(x, axis, [(i, i ^ flip) for i in range(size)])]
    ppermute x4, waiting for transfers between devices: 0.56 us -> 3.17 us  [shards(): blocks[j] = lax.ppermute(blocks[j], ('grp', 'pair'), moves)]
    pallas_call x8, Pallas kernels: 3.17 us -> 5.12 us  [add(): pl.pallas_call(functools.partial(add_kernel, cols, layout(cols)[1], len(k...]
    reduce_sum x2, other arithmetic: 2.54 us -> 1.1 us  [lookup(): return jnp.sum(picked, axis=-1)]
  transfers between devices with their start and end apart: 28 -> 28, of which waited for: 11 -> 15; matrix products, arithmetic and copies ran while one was open for 5% -> 4% of each run, Pallas kernels for 27% -> 29%
where the time goes in v4:
time: 77.3 us; the launch traced here: 77 us
  starting transfers between devices  30.5 us (39%)
  Pallas kernels  26.4 us (34%)
  waiting for transfers between devices  16.8 us (22%)
  other arithmetic  1.5 us (2%)
  local copies, waits for them, and re-layouts  1.37 us (2%)
    ppermute x24, starting transfers between devices, swap(): return lax.ppermute(x, axis, [(i, i ^ flip) for i in range(size)])  21.2 us
    ppermute x24, waiting for transfers between devices, swap(): return lax.ppermute(x, axis, [(i, i ^ flip) for i in range(size)])  13.7 us
    pallas_call x2, Pallas kernels, product(): pl.pallas_call(functools.partial(product_kernel, order, parts, cols, segm...  13.5 us
    ppermute x4, starting transfers between devices, shards(): blocks[j] = lax.ppermute(blocks[j], ('grp', 'pair'), moves)  9.25 us
    pallas_call x8, Pallas kernels, add(): pl.pallas_call(functools.partial(add_kernel, cols, layout(cols)[1], len(k...  5.12 us
    pallas_call x2, Pallas kernels, place_half(): pl.pallas_call(functools.partial(half_kernel, cols, segments, late), grid...  4.03 us
    ppermute x4, waiting for transfers between devices, shards(): blocks[j] = lax.ppermute(blocks[j], ('grp', 'pair'), moves)  3.17 us
    pallas_call x1, Pallas kernels, cut(): pl.pallas_call(cut_kernel, grid_spec=pltpu.PrefetchScalarGridSpec(num_sca...  2.04 us
  transfers between devices with their start and end apart: 28, of which 15 were waited for; matrix products, arithmetic and copies ran while one was open for 4% of the time, Pallas kernels for 29%

profile of v4, /device:TPU:1, one launch (start us, length us, event | category | flops | bytes accessed | tf_op | source)
XLA Modules:
  0.0 77.0 jit_solution(14439459287279013983)
XLA Ops:
  0.1 2.0 %cut_blocks.1 = (bf16[32,1296]{1,0:T(8,128)(2,1)S(1)}, bf16[32,1296]{1,0:T(8,128)(2,1)S(1)}, bf16[32,1296]{1,0:T(8,128)(2,1)S(1)}, bf16[32,1296]{1,0:T(8,128)(2,1)S(1)}) custom-call(s32[3]{0:T(128)S(1)} %pad_add_fusion.3.where, bf16[64,10368]{1,0:T(8,128)(2,1)} %a_ref.1), custom_call_target="tpu_custom_call" | custom-call | flops 1024 | bytes 1024 | tf_op jit(solution)/shard_map/cut_blocks/pallas_call | solution.py:90
  2.1 4.1 %collective-permute-start = (bf16[32,1296]{1,0:T(8,128)(2,1)S(1)}, bf16[32,1296]{1,0:T(8,128)(2,1)S(1)}, u32[]{:S(2)}, u32[]{:S(2)}) collective-permute-start(bf16[32,1296]{1,0:T(8,128)(2,1)S(1)} %get-tuple-element.38), channel_id=1, source_target_pairs={{0,1},{1,0},{2,3},{3,2},{4,5},{5,4},{6,7},{7,6},{8,13},{9,12},{10,... | collective-permute-start | bytes 248840 | tf_op jit(solution)/shard_map/ppermute | solution.py:508
  7.3 2.1 %collective-permute-start.2 = (bf16[32,1296]{1,0:T(8,128)(2,1)S(1)}, bf16[32,1296]{1,0:T(8,128)(2,1)S(1)}, u32[]{:S(2)}, u32[]{:S(2)}) collective-permute-start(bf16[32,1296]{1,0:T(8,128)(2,1)S(1)} %get-tuple-element.40), channel_id=1, source_target_pairs={{0,3},{1,2},{2,1},{3,0},{4,7},{5,6},{6,5},{7,4},{8,15},{9,14},{10,... | collective-permute-start | bytes 248840 | tf_op jit(solution)/shard_map/ppermute | solution.py:508
  9.5 1.9 %collective-permute-start.3 = (bf16[32,1296]{1,0:T(8,128)(2,1)S(1)}, bf16[32,1296]{1,0:T(8,128)(2,1)S(1)}, u32[]{:S(2)}, u32[]{:S(2)}) collective-permute-start(bf16[32,1296]{1,0:T(8,128)(2,1)S(1)} %get-tuple-element.41), channel_id=1, source_target_pairs={{0,0},{1,1},{2,2},{3,3},{4,4},{5,5},{6,6},{7,7},{8,12},{9,13},{10,... | collective-permute-start | bytes 248840 | tf_op jit(solution)/shard_map/ppermute | solution.py:508
  12.7 1.5 %collective-permute-done.2.refs_2_ = bf16[32,1296]{1,0:T(8,128)(2,1)S(1)} collective-permute-done((bf16[32,1296]{1,0:T(8,128)(2,1)S(1)}, bf16[32,1296]{1,0:T(8,128)(2,1)S(1)}, u32[]{:S(2)}, u32[]{:S(2)}) %collective-permute-start.2) | collective-permute-done | bytes 82976 | tf_op jit(solution)/shard_map/ppermute | solution.py:508
  14.2 1.6 %collective-permute-done.3.refs_3_ = bf16[32,1296]{1,0:T(8,128)(2,1)S(1)} collective-permute-done((bf16[32,1296]{1,0:T(8,128)(2,1)S(1)}, bf16[32,1296]{1,0:T(8,128)(2,1)S(1)}, u32[]{:S(2)}, u32[]{:S(2)}) %collective-permute-start.3) | collective-permute-done | bytes 82976 | tf_op jit(solution)/shard_map/ppermute | solution.py:508
  15.9 1.3 %collective-permute-start.4 = (bf16[4,32,1296]{2,1,0:T(8,128)(2,1)S(1)}, bf16[4,32,1296]{2,1,0:T(8,128)(2,1)S(1)}, u32[]{:S(2)}, u32[]{:S(2)}) collective-permute-start(bf16[4,32,1296]{2,1,0:T(8,128)(2,1)S(1)} %pack_blocks.2.refs_0_), channel_id=1, source_target_pairs={{0,16},{8,24},{16,0},{24,8},{1,17},{9,25},{17,1},{25,9},{2,18},{10... | collective-permute-start | bytes 995336 | tf_op jit(solution)/shard_map/ppermute | solution.py:495
  19.2 7.0 %partial_products.2 = (s16[64,2688]{1,0:T(8,128)(2,1)}, s16[64,2688]{1,0:T(8,128)(2,1)}, f32[64,2688]{1,0:T(8,128)S(1)}, f32[64,2688]{1,0:T(8,128)S(1)}) custom-call(s32[4]{0:T(128)S(1)} %pad_add_fusion.4.where, bf16[4,32,1296]{2,1,0:T(8,128)(2,1)S(1)} %pack_blocks.2.refs_0_, bf16[4,32,1296]{2,1,0:T(8,128)(2,1)S(1)} %pack_blocks.3.refs_1_, ...), custom_call_target="tpu_custom_call" | custom-call | flops 1024 | bytes 1024 | tf_op jit(solution)/shard_map/partial_products/pallas_call | solution.py:198
  28.0 6.4 %partial_products.3 = (s16[64,2688]{1,0:T(8,128)(2,1)S(1)}, s16[64,2688]{1,0:T(8,128)(2,1)S(1)}, f32[64,2688]{1,0:T(8,128)S(1)}, f32[64,2688]{1,0:T(8,128)S(1)}) custom-call(s32[4]{0:T(128)S(1)} %pad_add_fusion.1.where, bf16[4,32,1296]{2,1,0:T(8,128)(2,1)S(1)} %collective-permute-done.4.refs_0_, bf16[4,32,1296]{2,1,0:T(8,128)(2,1)S(1)} %collective-permute-done.9.refs_1_, ...), custom_call_target="tpu_custom_call" | custom-call | flops 1024 | bytes 1024 | tf_op jit(solution)/shard_map/partial_products/pallas_call | solution.py:198
  34.5 1.5 %collective-permute-start.10 = (s16[64,2688]{1,0:T(8,128)(2,1)S(1)}, s16[64,2688]{1,0:T(8,128)(2,1)S(1)}, u32[]{:S(2)}, u32[]{:S(2)}) collective-permute-start(s16[64,2688]{1,0:T(8,128)(2,1)S(1)} %get-tuple-element.45), channel_id=1, source_target_pairs={{0,2},{1,3},{2,0},{3,1},{4,6},{5,7},{6,4},{7,5},{8,10},{9,11},{10,... | collective-permute-start | bytes 1032200 | tf_op jit(solution)/shard_map/ppermute | solution.py:495
  36.5 1.6 %add_partial_sums.12 = (s16[32,2688]{1,0:T(8,128)(2,1)S(1)}, f32[32,2688]{1,0:T(8,128)S(1)}) custom-call(f32[64,2688]{1,0:T(8,128)S(1)} %get-tuple-element.42.refs_0_, s16[64,2688]{1,0:T(8,128)(2,1)} %collective-permute-done.16.refs_1_), custom_call_target="tpu_custom_call" | custom-call | flops 1024 | bytes 1024 | tf_op jit(solution)/shard_map/add_partial_sums/pallas_call | solution.py:267
  38.1 1.2 %collective-permute-start.20 = (s16[32,2688]{1,0:T(8,128)(2,1)S(1)}, s16[32,2688]{1,0:T(8,128)(2,1)S(1)}, u32[]{:S(2)}, u32[]{:S(2)}) collective-permute-start(s16[32,2688]{1,0:T(8,128)(2,1)S(1)} %get-tuple-element.60), channel_id=1, source_target_pairs={{0,1},{1,0},{2,3},{3,2},{4,5},{5,4},{6,7},{7,6},{8,9},{9,8},{10,11... | collective-permute-start | bytes 516104 | tf_op jit(solution)/shard_map/ppermute | solution.py:495
  39.3 1.6 %add_partial_sums.14 = (s16[32,2688]{1,0:T(8,128)(2,1)S(1)}, f32[32,2688]{1,0:T(8,128)S(1)}) custom-call(f32[64,2688]{1,0:T(8,128)S(1)} %get-tuple-element.62.refs_0_, s16[64,2688]{1,0:T(8,128)(2,1)} %collective-permute-done.21.refs_1_), custom_call_target="tpu_custom_call" | custom-call | flops 1024 | bytes 1024 | tf_op jit(solution)/shard_map/add_partial_sums/pallas_call | solution.py:267
  44.3 2.5 %collective-permute-start.11 = (s16[32,2688]{1,0:T(8,128)(2,1)S(1)}, s16[32,2688]{1,0:T(8,128)(2,1)S(1)}, u32[]{:S(2)}, u32[]{:S(2)}) collective-permute-start(s16[32,2688]{1,0:T(8,128)(2,1)S(1)} %get-tuple-element.47), channel_id=1, source_target_pairs={{0,1},{1,0},{2,3},{3,2},{4,5},{5,4},{6,7},{7,6},{8,9},{9,8},{10,11... | collective-permute-start | bytes 516104 | tf_op jit(solution)/shard_map/ppermute | solution.py:495
  48.5 1.6 %collective-permute-start.23 = (s16[16,2688]{1,0:T(8,128)(2,1)S(1)}, s16[16,2688]{1,0:T(8,128)(2,1)S(1)}, u32[]{:S(2)}, u32[]{:S(2)}) collective-permute-start(s16[16,2688]{1,0:T(8,128)(2,1)S(1)} %get-tuple-element.67), channel_id=1, source_target_pairs={{0,4},{1,5},{2,6},{3,7},{4,0},{5,1},{6,2},{7,3},{8,12},{9,13},{10,... | collective-permute-start | bytes 258056 | tf_op jit(solution)/shard_map/ppermute | solution.py:495
  52.1 1.6 %collective-permute-start.14 = (s16[16,2688]{1,0:T(8,128)(2,1)S(1)}, s16[16,2688]{1,0:T(8,128)(2,1)S(1)}, u32[]{:S(2)}, u32[]{:S(2)}) collective-permute-start(s16[16,2688]{1,0:T(8,128)(2,1)S(1)} %get-tuple-element.54), channel_id=1, source_target_pairs={{0,4},{1,5},{2,6},{3,7},{4,0},{5,1},{6,2},{7,3},{8,12},{9,13},{10,... | collective-permute-start | bytes 258056 | tf_op jit(solution)/shard_map/ppermute | solution.py:495
  53.8 3.2 %collective-permute-done.13.refs_1_ = s16[32,2688]{1,0:T(8,128)(2,1)S(1)} collective-permute-done((s16[32,2688]{1,0:T(8,128)(2,1)S(1)}, s16[32,2688]{1,0:T(8,128)(2,1)S(1)}, u32[]{:S(2)}, u32[]{:S(2)}) %collective-permute-start.13) | collective-permute-done | bytes 172064 | tf_op jit(solution)/shard_map/ppermute | solution.py:495
  57.3 2.5 %collective-permute-done.24.refs_3_ = s16[16,2688]{1,0:T(8,128)(2,1)S(1)} collective-permute-done((s16[16,2688]{1,0:T(8,128)(2,1)S(1)}, s16[16,2688]{1,0:T(8,128)(2,1)S(1)}, u32[]{:S(2)}, u32[]{:S(2)}) %collective-permute-start.24) | collective-permute-done | bytes 86048 | tf_op jit(solution)/shard_map/ppermute | solution.py:495
  60.8 3.2 %collective-permute-done.15.refs_3_ = s16[16,2688]{1,0:T(8,128)(2,1)S(1)} collective-permute-done((s16[16,2688]{1,0:T(8,128)(2,1)S(1)}, s16[16,2688]{1,0:T(8,128)(2,1)S(1)}, u32[]{:S(2)}, u32[]{:S(2)}) %collective-permute-start.15) | collective-permute-done | bytes 86048 | tf_op jit(solution)/shard_map/ppermute | solution.py:495
  65.0 1.8 %collective-permute-start.25 = (s16[32,2688]{1,0:T(8,128)(2,1)S(1)}, s16[32,2688]{1,0:T(8,128)(2,1)S(1)}, u32[]{:S(2)}, u32[]{:S(2)}) collective-permute-start(s16[32,2688]{1,0:T(8,128)(2,1)S(1)} %update_amplitudes.3.refs_0_), channel_id=1, source_target_pairs={{0,8},{8,0},{16,24},{24,16},{1,9},{9,1},{17,25},{25,17},{2,10},{10... | collective-permute-start | bytes 516104 | tf_op jit(solution)/shard_map/ppermute | solution.py:495
  66.9 3.6 %collective-permute-start.27 = (s16[32,2688]{1,0:T(8,128)(2,1)S(1)}, s16[32,2688]{1,0:T(8,128)(2,1)S(1)}, u32[]{:S(2)}, u32[]{:S(2)}) collective-permute-start(s16[32,2688]{1,0:T(8,128)(2,1)S(1)} %collective-permute-done.26.refs_2_), channel_id=1, source_target_pairs={{0,8},{8,0},{16,24},{24,16},{1,9},{9,1},{17,25},{25,17},{2,10},{10... | collective-permute-start | bytes 516104 | tf_op jit(solution)/shard_map/ppermute | solution.py:495
  71.3 1.6 %collective-permute-start.19 = (s16[32,2688]{1,0:T(8,128)(2,1)S(1)}, s16[32,2688]{1,0:T(8,128)(2,1)S(1)}, u32[]{:S(2)}, u32[]{:S(2)}) collective-permute-start(s16[32,2688]{1,0:T(8,128)(2,1)S(1)} %collective-permute-done.18.refs_2_), channel_id=1, source_target_pairs={{0,8},{8,0},{16,24},{24,16},{1,9},{9,1},{17,25},{25,17},{2,10},{10... | collective-permute-start | bytes 516104 | tf_op jit(solution)/shard_map/ppermute | solution.py:495
  72.9 2.0 %place_early_half.1 = (f32[64,10368]{1,0:T(8,128)}, f32[64,128]{1,0:T(8,128)S(1)}) custom-call(s32[1]{0:T(128)} %bitcast.where, s16[32,2688]{1,0:T(8,128)(2,1)S(1)} %update_amplitudes.3.refs_0_, s16[32,2688]{1,0:T(8,128)(2,1)S(1)} %collective-permute-done.25.refs_1_, s16[32,2688]{1,0:T(8,128)(2,1)S(1)} %collective-permute-done.26.refs_2_, ...), custom_call_target="tpu_custom_call" | custom-call | tf_op jit(solution)/shard_map/place_early_half/pallas_call | solution.py:465
  74.9 2.0 %place_late_half.1 = f32[64,10368]{1,0:T(8,128)} custom-call(s32[1]{0:T(128)} %bitcast.where, s16[32,2688]{1,0:T(8,128)(2,1)S(1)} %update_amplitudes.2.refs_0_, s16[32,2688]{1,0:T(8,128)(2,1)S(1)} %collective-permute-done.17.refs_1_, s16[32,2688]{1,0:T(8,128)(2,1)S(1)} %collective-permute-done.18.refs_2_, ...), custom_call_target="tpu_custom_call", output_to_operand_aliasing={{}: (6, {})} | custom-call | tf_op jit(solution)/shard_map/place_late_half/pallas_call | solution.py:465
  (78 shorter events, 17.0 us)
Async XLA Ops:
  2.1 10.6 %collective-permute-start = (bf16[32,1296]{1,0:T(8,128)(2,1)S(1)}, bf16[32,1296]{1,0:T(8,128)(2,1)S(1)}, u32[]{:S(2)}, u32[]{:S(2)}) collective-permute-start(bf16[32,1296]{1,0:T(8,128)(2,1)S(1)} %get-tuple-element.38), channel_id=1, source_target_pairs={{0,1},{1,0},{2,3},{3,2},{4,5},{5,4},{6,7},{7,6},{8,13},{9,12},{10,... | collective-permute-start | bytes 248840 | tf_op jit(solution)/shard_map/ppermute | solution.py:508
  6.2 6.5 %collective-permute-start.1 = (bf16[32,1296]{1,0:T(8,128)(2,1)S(1)}, bf16[32,1296]{1,0:T(8,128)(2,1)S(1)}, u32[]{:S(2)}, u32[]{:S(2)}) collective-permute-start(bf16[32,1296]{1,0:T(8,128)(2,1)S(1)} %get-tuple-element.39), channel_id=1, source_target_pairs={{0,2},{1,3},{2,0},{3,1},{4,6},{5,7},{6,4},{7,5},{8,14},{9,15},{10,... | collective-permute-start | bytes 248840 | tf_op jit(solution)/shard_map/ppermute | solution.py:508
  7.3 6.9 %collective-permute-start.2 = (bf16[32,1296]{1,0:T(8,128)(2,1)S(1)}, bf16[32,1296]{1,0:T(8,128)(2,1)S(1)}, u32[]{:S(2)}, u32[]{:S(2)}) collective-permute-start(bf16[32,1296]{1,0:T(8,128)(2,1)S(1)} %get-tuple-element.40), channel_id=1, source_target_pairs={{0,3},{1,2},{2,1},{3,0},{4,7},{5,6},{6,5},{7,4},{8,15},{9,14},{10,... | collective-permute-start | bytes 248840 | tf_op jit(solution)/shard_map/ppermute | solution.py:508
  9.5 6.4 %collective-permute-start.3 = (bf16[32,1296]{1,0:T(8,128)(2,1)S(1)}, bf16[32,1296]{1,0:T(8,128)(2,1)S(1)}, u32[]{:S(2)}, u32[]{:S(2)}) collective-permute-start(bf16[32,1296]{1,0:T(8,128)(2,1)S(1)} %get-tuple-element.41), channel_id=1, source_target_pairs={{0,0},{1,1},{2,2},{3,3},{4,4},{5,5},{6,6},{7,7},{8,12},{9,13},{10,... | collective-permute-start | bytes 248840 | tf_op jit(solution)/shard_map/ppermute | solution.py:508
  15.9 10.4 %collective-permute-start.4 = (bf16[4,32,1296]{2,1,0:T(8,128)(2,1)S(1)}, bf16[4,32,1296]{2,1,0:T(8,128)(2,1)S(1)}, u32[]{:S(2)}, u32[]{:S(2)}) collective-permute-start(bf16[4,32,1296]{2,1,0:T(8,128)(2,1)S(1)} %pack_blocks.2.refs_0_), channel_id=1, source_target_pairs={{0,16},{8,24},{16,0},{24,8},{1,17},{9,25},{17,1},{25,9},{2,18},{10... | collective-permute-start | bytes 995336 | tf_op jit(solution)/shard_map/ppermute | solution.py:495
  26.3 1.7 %collective-permute-start.9 = (bf16[4,32,1296]{2,1,0:T(8,128)(2,1)S(1)}, bf16[4,32,1296]{2,1,0:T(8,128)(2,1)S(1)}, u32[]{:S(2)}, u32[]{:S(2)}) collective-permute-start(bf16[4,32,1296]{2,1,0:T(8,128)(2,1)S(1)} %collective-permute-done.4.refs_0_), channel_id=1, source_target_pairs={{0,8},{8,0},{16,24},{24,16},{1,9},{9,1},{17,25},{25,17},{2,10},{10... | collective-permute-start | bytes 995336 | tf_op jit(solution)/shard_map/ppermute | solution.py:495
  26.7 9.8 %collective-permute-start.16 = (s16[64,2688]{1,0:T(8,128)(2,1)}, s16[64,2688]{1,0:T(8,128)(2,1)}, u32[]{:S(2)}, u32[]{:S(2)}) collective-permute-start(s16[64,2688]{1,0:T(8,128)(2,1)} %get-tuple-element.56), channel_id=1, source_target_pairs={{0,2},{1,3},{2,0},{3,1},{4,6},{5,7},{6,4},{7,5},{8,10},{9,11},{10,... | collective-permute-start | bytes 1032200 | tf_op jit(solution)/shard_map/ppermute | solution.py:495
  26.7 12.6 %collective-permute-start.21 = (s16[64,2688]{1,0:T(8,128)(2,1)}, s16[64,2688]{1,0:T(8,128)(2,1)}, u32[]{:S(2)}, u32[]{:S(2)}) collective-permute-start(s16[64,2688]{1,0:T(8,128)(2,1)} %get-tuple-element.63), channel_id=1, source_target_pairs={{0,1},{1,0},{2,3},{3,2},{4,5},{5,4},{6,7},{7,6},{8,9},{9,8},{10,11... | collective-permute-start | bytes 1032200 | tf_op jit(solution)/shard_map/ppermute | solution.py:495
  34.5 9.3 %collective-permute-start.10 = (s16[64,2688]{1,0:T(8,128)(2,1)S(1)}, s16[64,2688]{1,0:T(8,128)(2,1)S(1)}, u32[]{:S(2)}, u32[]{:S(2)}) collective-permute-start(s16[64,2688]{1,0:T(8,128)(2,1)S(1)} %get-tuple-element.45), channel_id=1, source_target_pairs={{0,2},{1,3},{2,0},{3,1},{4,6},{5,7},{6,4},{7,5},{8,10},{9,11},{10,... | collective-permute-start | bytes 1032200 | tf_op jit(solution)/shard_map/ppermute | solution.py:495
  36.0 10.8 %collective-permute-start.12 = (s16[64,2688]{1,0:T(8,128)(2,1)S(1)}, s16[64,2688]{1,0:T(8,128)(2,1)S(1)}, u32[]{:S(2)}, u32[]{:S(2)}) collective-permute-start(s16[64,2688]{1,0:T(8,128)(2,1)S(1)} %get-tuple-element.50), channel_id=1, source_target_pairs={{0,1},{1,0},{2,3},{3,2},{4,5},{5,4},{6,7},{7,6},{8,9},{9,8},{10,11... | collective-permute-start | bytes 1032200 | tf_op jit(solution)/shard_map/ppermute | solution.py:495
  38.1 10.1 %collective-permute-start.20 = (s16[32,2688]{1,0:T(8,128)(2,1)S(1)}, s16[32,2688]{1,0:T(8,128)(2,1)S(1)}, u32[]{:S(2)}, u32[]{:S(2)}) collective-permute-start(s16[32,2688]{1,0:T(8,128)(2,1)S(1)} %get-tuple-element.60), channel_id=1, source_target_pairs={{0,1},{1,0},{2,3},{3,2},{4,5},{5,4},{6,7},{7,6},{8,9},{9,8},{10,11... | collective-permute-start | bytes 516104 | tf_op jit(solution)/shard_map/ppermute | solution.py:495
  40.9 9.8 %collective-permute-start.22 = (s16[32,2688]{1,0:T(8,128)(2,1)S(1)}, s16[32,2688]{1,0:T(8,128)(2,1)S(1)}, u32[]{:S(2)}, u32[]{:S(2)}) collective-permute-start(s16[32,2688]{1,0:T(8,128)(2,1)S(1)} %get-tuple-element.65), channel_id=1, source_target_pairs={{0,4},{1,5},{2,6},{3,7},{4,0},{5,1},{6,2},{7,3},{8,12},{9,13},{10,... | collective-permute-start | bytes 516104 | tf_op jit(solution)/shard_map/ppermute | solution.py:495
  44.3 7.6 %collective-permute-start.11 = (s16[32,2688]{1,0:T(8,128)(2,1)S(1)}, s16[32,2688]{1,0:T(8,128)(2,1)S(1)}, u32[]{:S(2)}, u32[]{:S(2)}) collective-permute-start(s16[32,2688]{1,0:T(8,128)(2,1)S(1)} %get-tuple-element.47), channel_id=1, source_target_pairs={{0,1},{1,0},{2,3},{3,2},{4,5},{5,4},{6,7},{7,6},{8,9},{9,8},{10,11... | collective-permute-start | bytes 516104 | tf_op jit(solution)/shard_map/ppermute | solution.py:495
  47.4 9.6 %collective-permute-start.13 = (s16[32,2688]{1,0:T(8,128)(2,1)S(1)}, s16[32,2688]{1,0:T(8,128)(2,1)S(1)}, u32[]{:S(2)}, u32[]{:S(2)}) collective-permute-start(s16[32,2688]{1,0:T(8,128)(2,1)S(1)} %get-tuple-element.52), channel_id=1, source_target_pairs={{0,2},{1,3},{2,0},{3,1},{4,6},{5,7},{6,4},{7,5},{8,10},{9,11},{10,... | collective-permute-start | bytes 516104 | tf_op jit(solution)/shard_map/ppermute | solution.py:495
  48.5 8.8 %collective-permute-start.23 = (s16[16,2688]{1,0:T(8,128)(2,1)S(1)}, s16[16,2688]{1,0:T(8,128)(2,1)S(1)}, u32[]{:S(2)}, u32[]{:S(2)}) collective-permute-start(s16[16,2688]{1,0:T(8,128)(2,1)S(1)} %get-tuple-element.67), channel_id=1, source_target_pairs={{0,4},{1,5},{2,6},{3,7},{4,0},{5,1},{6,2},{7,3},{8,12},{9,13},{10,... | collective-permute-start | bytes 258056 | tf_op jit(solution)/shard_map/ppermute | solution.py:495
  50.9 8.9 %collective-permute-start.24 = (s16[16,2688]{1,0:T(8,128)(2,1)S(1)}, s16[16,2688]{1,0:T(8,128)(2,1)S(1)}, u32[]{:S(2)}, u32[]{:S(2)}) collective-permute-start(s16[16,2688]{1,0:T(8,128)(2,1)S(1)} %get-tuple-element.68), channel_id=1, source_target_pairs={{0,2},{1,3},{2,0},{3,1},{4,6},{5,7},{6,4},{7,5},{8,10},{9,11},{10,... | collective-permute-start | bytes 258056 | tf_op jit(solution)/shard_map/ppermute | solution.py:495
  52.1 8.7 %collective-permute-start.14 = (s16[16,2688]{1,0:T(8,128)(2,1)S(1)}, s16[16,2688]{1,0:T(8,128)(2,1)S(1)}, u32[]{:S(2)}, u32[]{:S(2)}) collective-permute-start(s16[16,2688]{1,0:T(8,128)(2,1)S(1)} %get-tuple-element.54), channel_id=1, source_target_pairs={{0,4},{1,5},{2,6},{3,7},{4,0},{5,1},{6,2},{7,3},{8,12},{9,13},{10,... | collective-permute-start | bytes 258056 | tf_op jit(solution)/shard_map/ppermute | solution.py:495
  57.2 6.8 %collective-permute-start.15 = (s16[16,2688]{1,0:T(8,128)(2,1)S(1)}, s16[16,2688]{1,0:T(8,128)(2,1)S(1)}, u32[]{:S(2)}, u32[]{:S(2)}) collective-permute-start(s16[16,2688]{1,0:T(8,128)(2,1)S(1)} %get-tuple-element.55), channel_id=1, source_target_pairs={{0,4},{1,5},{2,6},{3,7},{4,0},{5,1},{6,2},{7,3},{8,12},{9,13},{10,... | collective-permute-start | bytes 258056 | tf_op jit(solution)/shard_map/ppermute | solution.py:495
  60.7 6.1 %collective-permute-start.26 = (s16[32,2688]{1,0:T(8,128)(2,1)S(1)}, s16[32,2688]{1,0:T(8,128)(2,1)S(1)}, u32[]{:S(2)}, u32[]{:S(2)}) collective-permute-start(s16[32,2688]{1,0:T(8,128)(2,1)S(1)} %update_amplitudes.3.refs_0_), channel_id=1, source_target_pairs={{0,16},{8,24},{16,0},{24,8},{1,17},{9,25},{17,1},{25,9},{2,18},{10... | collective-permute-start | bytes 516104 | tf_op jit(solution)/shard_map/ppermute | solution.py:495
  64.8 6.4 %collective-permute-start.18 = (s16[32,2688]{1,0:T(8,128)(2,1)S(1)}, s16[32,2688]{1,0:T(8,128)(2,1)S(1)}, u32[]{:S(2)}, u32[]{:S(2)}) collective-permute-start(s16[32,2688]{1,0:T(8,128)(2,1)S(1)} %update_amplitudes.2.refs_0_), channel_id=1, source_target_pairs={{0,16},{8,24},{16,0},{24,8},{1,17},{9,25},{17,1},{25,9},{2,18},{10... | collective-permute-start | bytes 516104 | tf_op jit(solution)/shard_map/ppermute | solution.py:495
  65.0 7.8 %collective-permute-start.25 = (s16[32,2688]{1,0:T(8,128)(2,1)S(1)}, s16[32,2688]{1,0:T(8,128)(2,1)S(1)}, u32[]{:S(2)}, u32[]{:S(2)}) collective-permute-start(s16[32,2688]{1,0:T(8,128)(2,1)S(1)} %update_amplitudes.3.refs_0_), channel_id=1, source_target_pairs={{0,8},{8,0},{16,24},{24,16},{1,9},{9,1},{17,25},{25,17},{2,10},{10... | collective-permute-start | bytes 516104 | tf_op jit(solution)/shard_map/ppermute | solution.py:495
  66.9 6.0 %collective-permute-start.27 = (s16[32,2688]{1,0:T(8,128)(2,1)S(1)}, s16[32,2688]{1,0:T(8,128)(2,1)S(1)}, u32[]{:S(2)}, u32[]{:S(2)}) collective-permute-start(s16[32,2688]{1,0:T(8,128)(2,1)S(1)} %collective-permute-done.26.refs_2_), channel_id=1, source_target_pairs={{0,8},{8,0},{16,24},{24,16},{1,9},{9,1},{17,25},{25,17},{2,10},{10... | collective-permute-start | bytes 516104 | tf_op jit(solution)/shard_map/ppermute | solution.py:495
  70.4 4.5 %collective-permute-start.17 = (s16[32,2688]{1,0:T(8,128)(2,1)S(1)}, s16[32,2688]{1,0:T(8,128)(2,1)S(1)}, u32[]{:S(2)}, u32[]{:S(2)}) collective-permute-start(s16[32,2688]{1,0:T(8,128)(2,1)S(1)} %update_amplitudes.2.refs_0_), channel_id=1, source_target_pairs={{0,8},{8,0},{16,24},{24,16},{1,9},{9,1},{17,25},{25,17},{2,10},{10... | collective-permute-start | bytes 516104 | tf_op jit(solution)/shard_map/ppermute | solution.py:495
  71.3 3.7 %collective-permute-start.19 = (s16[32,2688]{1,0:T(8,128)(2,1)S(1)}, s16[32,2688]{1,0:T(8,128)(2,1)S(1)}, u32[]{:S(2)}, u32[]{:S(2)}) collective-permute-start(s16[32,2688]{1,0:T(8,128)(2,1)S(1)} %collective-permute-done.18.refs_2_), channel_id=1, source_target_pairs={{0,8},{8,0},{16,24},{24,16},{1,9},{9,1},{17,25},{25,17},{2,10},{10... | collective-permute-start | bytes 516104 | tf_op jit(solution)/shard_map/ppermute | solution.py:495
  (12 other events, 133.4 us)

commit v5 on v3

--- a/solution.py
+++ b/solution.py
@@ -399,19 +399,24 @@
 def half_kernel(cols, segments, late, where, *refs):
     coded, refs = refs[:4], refs[4:]
     if late:
-        seam_in, _, out_ref, slots, strips, sems = refs
+        seam_in, _, out_ref, strips, sems = refs
     else:
-        out_ref, seam_ref, slots, strips, sems = refs
+        out_ref, seam_ref, strips, sems = refs
     high = coded[0].shape[0]
     part = high // 2
     width = coded[0].shape[1]
     tile = width // segments
+    for chip in range(2):
+        seam = spans_of(cols, chip)[1] * LANES
+        strips[chip, :, seam : seam + LANES] = jnp.zeros((high, LANES), jnp.float32)
     for rel, ref in enumerate(coded):
         for group in range(4):
 
             @pl.when(where[0] ^ rel == group)
             def _():
                 shift = group * cols % LANES
+                strip = strips.at[group // 2]
+                seam = spans_of(cols, group // 2)[1] * LANES
                 for j in range(2):
                     at = slice(j * part, (j + 1) * part)
                     codes = codes_of(ref, at, cols, segments)
@@ -420,19 +425,18 @@
                         for n in range(segments)
                     ]
                     x = jnp.concatenate(pieces, axis=1)
-                    slots[group, at, :] = pltpu.roll(x, shift, 1) if shift else x
-    lane = lax.broadcasted_iota(jnp.int32, (high, LANES), 1)
+                    x = pltpu.roll(x, shift, 1) if shift else x
+                    if group % 2:
+                        tiles = spans_of(cols, group // 2)[3]
+                        strip[at, seam + LANES : tiles * LANES] = x[:, LANES : tiles * LANES - seam]
+                        strip[at, seam : seam + LANES] += x[:, :LANES]
+                    else:
+                        strip[at, :seam] = x[:, :seam]
+                        strip[at, seam : seam + LANES] += x[:, seam : seam + LANES]
     stores = []
     for chip in range(2):
-        _, turn, shift, tiles = spans_of(cols, chip)
-        one, two = slots.at[2 * chip], slots.at[2 * chip + 1]
+        tiles = spans_of(cols, chip)[3]
         strip = strips.at[chip]
-        strip[:, : turn * LANES] = one[:, : turn * LANES]
-        seam = turn * LANES
-        strip[:, seam : seam + LANES] = jnp.where(
-            lane < shift, one[:, seam : seam + LANES], two[:, :LANES]
-        )
-        strip[:, seam + LANES : tiles * LANES] = two[:, LANES : tiles * LANES - seam]
         top = (chip ^ late) * high
         shared = slice(0, LANES) if chip else slice((tiles - 1) * LANES, tiles * LANES)
         if late:
@@ -470,7 +474,6 @@
             in_specs=[whole(x) for x in blocks] + [whole(seam), anywhere] * late,
             out_specs=anywhere if late else (anywhere, whole(seam)),
             scratch_shapes=[
-                pltpu.VMEM((4, high, width), jnp.float32),
                 pltpu.VMEM((2, high, tiles * LANES), jnp.float32),
                 pltpu.SemaphoreType.DMA((2,)),
             ],
@@ -522,7 +525,7 @@
     bits = [1 << n for n in range(pairs.bit_length() - 1)]
     x_first, z_first = bits, bits[1::-1] + bits[2:]
     x_then_far = bits[:1] + bits[2:] + bits[1:2]
-    routes = ((z_first, x_then_far), (z_first, x_first))
+    routes = ((z_first, x_then_far), (x_first, z_first))
 
     def listed(value, left):
         if not left:

time: 76.9 us -> 77 us (level)
  starting transfers between devices: 27.7 us -> 31 us
  waiting for transfers between devices: 19.7 us -> 16.7 us
    ppermute x24, starting transfers between devices: 18.5 us -> 21.8 us  [swap(): return lax.ppermute(x, axis, [(i, i ^ flip) for i in range(size)])]
    ppermute x24, waiting for transfers between devices: 19.1 us -> 16.1 us  [swap(): return lax.ppermute(x, axis, [(i, i ^ flip) for i in range(size)])]
  transfers between devices with their start and end apart: 28 -> 28, of which waited for: 11 -> 10; matrix products, arithmetic and copies ran while one was open for 5% -> 5% of each run, Pallas kernels for 27% -> 27%
where the time goes in v5:
time: 77 us; the launch traced here: 76.6 us
  starting transfers between devices  31 us (40%)
  Pallas kernels  24.4 us (32%)
  waiting for transfers between devices  16.7 us (22%)
  other arithmetic  2.94 us (4%)
  local copies, waits for them, and re-layouts  1.36 us (2%)
    ppermute x24, starting transfers between devices, swap(): return lax.ppermute(x, axis, [(i, i ^ flip) for i in range(size)])  21.8 us
    ppermute x24, waiting for transfers between devices, swap(): return lax.ppermute(x, axis, [(i, i ^ flip) for i in range(size)])  16.1 us
    pallas_call x2, Pallas kernels, product(): pl.pallas_call(functools.partial(product_kernel, order, parts, cols, segm...  13.5 us
    ppermute x4, starting transfers between devices, shards(): blocks[j] = lax.ppermute(blocks[j], ('grp', 'pair'), moves)  9.25 us
    pallas_call x2, Pallas kernels, place_half(): pl.pallas_call(functools.partial(half_kernel, cols, segments, late), grid...  3.95 us
    pallas_call x8, Pallas kernels, add(): pl.pallas_call(functools.partial(add_kernel, cols, layout(cols)[1], len(k...  3.17 us
    reduce_sum x2, other arithmetic, lookup(): return jnp.sum(picked, axis=-1)  2.54 us
    pallas_call x1, Pallas kernels, cut(): pl.pallas_call(cut_kernel, grid_spec=pltpu.PrefetchScalarGridSpec(num_sca...  2.04 us
  transfers between devices with their start and end apart: 28, of which 10 were waited for; matrix products, arithmetic and copies ran while one was open for 5% of the time, Pallas kernels for 27%

profile of v5, /device:TPU:1, one launch (start us, length us, event | category | flops | bytes accessed | tf_op | source)
XLA Modules:
  0.0 76.6 jit_solution(3767281397804662482)
XLA Ops:
  0.1 2.0 %cut_blocks.1 = (bf16[32,1296]{1,0:T(8,128)(2,1)S(1)}, bf16[32,1296]{1,0:T(8,128)(2,1)S(1)}, bf16[32,1296]{1,0:T(8,128)(2,1)S(1)}, bf16[32,1296]{1,0:T(8,128)(2,1)S(1)}) custom-call(s32[3]{0:T(128)S(1)} %pad_add_fusion.3.where, bf16[64,10368]{1,0:T(8,128)(2,1)} %a_ref.1), custom_call_target="tpu_custom_call" | custom-call | flops 1024 | bytes 1024 | tf_op jit(solution)/shard_map/cut_blocks/pallas_call | solution.py:90
  2.1 4.1 %collective-permute-start = (bf16[32,1296]{1,0:T(8,128)(2,1)S(1)}, bf16[32,1296]{1,0:T(8,128)(2,1)S(1)}, u32[]{:S(2)}, u32[]{:S(2)}) collective-permute-start(bf16[32,1296]{1,0:T(8,128)(2,1)S(1)} %get-tuple-element.36), channel_id=1, source_target_pairs={{0,1},{1,0},{2,3},{3,2},{4,5},{5,4},{6,7},{7,6},{8,13},{9,12},{10,... | collective-permute-start | bytes 248840 | tf_op jit(solution)/shard_map/ppermute | solution.py:520
  7.3 2.1 %collective-permute-start.2 = (bf16[32,1296]{1,0:T(8,128)(2,1)S(1)}, bf16[32,1296]{1,0:T(8,128)(2,1)S(1)}, u32[]{:S(2)}, u32[]{:S(2)}) collective-permute-start(bf16[32,1296]{1,0:T(8,128)(2,1)S(1)} %get-tuple-element.38), channel_id=1, source_target_pairs={{0,3},{1,2},{2,1},{3,0},{4,7},{5,6},{6,5},{7,4},{8,15},{9,14},{10,... | collective-permute-start | bytes 248840 | tf_op jit(solution)/shard_map/ppermute | solution.py:520
  9.5 1.9 %collective-permute-start.3 = (bf16[32,1296]{1,0:T(8,128)(2,1)S(1)}, bf16[32,1296]{1,0:T(8,128)(2,1)S(1)}, u32[]{:S(2)}, u32[]{:S(2)}) collective-permute-start(bf16[32,1296]{1,0:T(8,128)(2,1)S(1)} %get-tuple-element.39), channel_id=1, source_target_pairs={{0,0},{1,1},{2,2},{3,3},{4,4},{5,5},{6,6},{7,7},{8,12},{9,13},{10,... | collective-permute-start | bytes 248840 | tf_op jit(solution)/shard_map/ppermute | solution.py:520
  12.3 1.7 %select_reduce_fusion = f32[2,2592]{1,0:T(2,128)S(1)} fusion(f32[288]{0:T(512)} %param.13, s32[2,2592]{1,0:T(2,128)} %param.15), kind=kLoop, calls=%fused_computation | loop fusion | flops 4473792 | bytes 42624 | tf_op jit(solution)/shard_map/reduce_sum | solution.py:22
  14.0 1.2 %constant_dynamic-slice_fusion.1.refs_4_ = bf16[64,2592]{1,0:T(8,128)(2,1)S(1)} fusion(bf16[64,10368]{1,0:T(8,128)(2,1)} %a_ref.1, s32[]{:T(128)S(6)} %select_n.32), kind=kLoop, calls=%fused_computation.13 | loop fusion | bytes 663556 | tf_op jit(solution)/shard_map/dynamic_slice | solution.py:500
  16.0 1.3 %collective-permute-start.4 = (bf16[4,32,1296]{2,1,0:T(8,128)(2,1)S(1)}, bf16[4,32,1296]{2,1,0:T(8,128)(2,1)S(1)}, u32[]{:S(2)}, u32[]{:S(2)}) collective-permute-start(bf16[4,32,1296]{2,1,0:T(8,128)(2,1)S(1)} %pack_blocks.2.refs_0_), channel_id=1, source_target_pairs={{0,16},{8,24},{16,0},{24,8},{1,17},{9,25},{17,1},{25,9},{2,18},{10... | collective-permute-start | bytes 995336 | tf_op jit(solution)/shard_map/ppermute | solution.py:498
  19.3 7.0 %partial_products.2 = (s16[64,2688]{1,0:T(8,128)(2,1)}, s16[64,2688]{1,0:T(8,128)(2,1)}, f32[64,2688]{1,0:T(8,128)S(1)}, f32[64,2688]{1,0:T(8,128)S(1)}) custom-call(s32[4]{0:T(128)S(1)} %pad_add_fusion.4.where, bf16[4,32,1296]{2,1,0:T(8,128)(2,1)S(1)} %pack_blocks.2.refs_0_, bf16[4,32,1296]{2,1,0:T(8,128)(2,1)S(1)} %pack_blocks.3.refs_1_, ...), custom_call_target="tpu_custom_call" | custom-call | flops 1024 | bytes 1024 | tf_op jit(solution)/shard_map/partial_products/pallas_call | solution.py:198
  27.6 1.2 %collective-permute-start.21 = (s16[64,2688]{1,0:T(8,128)(2,1)}, s16[64,2688]{1,0:T(8,128)(2,1)S(1)}, u32[]{:S(2)}, u32[]{:S(2)}) collective-permute-start(s16[64,2688]{1,0:T(8,128)(2,1)} %get-tuple-element.59), channel_id=1, source_target_pairs={{0,1},{1,0},{2,3},{3,2},{4,5},{5,4},{6,7},{7,6},{8,9},{9,8},{10,11... | collective-permute-start | bytes 1032200 | tf_op jit(solution)/shard_map/ppermute | solution.py:498
  28.9 6.4 %partial_products.3 = (s16[64,2688]{1,0:T(8,128)(2,1)S(1)}, s16[64,2688]{1,0:T(8,128)(2,1)S(1)}, f32[64,2688]{1,0:T(8,128)S(1)}, f32[64,2688]{1,0:T(8,128)S(1)}) custom-call(s32[4]{0:T(128)S(1)} %pad_add_fusion.1.where, bf16[4,32,1296]{2,1,0:T(8,128)(2,1)S(1)} %collective-permute-done.4.refs_0_, bf16[4,32,1296]{2,1,0:T(8,128)(2,1)S(1)} %collective-permute-done.9.refs_1_, ...), custom_call_target="tpu_custom_call" | custom-call | flops 1024 | bytes 1024 | tf_op jit(solution)/shard_map/partial_products/pallas_call | solution.py:198
  38.9 1.9 %collective-permute-start.22 = (s16[32,2688]{1,0:T(8,128)(2,1)S(1)}, s16[32,2688]{1,0:T(8,128)(2,1)S(1)}, u32[]{:S(2)}, u32[]{:S(2)}) collective-permute-start(s16[32,2688]{1,0:T(8,128)(2,1)S(1)} %get-tuple-element.61), channel_id=1, source_target_pairs={{0,4},{1,5},{2,6},{3,7},{4,0},{5,1},{6,2},{7,3},{8,12},{9,13},{10,... | collective-permute-start | bytes 516104 | tf_op jit(solution)/shard_map/ppermute | solution.py:498
  40.8 3.4 %collective-permute-done.10.refs_1_ = s16[64,2688]{1,0:T(8,128)(2,1)S(1)} collective-permute-done((s16[64,2688]{1,0:T(8,128)(2,1)S(1)}, s16[64,2688]{1,0:T(8,128)(2,1)S(1)}, u32[]{:S(2)}, u32[]{:S(2)}) %collective-permute-start.10) | collective-permute-done | bytes 344096 | tf_op jit(solution)/shard_map/ppermute | solution.py:498
  45.5 2.6 %collective-permute-done.12.refs_1_ = s16[64,2688]{1,0:T(8,128)(2,1)S(1)} collective-permute-done((s16[64,2688]{1,0:T(8,128)(2,1)S(1)}, s16[64,2688]{1,0:T(8,128)(2,1)S(1)}, u32[]{:S(2)}, u32[]{:S(2)}) %collective-permute-start.12) | collective-permute-done | bytes 344096 | tf_op jit(solution)/shard_map/ppermute | solution.py:498
  48.6 1.1 %collective-permute-start.13 = (s16[32,2688]{1,0:T(8,128)(2,1)S(1)}, s16[32,2688]{1,0:T(8,128)(2,1)S(1)}, u32[]{:S(2)}, u32[]{:S(2)}) collective-permute-start(s16[32,2688]{1,0:T(8,128)(2,1)S(1)} %get-tuple-element.50), channel_id=1, source_target_pairs={{0,1},{1,0},{2,3},{3,2},{4,5},{5,4},{6,7},{7,6},{8,9},{9,8},{10,11... | collective-permute-start | bytes 516104 | tf_op jit(solution)/shard_map/ppermute | solution.py:498
  50.5 2.3 %collective-permute-start.24 = (s16[16,2688]{1,0:T(8,128)(2,1)S(1)}, s16[16,2688]{1,0:T(8,128)(2,1)S(1)}, u32[]{:S(2)}, u32[]{:S(2)}) collective-permute-start(s16[16,2688]{1,0:T(8,128)(2,1)S(1)} %get-tuple-element.64), channel_id=1, source_target_pairs={{0,2},{1,3},{2,0},{3,1},{4,6},{5,7},{6,4},{7,5},{8,10},{9,11},{10,... | collective-permute-start | bytes 258056 | tf_op jit(solution)/shard_map/ppermute | solution.py:498
  54.2 1.5 %collective-permute-start.15 = (s16[16,2688]{1,0:T(8,128)(2,1)S(1)}, s16[16,2688]{1,0:T(8,128)(2,1)S(1)}, u32[]{:S(2)}, u32[]{:S(2)}) collective-permute-start(s16[16,2688]{1,0:T(8,128)(2,1)S(1)} %get-tuple-element.53), channel_id=1, source_target_pairs={{0,4},{1,5},{2,6},{3,7},{4,0},{5,1},{6,2},{7,3},{8,12},{9,13},{10,... | collective-permute-start | bytes 258056 | tf_op jit(solution)/shard_map/ppermute | solution.py:498
  57.0 5.0 %collective-permute-done.14.refs_2_ = s16[16,2688]{1,0:T(8,128)(2,1)S(1)} collective-permute-done((s16[16,2688]{1,0:T(8,128)(2,1)S(1)}, s16[16,2688]{1,0:T(8,128)(2,1)S(1)}, u32[]{:S(2)}, u32[]{:S(2)}) %collective-permute-start.14) | collective-permute-done | bytes 86048 | tf_op jit(solution)/shard_map/ppermute | solution.py:498
  62.1 2.8 %collective-permute-done.15.refs_3_ = s16[16,2688]{1,0:T(8,128)(2,1)S(1)} collective-permute-done((s16[16,2688]{1,0:T(8,128)(2,1)S(1)}, s16[16,2688]{1,0:T(8,128)(2,1)S(1)}, u32[]{:S(2)}, u32[]{:S(2)}) %collective-permute-start.15) | collective-permute-done | bytes 86048 | tf_op jit(solution)/shard_map/ppermute | solution.py:498
  66.0 1.7 %collective-permute-start.25 = (s16[32,2688]{1,0:T(8,128)(2,1)S(1)}, s16[32,2688]{1,0:T(8,128)(2,1)S(1)}, u32[]{:S(2)}, u32[]{:S(2)}) collective-permute-start(s16[32,2688]{1,0:T(8,128)(2,1)S(1)} %update_amplitudes.3.refs_0_), channel_id=1, source_target_pairs={{0,8},{8,0},{16,24},{24,16},{1,9},{9,1},{17,25},{25,17},{2,10},{10... | collective-permute-start | bytes 516104 | tf_op jit(solution)/shard_map/ppermute | solution.py:498
  67.6 1.4 %collective-permute-start.27 = (s16[32,2688]{1,0:T(8,128)(2,1)S(1)}, s16[32,2688]{1,0:T(8,128)(2,1)S(1)}, u32[]{:S(2)}, u32[]{:S(2)}) collective-permute-start(s16[32,2688]{1,0:T(8,128)(2,1)S(1)} %collective-permute-done.26.refs_2_), channel_id=1, source_target_pairs={{0,8},{8,0},{16,24},{24,16},{1,9},{9,1},{17,25},{25,17},{2,10},{10... | collective-permute-start | bytes 516104 | tf_op jit(solution)/shard_map/ppermute | solution.py:498
  69.0 1.4 %collective-permute-done.17.refs_2_ = s16[32,2688]{1,0:T(8,128)(2,1)S(1)} collective-permute-done((s16[32,2688]{1,0:T(8,128)(2,1)S(1)}, s16[32,2688]{1,0:T(8,128)(2,1)S(1)}, u32[]{:S(2)}, u32[]{:S(2)}) %collective-permute-start.17) | collective-permute-done | bytes 172064 | tf_op jit(solution)/shard_map/ppermute | solution.py:498
  70.4 2.2 %collective-permute-start.18 = (s16[32,2688]{1,0:T(8,128)(2,1)S(1)}, s16[32,2688]{1,0:T(8,128)(2,1)S(1)}, u32[]{:S(2)}, u32[]{:S(2)}) collective-permute-start(s16[32,2688]{1,0:T(8,128)(2,1)S(1)} %collective-permute-done.17.refs_2_), channel_id=1, source_target_pairs={{0,8},{8,0},{16,24},{24,16},{1,9},{9,1},{17,25},{25,17},{2,10},{10... | collective-permute-start | bytes 516104 | tf_op jit(solution)/shard_map/ppermute | solution.py:498
  72.7 2.0 %place_early_half.1 = (f32[64,10368]{1,0:T(8,128)}, f32[64,128]{1,0:T(8,128)S(1)}) custom-call(s32[1]{0:T(128)} %bitcast.where, s16[32,2688]{1,0:T(8,128)(2,1)S(1)} %update_amplitudes.3.refs_0_, s16[32,2688]{1,0:T(8,128)(2,1)S(1)} %collective-permute-done.25.refs_1_, s16[32,2688]{1,0:T(8,128)(2,1)S(1)} %collective-permute-done.26.refs_2_, ...), custom_call_target="tpu_custom_call" | custom-call | tf_op jit(solution)/shard_map/place_early_half/pallas_call | solution.py:469
  74.7 2.0 %place_late_half.1 = f32[64,10368]{1,0:T(8,128)} custom-call(s32[1]{0:T(128)} %bitcast.where, s16[32,2688]{1,0:T(8,128)(2,1)S(1)} %update_amplitudes.2.refs_0_, s16[32,2688]{1,0:T(8,128)(2,1)S(1)} %collective-permute-done.16.refs_1_, s16[32,2688]{1,0:T(8,128)(2,1)S(1)} %collective-permute-done.17.refs_2_, ...), custom_call_target="tpu_custom_call", output_to_operand_aliasing={{}: (6, {})} | custom-call | tf_op jit(solution)/shard_map/place_late_half/pallas_call | solution.py:469
  (70 shorter events, 16.1 us)
Async XLA Ops:
  2.1 13.2 %collective-permute-start = (bf16[32,1296]{1,0:T(8,128)(2,1)S(1)}, bf16[32,1296]{1,0:T(8,128)(2,1)S(1)}, u32[]{:S(2)}, u32[]{:S(2)}) collective-permute-start(bf16[32,1296]{1,0:T(8,128)(2,1)S(1)} %get-tuple-element.36), channel_id=1, source_target_pairs={{0,1},{1,0},{2,3},{3,2},{4,5},{5,4},{6,7},{7,6},{8,13},{9,12},{10,... | collective-permute-start | bytes 248840 | tf_op jit(solution)/shard_map/ppermute | solution.py:520
  6.2 9.1 %collective-permute-start.1 = (bf16[32,1296]{1,0:T(8,128)(2,1)S(1)}, bf16[32,1296]{1,0:T(8,128)(2,1)S(1)}, u32[]{:S(2)}, u32[]{:S(2)}) collective-permute-start(bf16[32,1296]{1,0:T(8,128)(2,1)S(1)} %get-tuple-element.37), channel_id=1, source_target_pairs={{0,2},{1,3},{2,0},{3,1},{4,6},{5,7},{6,4},{7,5},{8,14},{9,15},{10,... | collective-permute-start | bytes 248840 | tf_op jit(solution)/shard_map/ppermute | solution.py:520
  7.3 8.0 %collective-permute-start.2 = (bf16[32,1296]{1,0:T(8,128)(2,1)S(1)}, bf16[32,1296]{1,0:T(8,128)(2,1)S(1)}, u32[]{:S(2)}, u32[]{:S(2)}) collective-permute-start(bf16[32,1296]{1,0:T(8,128)(2,1)S(1)} %get-tuple-element.38), channel_id=1, source_target_pairs={{0,3},{1,2},{2,1},{3,0},{4,7},{5,6},{6,5},{7,4},{8,15},{9,14},{10,... | collective-permute-start | bytes 248840 | tf_op jit(solution)/shard_map/ppermute | solution.py:520
  9.5 6.4 %collective-permute-start.3 = (bf16[32,1296]{1,0:T(8,128)(2,1)S(1)}, bf16[32,1296]{1,0:T(8,128)(2,1)S(1)}, u32[]{:S(2)}, u32[]{:S(2)}) collective-permute-start(bf16[32,1296]{1,0:T(8,128)(2,1)S(1)} %get-tuple-element.39), channel_id=1, source_target_pairs={{0,0},{1,1},{2,2},{3,3},{4,4},{5,5},{6,6},{7,7},{8,12},{9,13},{10,... | collective-permute-start | bytes 248840 | tf_op jit(solution)/shard_map/ppermute | solution.py:520
  16.0 10.4 %collective-permute-start.4 = (bf16[4,32,1296]{2,1,0:T(8,128)(2,1)S(1)}, bf16[4,32,1296]{2,1,0:T(8,128)(2,1)S(1)}, u32[]{:S(2)}, u32[]{:S(2)}) collective-permute-start(bf16[4,32,1296]{2,1,0:T(8,128)(2,1)S(1)} %pack_blocks.2.refs_0_), channel_id=1, source_target_pairs={{0,16},{8,24},{16,0},{24,8},{1,17},{9,25},{17,1},{25,9},{2,18},{10... | collective-permute-start | bytes 995336 | tf_op jit(solution)/shard_map/ppermute | solution.py:498
  26.4 2.5 %collective-permute-start.9 = (bf16[4,32,1296]{2,1,0:T(8,128)(2,1)S(1)}, bf16[4,32,1296]{2,1,0:T(8,128)(2,1)S(1)}, u32[]{:S(2)}, u32[]{:S(2)}) collective-permute-start(bf16[4,32,1296]{2,1,0:T(8,128)(2,1)S(1)} %collective-permute-done.4.refs_0_), channel_id=1, source_target_pairs={{0,8},{8,0},{16,24},{24,16},{1,9},{9,1},{17,25},{25,17},{2,10},{10... | collective-permute-start | bytes 995336 | tf_op jit(solution)/shard_map/ppermute | solution.py:498
  26.8 9.9 %collective-permute-start.19 = (s16[64,2688]{1,0:T(8,128)(2,1)}, s16[64,2688]{1,0:T(8,128)(2,1)S(1)}, u32[]{:S(2)}, u32[]{:S(2)}) collective-permute-start(s16[64,2688]{1,0:T(8,128)(2,1)} %get-tuple-element.54), channel_id=1, source_target_pairs={{0,2},{1,3},{2,0},{3,1},{4,6},{5,7},{6,4},{7,5},{8,10},{9,11},{10,... | collective-permute-start | bytes 1032200 | tf_op jit(solution)/shard_map/ppermute | solution.py:498
  27.6 10.7 %collective-permute-start.21 = (s16[64,2688]{1,0:T(8,128)(2,1)}, s16[64,2688]{1,0:T(8,128)(2,1)S(1)}, u32[]{:S(2)}, u32[]{:S(2)}) collective-permute-start(s16[64,2688]{1,0:T(8,128)(2,1)} %get-tuple-element.59), channel_id=1, source_target_pairs={{0,1},{1,0},{2,3},{3,2},{4,5},{5,4},{6,7},{7,6},{8,9},{9,8},{10,11... | collective-permute-start | bytes 1032200 | tf_op jit(solution)/shard_map/ppermute | solution.py:498
  35.3 8.9 %collective-permute-start.10 = (s16[64,2688]{1,0:T(8,128)(2,1)S(1)}, s16[64,2688]{1,0:T(8,128)(2,1)S(1)}, u32[]{:S(2)}, u32[]{:S(2)}) collective-permute-start(s16[64,2688]{1,0:T(8,128)(2,1)S(1)} %get-tuple-element.43), channel_id=1, source_target_pairs={{0,1},{1,0},{2,3},{3,2},{4,5},{5,4},{6,7},{7,6},{8,9},{9,8},{10,11... | collective-permute-start | bytes 1032200 | tf_op jit(solution)/shard_map/ppermute | solution.py:498
  35.7 12.3 %collective-permute-start.12 = (s16[64,2688]{1,0:T(8,128)(2,1)S(1)}, s16[64,2688]{1,0:T(8,128)(2,1)S(1)}, u32[]{:S(2)}, u32[]{:S(2)}) collective-permute-start(s16[64,2688]{1,0:T(8,128)(2,1)S(1)} %get-tuple-element.48), channel_id=1, source_target_pairs={{0,2},{1,3},{2,0},{3,1},{4,6},{5,7},{6,4},{7,5},{8,10},{9,11},{10,... | collective-permute-start | bytes 1032200 | tf_op jit(solution)/shard_map/ppermute | solution.py:498
  37.2 12.6 %collective-permute-start.20 = (s16[32,2688]{1,0:T(8,128)(2,1)S(1)}, s16[32,2688]{1,0:T(8,128)(2,1)S(1)}, u32[]{:S(2)}, u32[]{:S(2)}) collective-permute-start(s16[32,2688]{1,0:T(8,128)(2,1)S(1)} %get-tuple-element.56), channel_id=1, source_target_pairs={{0,1},{1,0},{2,3},{3,2},{4,5},{5,4},{6,7},{7,6},{8,9},{9,8},{10,11... | collective-permute-start | bytes 516104 | tf_op jit(solution)/shard_map/ppermute | solution.py:498
  38.9 11.5 %collective-permute-start.22 = (s16[32,2688]{1,0:T(8,128)(2,1)S(1)}, s16[32,2688]{1,0:T(8,128)(2,1)S(1)}, u32[]{:S(2)}, u32[]{:S(2)}) collective-permute-start(s16[32,2688]{1,0:T(8,128)(2,1)S(1)} %get-tuple-element.61), channel_id=1, source_target_pairs={{0,4},{1,5},{2,6},{3,7},{4,0},{5,1},{6,2},{7,3},{8,12},{9,13},{10,... | collective-permute-start | bytes 516104 | tf_op jit(solution)/shard_map/ppermute | solution.py:498
  44.8 8.0 %collective-permute-start.11 = (s16[32,2688]{1,0:T(8,128)(2,1)S(1)}, s16[32,2688]{1,0:T(8,128)(2,1)S(1)}, u32[]{:S(2)}, u32[]{:S(2)}) collective-permute-start(s16[32,2688]{1,0:T(8,128)(2,1)S(1)} %get-tuple-element.45), channel_id=1, source_target_pairs={{0,2},{1,3},{2,0},{3,1},{4,6},{5,7},{6,4},{7,5},{8,10},{9,11},{10,... | collective-permute-start | bytes 516104 | tf_op jit(solution)/shard_map/ppermute | solution.py:498
  48.6 5.4 %collective-permute-start.13 = (s16[32,2688]{1,0:T(8,128)(2,1)S(1)}, s16[32,2688]{1,0:T(8,128)(2,1)S(1)}, u32[]{:S(2)}, u32[]{:S(2)}) collective-permute-start(s16[32,2688]{1,0:T(8,128)(2,1)S(1)} %get-tuple-element.50), channel_id=1, source_target_pairs={{0,1},{1,0},{2,3},{3,2},{4,5},{5,4},{6,7},{7,6},{8,9},{9,8},{10,11... | collective-permute-start | bytes 516104 | tf_op jit(solution)/shard_map/ppermute | solution.py:498
  50.0 5.8 %collective-permute-start.23 = (s16[16,2688]{1,0:T(8,128)(2,1)S(1)}, s16[16,2688]{1,0:T(8,128)(2,1)S(1)}, u32[]{:S(2)}, u32[]{:S(2)}) collective-permute-start(s16[16,2688]{1,0:T(8,128)(2,1)S(1)} %get-tuple-element.63), channel_id=1, source_target_pairs={{0,4},{1,5},{2,6},{3,7},{4,0},{5,1},{6,2},{7,3},{8,12},{9,13},{10,... | collective-permute-start | bytes 258056 | tf_op jit(solution)/shard_map/ppermute | solution.py:498
  50.5 5.3 %collective-permute-start.24 = (s16[16,2688]{1,0:T(8,128)(2,1)S(1)}, s16[16,2688]{1,0:T(8,128)(2,1)S(1)}, u32[]{:S(2)}, u32[]{:S(2)}) collective-permute-start(s16[16,2688]{1,0:T(8,128)(2,1)S(1)} %get-tuple-element.64), channel_id=1, source_target_pairs={{0,2},{1,3},{2,0},{3,1},{4,6},{5,7},{6,4},{7,5},{8,10},{9,11},{10,... | collective-permute-start | bytes 258056 | tf_op jit(solution)/shard_map/ppermute | solution.py:498
  53.0 9.0 %collective-permute-start.14 = (s16[16,2688]{1,0:T(8,128)(2,1)S(1)}, s16[16,2688]{1,0:T(8,128)(2,1)S(1)}, u32[]{:S(2)}, u32[]{:S(2)}) collective-permute-start(s16[16,2688]{1,0:T(8,128)(2,1)S(1)} %get-tuple-element.52), channel_id=1, source_target_pairs={{0,4},{1,5},{2,6},{3,7},{4,0},{5,1},{6,2},{7,3},{8,12},{9,13},{10,... | collective-permute-start | bytes 258056 | tf_op jit(solution)/shard_map/ppermute | solution.py:498
  54.2 10.6 %collective-permute-start.15 = (s16[16,2688]{1,0:T(8,128)(2,1)S(1)}, s16[16,2688]{1,0:T(8,128)(2,1)S(1)}, u32[]{:S(2)}, u32[]{:S(2)}) collective-permute-start(s16[16,2688]{1,0:T(8,128)(2,1)S(1)} %get-tuple-element.53), channel_id=1, source_target_pairs={{0,4},{1,5},{2,6},{3,7},{4,0},{5,1},{6,2},{7,3},{8,12},{9,13},{10,... | collective-permute-start | bytes 258056 | tf_op jit(solution)/shard_map/ppermute | solution.py:498
  56.7 11.0 %collective-permute-start.26 = (s16[32,2688]{1,0:T(8,128)(2,1)S(1)}, s16[32,2688]{1,0:T(8,128)(2,1)S(1)}, u32[]{:S(2)}, u32[]{:S(2)}) collective-permute-start(s16[32,2688]{1,0:T(8,128)(2,1)S(1)} %update_amplitudes.3.refs_0_), channel_id=1, source_target_pairs={{0,16},{8,24},{16,0},{24,8},{1,17},{9,25},{17,1},{25,9},{2,18},{10... | collective-permute-start | bytes 516104 | tf_op jit(solution)/shard_map/ppermute | solution.py:498
  65.7 4.8 %collective-permute-start.17 = (s16[32,2688]{1,0:T(8,128)(2,1)S(1)}, s16[32,2688]{1,0:T(8,128)(2,1)S(1)}, u32[]{:S(2)}, u32[]{:S(2)}) collective-permute-start(s16[32,2688]{1,0:T(8,128)(2,1)S(1)} %update_amplitudes.2.refs_0_), channel_id=1, source_target_pairs={{0,16},{8,24},{16,0},{24,8},{1,17},{9,25},{17,1},{25,9},{2,18},{10... | collective-permute-start | bytes 516104 | tf_op jit(solution)/shard_map/ppermute | solution.py:498
  66.0 6.7 %collective-permute-start.25 = (s16[32,2688]{1,0:T(8,128)(2,1)S(1)}, s16[32,2688]{1,0:T(8,128)(2,1)S(1)}, u32[]{:S(2)}, u32[]{:S(2)}) collective-permute-start(s16[32,2688]{1,0:T(8,128)(2,1)S(1)} %update_amplitudes.3.refs_0_), channel_id=1, source_target_pairs={{0,8},{8,0},{16,24},{24,16},{1,9},{9,1},{17,25},{25,17},{2,10},{10... | collective-permute-start | bytes 516104 | tf_op jit(solution)/shard_map/ppermute | solution.py:498
  67.6 5.0 %collective-permute-start.27 = (s16[32,2688]{1,0:T(8,128)(2,1)S(1)}, s16[32,2688]{1,0:T(8,128)(2,1)S(1)}, u32[]{:S(2)}, u32[]{:S(2)}) collective-permute-start(s16[32,2688]{1,0:T(8,128)(2,1)S(1)} %collective-permute-done.26.refs_2_), channel_id=1, source_target_pairs={{0,8},{8,0},{16,24},{24,16},{1,9},{9,1},{17,25},{25,17},{2,10},{10... | collective-permute-start | bytes 516104 | tf_op jit(solution)/shard_map/ppermute | solution.py:498
  69.0 5.6 %collective-permute-start.16 = (s16[32,2688]{1,0:T(8,128)(2,1)S(1)}, s16[32,2688]{1,0:T(8,128)(2,1)S(1)}, u32[]{:S(2)}, u32[]{:S(2)}) collective-permute-start(s16[32,2688]{1,0:T(8,128)(2,1)S(1)} %update_amplitudes.2.refs_0_), channel_id=1, source_target_pairs={{0,8},{8,0},{16,24},{24,16},{1,9},{9,1},{17,25},{25,17},{2,10},{10... | collective-permute-start | bytes 516104 | tf_op jit(solution)/shard_map/ppermute | solution.py:498
  70.4 4.2 %collective-permute-start.18 = (s16[32,2688]{1,0:T(8,128)(2,1)S(1)}, s16[32,2688]{1,0:T(8,128)(2,1)S(1)}, u32[]{:S(2)}, u32[]{:S(2)}) collective-permute-start(s16[32,2688]{1,0:T(8,128)(2,1)S(1)} %collective-permute-done.17.refs_2_), channel_id=1, source_target_pairs={{0,8},{8,0},{16,24},{24,16},{1,9},{9,1},{17,25},{25,17},{2,10},{10... | collective-permute-start | bytes 516104 | tf_op jit(solution)/shard_map/ppermute | solution.py:498
  (8 other events, 55.8 us)
